TPU v7x, 256 devices: a whole 4x4x8 slice. The times are simulated.
256 devices in a mesh: dp: 8 (over z_lo, y), seq: 32 (over x, z_hi, core).
Axes of the slice: x: 4, y: 4, z: 8 (z_hi: 4, z_lo: 2; z = z_hi * 2 + z_lo), core: 2. Of those that a mesh axis runs over, the one named last changes fastest.
Arguments:
- query: bfloat16 [8, 4096, 4096], P('dp', 'seq'), may hold values from -6 to 6
- key_stream: bfloat16 [8, 4096, 4096], P('dp', 'seq'), may hold values from -6 to 6
- value_stream: bfloat16 [8, 4096, 4096], P('dp', 'seq'), may hold values from -6 to 6
- upstream: bfloat16 [8, 4096, 4096], P('dp', 'seq'), may hold values from -6 to 6
- bases: int32 [8, 4096], P('dp', 'seq'), may hold values from 0 to 3
- base_rows: bfloat16 [4, 4096], replicated, may hold values from -6 to 6
- long_filter: float32 [4096, 4096], P('seq', 'dp'), may hold values from -6 to 6
- skip_weight: float32 [4096], P('seq'), may hold values from -4 to 4
Outputs:
- query_grad: bfloat16 [8, 4096, 4096], P('dp', 'seq')
- key_grad: bfloat16 [8, 4096, 4096], P('dp', 'seq')
- value_grad: bfloat16 [8, 4096, 4096], P('dp', 'seq')
- filter_grad: float32 [4096, 4096], P('seq', 'dp')
Inputs may be any that keep to these rules, and one draw needn't show every extreme that they name: `bases`: each entry names one base.
All inputs are finite; a program needn't handle non-finite values.
Results may differ from a plain program's by a relative error of at most 0.018.
Values may be sent and summed in bfloat16 or wider, within the bound.
No kernel may reach another device: no remote copies, remote signals or barrier semaphores. Data moves between devices by JAX's collectives and lax.ppermute only.
A program may use at most 192 MiB of HBM per device.

v0:
```python
import math

import jax
import jax.numpy as jnp
from jax import lax
from jax.sharding import PartitionSpec as P

PRECISE = lax.Precision.HIGHEST


def outer_table(inner_len, outer_len, half_outer, points):
    inner_idx = jnp.arange(inner_len, dtype=jnp.int32)[:, None, None]
    freq_idx = jnp.arange(outer_len, dtype=jnp.int32)[None, :, None]
    outer_idx = jnp.arange(half_outer, dtype=jnp.int32)[None, None, :]
    phase = freq_idx * (outer_idx * inner_len + inner_idx) % points
    angle = 2.0 * math.pi / points * phase.astype(jnp.float32)
    return jnp.stack([jnp.cos(angle), -jnp.sin(angle)], axis=1)


def inner_tables(inner_len):
    row_idx = jnp.arange(inner_len, dtype=jnp.int32)[:, None]
    col_idx = jnp.arange(inner_len, dtype=jnp.int32)[None, :]
    angle = 2.0 * math.pi / inner_len * (row_idx * col_idx % inner_len).astype(jnp.float32)
    cosine = jnp.cos(angle)
    sine = jnp.sin(angle)
    ahead = jnp.stack([jnp.stack([cosine, sine]), jnp.stack([-sine, cosine])])
    back = jnp.stack([jnp.stack([cosine, -sine]), jnp.stack([sine, cosine])])
    return (ahead, back)


def forward_taps(taps, tables):
    twisted, ahead, back = tables
    first_section = jnp.einsum("bska,cab->bskc", twisted, taps, precision=PRECISE)
    return jnp.einsum("rsqb,bskc->rqkc", ahead, first_section, precision=PRECISE)


def forward_signal(signal, tables):
    twisted, ahead, back = tables
    table_high = twisted.astype(jnp.bfloat16)
    table_low = (twisted - table_high.astype(jnp.float32)).astype(jnp.bfloat16)
    first_section = jnp.einsum(
        "bska,abc->bskc", table_high, signal, preferred_element_type=jnp.float32
    ) + jnp.einsum("bska,abc->bskc", table_low, signal, preferred_element_type=jnp.float32)
    return jnp.einsum("rsqb,bskc->rqkc", ahead, first_section, precision=PRECISE)


def inverse(spectrum, pattern, tables, points):
    twisted, ahead, back = tables
    middle = jnp.einsum("rsbq,sqkc->brkc", back, spectrum, precision=PRECISE)
    return jnp.einsum(pattern, twisted, middle, precision=PRECISE) * (1.0 / points)


def local(query, key_stream, value_stream, upstream, bases, base_rows, long_filter, skip_weight):
    groups = lax.axis_size("seq")
    tok_rows = query.shape[1]
    length = tok_rows * groups
    points = 2 * length
    inner_len = 64
    outer_len = points // inner_len
    half_outer = outer_len // 2
    channels = long_filter.shape[0]
    ahead, back = inner_tables(inner_len)
    tables = (outer_table(inner_len, outer_len, half_outer, points), ahead, back)
    filter_scale = length ** (-0.5)
    query_rows = query[0].astype(jnp.float32)
    key_rows = key_stream[0].astype(jnp.float32)
    value_rows = value_stream[0].astype(jnp.float32)
    one_hot = (
        bases[0][:, None] == jnp.arange(base_rows.shape[0], dtype=jnp.int32)[None, :]
    ).astype(jnp.bfloat16)
    out_grad = upstream[0].astype(jnp.float32) - jnp.dot(
        one_hot, base_rows, preferred_element_type=jnp.float32
    )
    gated = (key_rows * value_rows).astype(jnp.bfloat16)
    conv_grad = (out_grad * query_rows).astype(jnp.bfloat16)
    gated_cols, grad_cols = (
        lax.all_to_all(gated, "seq", split_axis=1, concat_axis=0, tiled=True),
        lax.all_to_all(conv_grad, "seq", split_axis=1, concat_axis=0, tiled=True),
    )
    all_taps = lax.all_gather(long_filter.astype(jnp.bfloat16), "dp", axis=1, tiled=True).astype(
        long_filter.dtype
    )
    filt_spectrum = forward_taps(all_taps.reshape(channels, half_outer, inner_len), tables)
    filt_real = filt_spectrum[0] * filter_scale
    filt_imag = filt_spectrum[1] * filter_scale
    both_cols = jnp.concatenate([gated_cols, grad_cols], axis=1)
    signal_spectrum = forward_signal(both_cols.reshape(half_outer, inner_len, 2 * channels), tables)
    sig_real = signal_spectrum[0]
    sig_imag = signal_spectrum[1]
    wide_real = jnp.concatenate([filt_real, filt_real], axis=-1)
    wide_imag = jnp.concatenate([filt_imag, -filt_imag], axis=-1)
    product = jnp.stack(
        [sig_real * wide_real - sig_imag * wide_imag, sig_real * wide_imag + sig_imag * wide_real]
    )
    combined = inverse(product, "bska,bskc->bac", tables, points)
    combined = jnp.transpose(combined, (1, 0, 2)).reshape(length, 2 * channels)
    gated_wide = gated_cols.astype(jnp.float32)
    grad_wide = grad_cols.astype(jnp.float32)
    conv_out = (combined[:, :channels] + skip_weight * gated_wide).astype(jnp.bfloat16)
    corr_out = (combined[:, channels:] + skip_weight * grad_wide).astype(jnp.bfloat16)
    conv_rows, corr_rows = (
        lax.all_to_all(conv_out, "seq", split_axis=0, concat_axis=1, tiled=True),
        lax.all_to_all(corr_out, "seq", split_axis=0, concat_axis=1, tiled=True),
    )
    gated_real = sig_real[..., :channels]
    gated_imag = sig_imag[..., :channels]
    grad_real = sig_real[..., channels:]
    grad_imag = sig_imag[..., channels:]
    cross = jnp.stack(
        [
            gated_real * grad_real + gated_imag * grad_imag,
            gated_real * grad_imag - gated_imag * grad_real,
        ]
    )
    tap_grad = inverse(cross, "bska,bskc->cab", tables, points).reshape(channels, length)
    filter_grad = (
        lax.psum_scatter(
            tap_grad.astype(jnp.bfloat16), "dp", scatter_dimension=1, tiled=True
        ).astype(jnp.float32)
        * filter_scale
    )
    corr_wide = corr_rows.astype(jnp.float32)
    query_grad = (out_grad * conv_rows.astype(jnp.float32)).astype(jnp.bfloat16)[None]
    key_grad = (corr_wide * value_rows).astype(jnp.bfloat16)[None]
    value_grad = (corr_wide * key_rows).astype(jnp.bfloat16)[None]
    return (query_grad, key_grad, value_grad, filter_grad)


def solution(mesh):
    return jax.shard_map(
        local,
        mesh=mesh,
        in_specs=(
            P("dp", "seq", None),
            P("dp", "seq", None),
            P("dp", "seq", None),
            P("dp", "seq", None),
            P("dp", "seq"),
            P(),
            P("seq", "dp"),
            P("seq"),
        ),
        out_specs=(
            P("dp", "seq", None),
            P("dp", "seq", None),
            P("dp", "seq", None),
            P("seq", "dp"),
        ),
        check_vma=False,
    )
```

profile of v0, /device:TPU:2, one launch (start us, length us, event | category | flops | bytes accessed | tf_op | source)
XLA Modules:
  0.0 368.2 jit_solution(2775089772217987518)
XLA Ops:
  13.6 11.6 %all-to-all-start.1 = ((bf16[128,32,128]{2,0,1:T(8,128)(2,1)}), bf16[128,32,128]{2,0,1:T(8,128)(2,1)S(1)}, u32[]{:S(2)}, u32[]{:S(2)}) async-start(bf16[128,32,128]{2,0,1:T(8,128)(2,1)} %copy_bitcast_fusion), calls=%async_computation.1 | async-start | bytes 2097152 | tf_op jit(solution)/shard_map/all_to_all | solution.py:78
  30.3 24.4 %all-to-all-done.1 = bf16[128,32,128]{2,0,1:T(8,128)(2,1)S(1)} async-done(((bf16[128,32,128]{2,0,1:T(8,128)(2,1)}), bf16[128,32,128]{2,0,1:T(8,128)(2,1)S(1)}, u32[]{:S(2)}, u32[]{:S(2)}) %all-to-all-start.1) | async-done | bytes 1048608 | tf_op jit(solution)/shard_map/all_to_all | solution.py:78
  54.6 6.8 %all-to-all-start = ((bf16[128,32,128]{0,2,1:T(8,128)(2,1)}), bf16[128,32,128]{0,2,1:T(8,128)(2,1)}, u32[]{:S(2)}, u32[]{:S(2)}) async-start(bf16[128,32,128]{0,2,1:T(8,128)(2,1)} %bitcast.137), calls=%async_computation | async-start | bytes 2097152 | tf_op jit(solution)/shard_map/all_to_all | solution.py:77
  61.7 9.8 %fusion.60 = (f32[64,1,128,64]{2,3,1,0:T(8,128)S(1)}, f32[64,1,128,64]{2,3,1,0:T(8,128)}) fusion(s32[64,64]{1,0:T(8,128)S(1)} %iota_add_fusion), kind=kLoop, calls=%fused_computation.77 | loop fusion | flops 7864320 | bytes 4210688 | tf_op jit(solution)/shard_map/cos | solution.py:17
  71.5 7.6 %all-gather.2.cloned.1.call-done = bf16[128,4096]{0,1:T(8,128)(2,1)} async-done(((bf16[128,512]{0,1:T(8,128)(2,1)}), bf16[128,4096]{0,1:T(8,128)(2,1)}) %all-gather.2.cloned.1.call-update) | async-done | bytes 1048592 | tf_op jit(solution)/shard_map/all_gather | solution.py:80
  79.0 9.2 %fusion.53 = f32[64,2,128,128]{3,2,1,0:T(8,128)S(1)} fusion(f32[64,1,128,64]{2,3,1,0:T(8,128)} %get-tuple-element.34, f32[64,1,128,64]{2,3,1,0:T(8,128)S(1)} %get-tuple-element.33, bf16[128,64,64,1]{0,2,1,3:T(8,128)(2,1)} %bitcast.141), kind=kOutput, calls=%fused_computation.71 | convolution fusion | flops 1611661312 | bytes 13631488 | tf_op jit(solution)/shard_map/bska,cab->bskc/dot_general | solution.py:33
  88.3 12.1 %fusion.25 = f32[2,64,128,128]{3,1,2,0:T(8,128)S(1)} fusion(f32[64,2,128,128]{3,2,1,0:T(8,128)S(1)} %fusion.53, f32[1,2,64,64]{3,2,1,0:T(8,128)S(1)} %get-tuple-element.28, f32[1,2,64,64]{3,2,1,0:T(8,128)S(1)} %get-tuple-element.31), kind=kOutput, calls=%fused_computation.36 | convolution fusion | flops 3221241856 | bytes 16842752 | tf_op jit(solution)/shard_map/rsqb,bskc->rqkc/dot_general | solution.py:34
  100.4 5.0 %slice_multiply_fusion = (f32[1,64,128,128]{3,1,2,0:T(8,128)}, f32[1,64,128,128]{3,1,2,0:T(8,128)}, f32[1,64,128,128]{3,1,2,0:T(8,128)}) fusion(f32[2,64,128,128]{3,1,2,0:T(8,128)S(1)} %fusion.25), kind=kLoop, calls=%fused_computation.28 | loop fusion | flops 3145728 | bytes 20971520 | tf_op jit(solution)/shard_map/mul | solution.py:85
  110.3 9.9 %fusion.52 = f32[64,2,128,256]{3,2,1,0:T(8,128)} fusion(bf16[64,64,128]{2,0,1:T(8,128)(2,1)S(1)} %copy.23, bf16[64,64,128]{2,0,1:T(8,128)(2,1)S(1)} %copy.22, f32[64,1,128,64]{2,3,1,0:T(8,128)} %get-tuple-element.34, f32[64,1,128,64]{2,3,1,0:T(8,128)S(1)} %get-tuple-element.33), kind=kOutput, calls=%fused_computation.70 | convolution fusion | flops 542113792 | bytes 23068672 | tf_op jit(solution)/shard_map/bska,abc->bskc/dot_general | solution.py:41
  120.2 10.5 %convolution_add_fusion = f32[64,2,128,256]{3,2,1,0:T(8,128)} fusion(f32[64,2,128,256]{3,2,1,0:T(8,128)} %fusion.52, bf16[64,64,128]{2,0,1:T(8,128)(2,1)S(1)} %copy.23, bf16[64,64,128]{2,0,1:T(8,128)(2,1)S(1)} %copy.22, f32[64,1,128,64]{2,3,1,0:T(8,128)S(1)} %copy-done.2, f32[64,1,128,64]{2,3,1,0:T(8,128)S(1)} %get-tuple-element.33), kind=kOutput, calls=%fused_computation.8 | convolution fusion | flops 550502400 | bytes 39845888 | tf_op jit(solution)/shard_map/bska,abc->bskc/dot_general | solution.py:43
  130.7 33.0 %fusion.21 = f32[2,64,128,256]{3,1,2,0:T(8,128)} fusion(f32[64,2,128,256]{3,2,1,0:T(8,128)} %convolution_add_fusion, f32[1,2,64,64]{3,2,1,0:T(8,128)S(1)} %get-tuple-element.28, f32[1,2,64,64]{3,2,1,0:T(8,128)S(1)} %get-tuple-element.31), kind=kOutput, calls=%fused_computation.26 | convolution fusion | flops 6442467328 | bytes 33619968 | tf_op jit(solution)/shard_map/rsqb,bskc->rqkc/dot_general | solution.py:44
  163.7 24.5 %slice_bitcast_fusion.1 = (f32[64,128,256]{2,0,1:T(8,128)}, f32[64,128,256]{2,0,1:T(8,128)}, f32[1,64,128,256]{3,1,2,0:T(8,128)}, f32[1,64,128,256]{3,1,2,0:T(8,128)}) fusion(f32[2,64,128,256]{3,1,2,0:T(8,128)} %fusion.21, f32[1,64,128,128]{3,1,2,0:T(8,128)} %get-tuple-element.22, f32[1,64,128,128]{3,1,2,0:T(8,128)} %get-tuple-element.21, ...), kind=kLoop, calls=%fused_computation.25 | loop fusion | flops 16777216 | bytes 62914560 | tf_op jit(solution)/shard_map/squeeze | solution.py:88
  188.1 20.1 %fusion.7 = f32[64,2,128,256]{3,0,1,2:T(8,128)} fusion(f32[1,2,64,64]{3,2,1,0:T(8,128)S(1)} %get-tuple-element.32, f32[1,2,64,64]{3,2,1,0:T(8,128)S(1)} %get-tuple-element.27, f32[1,64,128,256]{3,1,2,0:T(8,128)} %get-tuple-element.18, f32[1,64,128,256]{3,1,2,0:T(8,128)} %get-tuple-element.19), kind=kOutput, calls=%fused_computation.9 | convolution fusion | flops 6446661632 | bytes 33619968 | tf_op jit(solution)/shard_map/rsbq,sqkc->brkc/dot_general | solution.py:49
  208.2 25.2 %fusion.24 = f32[64,64,256]{2,0,1:T(8,128)S(1)} fusion(f32[64,2,128,256]{3,0,1,2:T(8,128)} %fusion.7, f32[64,1,128,64]{2,3,1,0:T(8,128)S(1)} %copy-done.2, f32[64,1,128,64]{2,3,1,0:T(8,128)S(1)} %get-tuple-element.33), kind=kOutput, calls=%fused_computation.32 | convolution fusion | flops 3223322624 | bytes 25165824 | tf_op jit(solution)/shard_map/bska,bskc->bac/dot_general | solution.py:50
  233.4 4.4 %copy.30 = f32[64,64,256]{2,1,0:T(8,128)} copy(f32[64,64,256]{2,0,1:T(8,128)S(1)} %fusion.24) | data formatting | bytes 8388608 | tf_op jit(solution)/shard_map/mul | solution.py:50
  243.8 4.7 %fusion.40 = (bf16[4096,128]{1,0:T(8,128)(2,1)}, bf16[4096,128]{1,0:T(8,128)(2,1)}) fusion(f32[4096,256]{1,0:T(8,128)} %bitcast.135, bf16[128,32,128]{2,0,1:T(8,128)(2,1)S(1)} %copy-done.9, f32[128]{0:T(128)S(1)} %copy-done.16, f32[32,128,128]{2,1,0:T(8,128)} %copy.31), kind=kLoop, calls=%fused_computation.53 | loop fusion | flops 3670016 | bytes 9437696 | tf_op jit(solution)/shard_map/convert_element_type | solution.py:100
  248.4 10.2 %all-to-all-start.3 = ((bf16[32,128,128]{2,1,0:T(8,128)(2,1)}), bf16[32,128,128]{2,1,0:T(8,128)(2,1)S(1)}, u32[]{:S(2)}, u32[]{:S(2)}) async-start(bf16[32,128,128]{2,1,0:T(8,128)(2,1)} %bitcast.138), calls=%async_computation.3 | async-start | bytes 2097152 | tf_op jit(solution)/shard_map/all_to_all | solution.py:103
  258.6 9.3 %add_bitcast_fusion = (f32[1,64,128,128]{3,1,2,0:T(8,128)}, f32[1,64,128,128]{3,1,2,0:T(8,128)}) fusion(f32[64,128,256]{2,0,1:T(8,128)} %get-tuple-element.17, f32[64,128,256]{2,0,1:T(8,128)} %get-tuple-element.16), kind=kLoop, calls=%fused_computation.34 | loop fusion | flops 6291456 | bytes 25165824 | tf_op jit(solution)/shard_map/stack | solution.py:109
  268.0 15.6 %all-to-all-done.3 = bf16[32,128,128]{2,1,0:T(8,128)(2,1)S(1)} async-done(((bf16[32,128,128]{2,1,0:T(8,128)(2,1)}), bf16[32,128,128]{2,1,0:T(8,128)(2,1)S(1)}, u32[]{:S(2)}, u32[]{:S(2)}) %all-to-all-start.3) | async-done | bytes 1048608 | tf_op jit(solution)/shard_map/all_to_all | solution.py:103
  283.6 8.4 %all-to-all-start.2 = ((bf16[32,128,128]{2,1,0:T(8,128)(2,1)}), bf16[32,128,128]{2,1,0:T(8,128)(2,1)}, u32[]{:S(2)}, u32[]{:S(2)}) async-start(bf16[32,128,128]{2,1,0:T(8,128)(2,1)} %bitcast.36), calls=%async_computation.2 | async-start | bytes 2097152 | tf_op jit(solution)/shard_map/all_to_all | solution.py:102
  292.1 11.0 %fusion.28 = f32[64,2,128,128]{3,0,1,2:T(8,128)S(1)} fusion(f32[1,2,64,64]{3,2,1,0:T(8,128)S(1)} %get-tuple-element.32, f32[1,2,64,64]{3,2,1,0:T(8,128)S(1)} %get-tuple-element.27, f32[1,64,128,128]{3,1,2,0:T(8,128)} %get-tuple-element.15, f32[1,64,128,128]{3,1,2,0:T(8,128)} %get-tuple-element.14), kind=kOutput, calls=%fused_computation.37 | convolution fusion | flops 3223339008 | bytes 16842752 | tf_op jit(solution)/shard_map/rsbq,sqkc->brkc/dot_general | solution.py:49
  303.1 10.8 %fusion.49 = bf16[128,64,64]{0,1,2:T(8,128)(2,1)S(1)} fusion(f32[64,2,128,128]{3,0,1,2:T(8,128)S(1)} %fusion.28, f32[64,1,128,64]{2,3,1,0:T(8,128)S(1)} %copy-done.3, f32[64,1,128,64]{2,3,1,0:T(8,128)S(1)} %get-tuple-element.33), kind=kOutput, calls=%fused_computation.69 | convolution fusion | flops 1612709888 | bytes 13631488 | tf_op jit(solution)/shard_map/bska,bskc->cab/dot_general | solution.py:50
  318.9 3.8 %fusion.33 = (bf16[1,128,4096]{1,2,0:T(8,128)(2,1)}, bf16[1,128,4096]{1,2,0:T(8,128)(2,1)}) fusion(bf16[1,128,4096]{1,2,0:T(8,128)(2,1)} %copy-done.12, f32[128,32,128]{0,2,1:T(8,128)} %copy.33, bf16[1,128,4096]{1,2,0:T(8,128)(2,1)S(1)} %copy-done.11), kind=kLoop, calls=%fused_computation.44 | loop fusion | flops 3145728 | bytes 6291456 | tf_op jit(solution)/shard_map/convert_element_type | solution.py:125
  329.6 29.8 %reduce-scatter.2.cloned.1.call-done = bf16[128,512]{0,1:T(8,128)(2,1)} async-done(((bf16[128,4096]{0,1:T(8,128)(2,1)}), bf16[128,512]{0,1:T(8,128)(2,1)}) %reduce-scatter.2.cloned.1.call-update) | async-done | bytes 131088 | tf_op jit(solution)/shard_map/reduce_scatter | solution.py:117
  (64 shorter events, 36.1 us)
Async XLA Ops:
  7.2 0.8 copy-start
  7.9 17.4 %copy-start.15 = (f32[128,512]{1,0:T(8,128)S(1)}, f32[128,512]{1,0:T(8,128)}, u32[]{:S(2)}) copy-start(f32[128,512]{1,0:T(8,128)} %param.14) | copy-start | bytes 786436
  9.7 1.3 copy-start.4
  11.1 15.2 %copy-start.14 = (bf16[1,128,4096]{2,1,0:T(8,128)(2,1)S(1)}, bf16[1,128,4096]{2,1,0:T(8,128)(2,1)}, u32[]{:S(2)}) copy-start(bf16[1,128,4096]{2,1,0:T(8,128)(2,1)} %param.10) | copy-start | bytes 3145732
  13.6 41.0 %all-to-all-start.1 = ((bf16[128,32,128]{2,0,1:T(8,128)(2,1)}), bf16[128,32,128]{2,0,1:T(8,128)(2,1)S(1)}, u32[]{:S(2)}, u32[]{:S(2)}) async-start(bf16[128,32,128]{2,0,1:T(8,128)(2,1)} %copy_bitcast_fusion), calls=%async_computation.1 | async-start | bytes 2097152 | tf_op jit(solution)/shard_map/all_to_all | solution.py:78
  25.2 53.8 %all-gather.2.cloned.1.call-start = ((), (), s32[]{:S(2)}) async-start(), calls=%async_computation.5 | async-start | bytes 1179648 | tf_op jit(solution)/shard_map/all_gather | solution.py:80
  26.9 34.7 %copy-start.10 = (bf16[1,128,4096]{1,2,0:T(8,128)(2,1)}, bf16[1,128,4096]{1,2,0:T(8,128)(2,1)S(1)}, u32[]{:S(2)}) copy-start(bf16[1,128,4096]{1,2,0:T(8,128)(2,1)S(1)} %copy.19) | copy-start | bytes 3145732
  28.9 32.7 %copy-start.12 = (bf16[1,128,4096]{1,2,0:T(8,128)(2,1)}, bf16[1,128,4096]{1,2,0:T(8,128)(2,1)S(1)}, u32[]{:S(2)}) copy-start(bf16[1,128,4096]{1,2,0:T(8,128)(2,1)S(1)} %copy.18) | copy-start | bytes 3145732
  54.6 33.6 %copy-start.7 = (bf16[128,32,128]{2,0,1:T(8,128)(2,1)}, bf16[128,32,128]{2,0,1:T(8,128)(2,1)S(1)}, u32[]{:S(2)}) copy-start(bf16[128,32,128]{2,0,1:T(8,128)(2,1)S(1)} %all-to-all-done.1) | copy-start | bytes 3145732
  54.6 51.5 %all-to-all-start = ((bf16[128,32,128]{0,2,1:T(8,128)(2,1)}), bf16[128,32,128]{0,2,1:T(8,128)(2,1)}, u32[]{:S(2)}, u32[]{:S(2)}) async-start(bf16[128,32,128]{0,2,1:T(8,128)(2,1)} %bitcast.137), calls=%async_computation | async-start | bytes 2097152 | tf_op jit(solution)/shard_map/all_to_all | solution.py:77
  100.4 5.0 %copy-start.8 = (bf16[128,32,128]{2,0,1:T(8,128)(2,1)S(1)}, bf16[128,32,128]{2,0,1:T(8,128)(2,1)}, u32[]{:S(2)}) copy-start(bf16[128,32,128]{2,0,1:T(8,128)(2,1)} %copy-done.7) | copy-start | bytes 3145732
  110.3 9.9 %copy-start.2 = (f32[64,1,128,64]{2,3,1,0:T(8,128)S(1)}, f32[64,1,128,64]{2,3,1,0:T(8,128)}, u32[]{:S(2)}) copy-start(f32[64,1,128,64]{2,3,1,0:T(8,128)} %get-tuple-element.34) | copy-start | bytes 6291460
  130.7 33.0 %copy-start.6 = (f32[1,64,128,128]{3,1,2,0:T(8,128)S(1)}, f32[1,64,128,128]{3,1,2,0:T(8,128)}, u32[]{:S(2)}) copy-start(f32[1,64,128,128]{3,1,2,0:T(8,128)} %get-tuple-element.20) | copy-start | bytes 12582916
  237.8 5.9 %copy-start.9 = (bf16[128,32,128]{2,0,1:T(8,128)(2,1)S(1)}, bf16[128,32,128]{2,0,1:T(8,128)(2,1)}, u32[]{:S(2)}) copy-start(bf16[128,32,128]{2,0,1:T(8,128)(2,1)} %copy-done.7) | copy-start | bytes 3145732
  237.8 5.9 %copy-start.16 = (f32[128]{0:T(128)S(1)}, f32[128]{0:T(128)}, u32[]{:S(2)}) copy-start(f32[128]{0:T(128)} %param.15) | copy-start | bytes 1540
  248.4 35.1 %all-to-all-start.3 = ((bf16[32,128,128]{2,1,0:T(8,128)(2,1)}), bf16[32,128,128]{2,1,0:T(8,128)(2,1)S(1)}, u32[]{:S(2)}, u32[]{:S(2)}) async-start(bf16[32,128,128]{2,1,0:T(8,128)(2,1)} %bitcast.138), calls=%async_computation.3 | async-start | bytes 2097152 | tf_op jit(solution)/shard_map/all_to_all | solution.py:103
  283.6 19.5 %copy-start.13 = (bf16[32,128,128]{2,1,0:T(8,128)(2,1)}, bf16[32,128,128]{2,1,0:T(8,128)(2,1)S(1)}, u32[]{:S(2)}) copy-start(bf16[32,128,128]{2,1,0:T(8,128)(2,1)S(1)} %all-to-all-done.3) | copy-start | bytes 3145732
  283.6 43.6 %all-to-all-start.2 = ((bf16[32,128,128]{2,1,0:T(8,128)(2,1)}), bf16[32,128,128]{2,1,0:T(8,128)(2,1)}, u32[]{:S(2)}, u32[]{:S(2)}) async-start(bf16[32,128,128]{2,1,0:T(8,128)(2,1)} %bitcast.36), calls=%async_computation.2 | async-start | bytes 2097152 | tf_op jit(solution)/shard_map/all_to_all | solution.py:102
  292.0 67.4 %reduce-scatter.2.cloned.1.call-start = ((), (), s32[]{:S(2)}) async-start(), calls=%async_computation.6 | async-start | bytes 1179648 | tf_op jit(solution)/shard_map/reduce_scatter | solution.py:117
  292.1 11.0 %copy-start.3 = (f32[64,1,128,64]{2,3,1,0:T(8,128)S(1)}, f32[64,1,128,64]{2,3,1,0:T(8,128)}, u32[]{:S(2)}) copy-start(f32[64,1,128,64]{2,3,1,0:T(8,128)} %get-tuple-element.34) | copy-start | bytes 6291460
  315.5 3.4 copy-start.11
  318.9 8.3 %copy-start.5 = (f32[128,4096]{1,0:T(8,128)S(1)}, f32[128,4096]{1,0:T(8,128)}, u32[]{:S(2)}) copy-start(f32[128,4096]{1,0:T(8,128)} %copy-done.4) | copy-start | bytes 6291460
  322.7 38.5 %copy-start.1 = (bf16[4,4096]{1,0:T(4,128)(2,1)S(1)}, bf16[4,4096]{1,0:T(4,128)(2,1)}, u32[]{:S(2)}) copy-start(bf16[4,4096]{1,0:T(4,128)(2,1)} %param.13) | copy-start | bytes 98308
Sparse Core Ops, SparseCore 0:
  28.4 50.5 all-gather.1
  315.6 43.7 reduce-scatter.1
where the time goes:
time: 373 us; the launch traced here: 368 us
  matrix products  143 us (38%)
  waiting for transfers between devices  77.4 us (21%)
  other arithmetic  69.1 us (19%)
  starting transfers between devices  37.1 us (10%)
  local copies, waits for them, and re-layouts  26.6 us (7%)
  between operations  14.5 us (4%)
    dot_general x2, matrix products, inverse(): jnp.einsum(pattern, twisted, middle, precision=PRECISE) * (1.0 / points)  35.9 us
    dot_general x1, matrix products, forward_signal(): jnp.einsum('rsqb,bskc->rqkc', ahead, first_section, precision=PRECISE)  33 us
    dot_general x2, matrix products, inverse(): middle = jnp.einsum('rsbq,sqkc->brkc', back, spectrum, precision=PRECISE)  31.1 us
    reduce_scatter x1, waiting for transfers between devices, local(): lax.psum_scatter(tap_grad.astype(jnp.bfloat16), 'dp', scatter_dimension=1...  29.8 us
    squeeze x1, other arithmetic, local(): sig_real = signal_spectrum[0]  24.5 us
    all_to_all x1, waiting for transfers between devices, local(): lax.all_to_all(conv_grad, 'seq', split_axis=1, concat_axis=0, tiled=True)  24.4 us
    all_to_all x1, waiting for transfers between devices, local(): lax.all_to_all(corr_out, 'seq', split_axis=0, concat_axis=1, tiled=True)  15.6 us
    dot_general x1, matrix products, forward_taps(): jnp.einsum('rsqb,bskc->rqkc', ahead, first_section, precision=PRECISE)  12.1 us
  transfers between devices with their start and end apart: 6, of which 4 were waited for; matrix products, arithmetic and copies ran while one was open for 24% of the time, Pallas kernels for 0%

commit v1 on v0

v1 whole, which is shorter than its diff:
```python
import math

import jax
import jax.numpy as jnp
import ml_dtypes
import numpy as np
from jax import lax
from jax.experimental import pallas as pl
from jax.experimental.pallas import tpu as pltpu
from jax.sharding import PartitionSpec as P

LANES = 128
SUB = 8
VMEM_BYTES = 56 * 1024 * 1024


def transform_tables(blocks, rows, scale):
    points = 2 * blocks * rows
    half = rows // 2
    low = np.arange(blocks)[:, None, None]
    point = np.arange(blocks)[None, None, :] * rows + np.arange(rows)[None, :, None]
    angle = 2.0 * math.pi / points * (low * point % points)
    first = np.stack([np.cos(angle), -np.sin(angle)], axis=1)
    first[0, 1] = np.where(np.arange(blocks) % 2 == 0, 1.0, -1.0)[None, :]
    first = first.reshape(2 * blocks, rows // SUB, SUB, blocks)
    ahead = np.einsum("mhaj,ab->hmajb", first, np.eye(SUB))
    ahead = ahead.reshape(rows // SUB, 2 * blocks * SUB, blocks * SUB)
    back = np.ascontiguousarray(np.swapaxes(ahead, 1, 2))

    row = np.arange(rows)[None, :]
    high = np.arange(rows)[:, None]
    angle = 2.0 * math.pi / rows * (high * row % rows)
    cosine, sine = np.cos(angle), np.sin(angle)
    usual = np.block([[cosine, sine], [-sine, cosine]])
    odd = 2.0 * math.pi / (2 * rows) * ((2 * high[:half] + 1) * row % (2 * rows))
    blank = np.zeros((half, rows))
    special = np.block(
        [
            [cosine[:half], blank],
            [blank, np.cos(odd)],
            [-sine[:half], blank],
            [blank, -np.sin(odd)],
        ]
    )
    special[rows, :rows] = np.where(np.arange(rows) % 2 == 0, 1.0, -1.0)
    second = np.stack([special, usual])
    weight = np.full((2, 2 * rows, 1), 2.0 / points)
    weight[0, 0] = weight[0, rows] = 1.0 / points
    undo = np.ascontiguousarray(np.swapaxes(second * weight * scale, 1, 2))
    return tuple(table.astype(ml_dtypes.bfloat16) for table in (ahead, back, second, undo))


def dot(left, right):
    return jnp.dot(left, right, preferred_element_type=jnp.float32)


def readout(bases_ref, rows_ref, columns):
    letters = bases_ref[...]
    picked = rows_ref[0:1, columns].astype(jnp.float32)
    for letter in range(1, rows_ref.shape[0]):
        picked = jnp.where(
            letters == letter, rows_ref[letter : letter + 1, columns].astype(jnp.float32), picked
        )
    return picked


def gate_kernel(query_ref, key_ref, value_ref, upstream_ref, bases_ref, rows_ref, out_ref):
    tokens = query_ref.shape[0]
    for block in range(out_ref.shape[0]):
        columns = slice(block * LANES, (block + 1) * LANES)
        gated = key_ref[:, columns].astype(jnp.float32) * value_ref[:, columns].astype(jnp.float32)
        out_grad = upstream_ref[:, columns].astype(jnp.float32) - readout(bases_ref, rows_ref, columns)
        grad = out_grad * query_ref[:, columns].astype(jnp.float32)
        out_ref[block, :tokens, :] = gated.astype(jnp.bfloat16)
        out_ref[block, tokens:, :] = grad.astype(jnp.bfloat16)


def ungate_kernel(back_ref, key_ref, value_ref, upstream_ref, bases_ref, rows_ref, query_out, key_out, value_out):
    tokens = key_ref.shape[0]
    for block in range(back_ref.shape[0]):
        columns = slice(block * LANES, (block + 1) * LANES)
        conv = back_ref[block, :tokens, :].astype(jnp.float32)
        corr = back_ref[block, tokens:, :].astype(jnp.float32)
        out_grad = upstream_ref[:, columns].astype(jnp.float32) - readout(bases_ref, rows_ref, columns)
        query_out[:, columns] = (out_grad * conv).astype(jnp.bfloat16)
        key_out[:, columns] = (corr * value_ref[:, columns].astype(jnp.float32)).astype(jnp.bfloat16)
        value_out[:, columns] = (corr * key_ref[:, columns].astype(jnp.float32)).astype(jnp.bfloat16)


def first_stage(load, ahead_ref, mid_ref):
    for pair in range(ahead_ref.shape[0] // 2):
        both = load(pair)
        for part in range(2):
            step = 2 * pair + part
            piece = both[:, part * SUB : (part + 1) * SUB, :]
            piece = piece.reshape(piece.shape[0] * SUB, piece.shape[2]).astype(jnp.bfloat16)
            mid = dot(ahead_ref[step], piece)
            mid_ref[:, step * SUB : (step + 1) * SUB, :] = mid.reshape(-1, SUB, mid.shape[1])


def last_stage(back_ref, mid_ref, step):
    piece = mid_ref[:, step * SUB : (step + 1) * SUB, :]
    piece = piece.reshape(piece.shape[0] * SUB, piece.shape[2]).astype(jnp.bfloat16)
    out = dot(back_ref[step], piece)
    return out.reshape(-1, SUB, out.shape[1])


def group_of(mid_ref, group):
    both = mid_ref[pl.ds(2 * group, 2)]
    return both.reshape(2 * both.shape[1], both.shape[2])


def taps_kernel(taps_ref, ahead_ref, second_ref, spectrum_ref, mid_ref):
    first_stage(
        lambda pair: taps_ref[:, pair * 2 * SUB : (pair + 1) * 2 * SUB, :].astype(jnp.float32), ahead_ref, mid_ref
    )

    def work(group, which):
        mid = group_of(mid_ref, group).astype(jnp.bfloat16)
        spectrum_ref[group] = dot(second_ref[which], mid)

    work(0, 0)

    @pl.loop(1, spectrum_ref.shape[0])
    def _(group):
        work(group, 1)


def times(left, right, conjugate, first_group):
    half = left.shape[0] // 2
    left_real, left_imag = left[:half], left[half:]
    right_real, right_imag = right[:half], right[half:]
    real_real, imag_imag = left_real * right_real, left_imag * right_imag
    if conjugate:
        real = real_real + imag_imag
        imag = left_imag * right_real - left_real * right_imag
    else:
        real = real_real - imag_imag
        imag = left_imag * right_real + left_real * right_imag
    if first_group:
        apart = lax.broadcasted_iota(jnp.int32, real.shape, 0) == 0
        real = jnp.where(apart, real_real, real)
        imag = jnp.where(apart, imag_imag, imag)
    return jnp.concatenate([real, imag], axis=0)


def main_kernel(
    both_ref, filter_ref, skip_ref, ahead_ref, back_ref, second_ref, undo_ref, out_ref, cross_ref, mid_ref
):
    tokens = both_ref.shape[1] // 2

    def load(pair):
        rows = slice(pair * 2 * SUB, (pair + 1) * 2 * SUB)
        more = slice(tokens + pair * 2 * SUB, tokens + (pair + 1) * 2 * SUB)
        return jnp.concatenate([both_ref[:, rows, :], both_ref[:, more, :]], axis=2).astype(jnp.float32)

    first_stage(load, ahead_ref, mid_ref)

    def work(group, which):
        spectrum = dot(second_ref[which], group_of(mid_ref, group).astype(jnp.bfloat16))
        gated, grad = spectrum[:, :LANES], spectrum[:, LANES:]
        taps = filter_ref[group]
        conv = times(gated, taps, False, which == 0)
        corr = times(grad, taps, True, which == 0)
        cross_ref[group] = times(grad, gated, True, which == 0)
        product = jnp.concatenate([conv, corr], axis=1).astype(jnp.bfloat16)
        undone = dot(undo_ref[which], product)
        mid_ref[pl.ds(2 * group, 2)] = undone.reshape(2, -1, undone.shape[1])

    work(0, 0)

    @pl.loop(1, filter_ref.shape[0])
    def _(group):
        work(group, 1)

    skip = skip_ref[...]
    for pair in range(back_ref.shape[0] // 2):
        sums = jnp.concatenate(
            [last_stage(back_ref, mid_ref, 2 * pair), last_stage(back_ref, mid_ref, 2 * pair + 1)], axis=1
        )
        for part in range(2):
            rows = slice(part * tokens + pair * 2 * SUB, part * tokens + (pair + 1) * 2 * SUB)
            direct = skip * both_ref[:, rows, :].astype(jnp.float32)
            out_ref[:, rows, :] = (sums[:, :, part * LANES : (part + 1) * LANES] + direct).astype(jnp.bfloat16)


def tap_grad_kernel(cross_ref, back_ref, undo_ref, out_ref, mid_ref):
    def work(group, which):
        undone = dot(undo_ref[which], cross_ref[group].astype(jnp.bfloat16))
        mid_ref[pl.ds(2 * group, 2)] = undone.reshape(2, -1, undone.shape[1])

    work(0, 0)

    @pl.loop(1, cross_ref.shape[0])
    def _(group):
        work(group, 1)

    for pair in range(back_ref.shape[0] // 2):
        sums = jnp.concatenate(
            [last_stage(back_ref, mid_ref, 2 * pair), last_stage(back_ref, mid_ref, 2 * pair + 1)], axis=1
        )
        out_ref[:, pair * 2 * SUB : (pair + 1) * 2 * SUB, :] = sums.astype(jnp.bfloat16)


def call(kernel, out_shape, scratch=(), flops=0, moved=0, **grid):
    return pl.pallas_call(
        kernel,
        out_shape=out_shape,
        scratch_shapes=scratch,
        cost_estimate=pl.CostEstimate(flops=flops, bytes_accessed=moved, transcendentals=0),
        compiler_params=pltpu.CompilerParams(vmem_limit_bytes=VMEM_BYTES),
        **grid,
    )


def local(query, key_stream, value_stream, upstream, bases, base_rows, long_filter, skip_weight):
    groups = lax.axis_size("seq")
    tokens, width = query.shape[1:]
    length = tokens * groups
    channels = long_filter.shape[0]
    ahead, back, second, undo = transform_tables(groups, tokens, length ** (-0.5))
    letters = bases.reshape(tokens, 1)
    steps = 8
    per_step = groups // steps
    stream = pl.BlockSpec((None, tokens, width // steps), lambda i: (0, 0, i))
    cols = pl.BlockSpec((per_step, 2 * tokens, channels), lambda i: (i, 0, 0))
    letter_spec = pl.BlockSpec((tokens, 1), lambda i: (0, 0))
    row_spec = pl.BlockSpec((base_rows.shape[0], width // steps), lambda i: (0, i))
    packed = jax.ShapeDtypeStruct((groups, 2 * tokens, channels), jnp.bfloat16)
    array_bytes = tokens * width * 2

    gates = call(
        gate_kernel,
        packed,
        moved=6 * array_bytes,
        grid=(steps,),
        in_specs=[stream, stream, stream, stream, letter_spec, row_spec],
        out_specs=cols,
    )(query, key_stream, value_stream, upstream, letters, base_rows)
    both = lax.all_to_all(gates, "seq", split_axis=0, concat_axis=0, tiled=True)

    all_taps = lax.all_gather(long_filter.T.astype(jnp.bfloat16), "dp", axis=0, tiled=True)
    spectrum_shape = jax.ShapeDtypeStruct((groups, 2 * tokens, channels), jnp.float32)
    one_pass = 2 * 4 * length * 256 * channels
    spectrum = call(
        taps_kernel,
        spectrum_shape,
        [pltpu.VMEM((2 * groups, tokens, channels), jnp.float32)],
        flops=one_pass,
        moved=9 * array_bytes,
    )(all_taps.reshape(groups, tokens, channels), ahead, second)

    out, cross = call(
        main_kernel,
        (packed, spectrum_shape),
        [pltpu.VMEM((2 * groups, tokens, 2 * channels), jnp.float32)],
        flops=4 * one_pass,
        moved=20 * array_bytes,
    )(both, spectrum, skip_weight.reshape(1, channels), ahead, back, second, undo)
    home = lax.all_to_all(out, "seq", split_axis=0, concat_axis=0, tiled=True)

    tap_grad = call(
        tap_grad_kernel,
        jax.ShapeDtypeStruct((groups, tokens, channels), jnp.bfloat16),
        [pltpu.VMEM((2 * groups, tokens, channels), jnp.float32)],
        flops=one_pass,
        moved=9 * array_bytes,
    )(cross, back, undo)
    filter_grad = lax.psum_scatter(
        tap_grad.reshape(length, channels), "dp", scatter_dimension=0, tiled=True
    ).T.astype(jnp.float32)

    grad_shape = jax.ShapeDtypeStruct(query.shape, jnp.bfloat16)
    query_grad, key_grad, value_grad = call(
        ungate_kernel,
        (grad_shape, grad_shape, grad_shape),
        moved=8 * array_bytes,
        grid=(steps,),
        in_specs=[cols, stream, stream, stream, letter_spec, row_spec],
        out_specs=[stream, stream, stream],
    )(home, key_stream, value_stream, upstream, letters, base_rows)
    return (query_grad, key_grad, value_grad, filter_grad)


def solution(mesh):
    return jax.shard_map(
        local,
        mesh=mesh,
        in_specs=(
            P("dp", "seq", None),
            P("dp", "seq", None),
            P("dp", "seq", None),
            P("dp", "seq", None),
            P("dp", "seq"),
            P(),
            P("seq", "dp"),
            P("seq"),
        ),
        out_specs=(
            P("dp", "seq", None),
            P("dp", "seq", None),
            P("dp", "seq", None),
            P("seq", "dp"),
        ),
        check_vma=False,
    )
```

time: 373 us -> 219 us (0.59); the launches traced: 368 us -> 218 us
  matrix products: 143 us -> 0 us
  other arithmetic: 69.1 us -> 2.3 us
  Pallas kernels: 0 us -> 60.2 us
  waiting for transfers between devices: 77.4 us -> 113 us
  local copies, waits for them, and re-layouts: 26.6 us -> 8.56 us
  starting transfers between devices: 37.1 us -> 20.3 us
    dot_general x10 -> x0, matrix products: 143 us -> none  [the longest x2 35.9 us: inverse(): jnp.einsum(pattern, twisted, middle, precision=PRECISE) * (1.0 / points)]
    pallas_call x0 -> x5, Pallas kernels: none -> 60.2 us  [the longest x1 22.6 us: local(): call(main_kernel, (packed, spectrum_shape), [pltpu.VMEM((2 * groups, toke...]
    all_gather x1, waiting for transfers between devices: 7.55 us -> 57 us  [local(): lax.all_gather(long_filter.T.astype(jnp.bfloat16), 'dp', axis=0, tiled=True)]
    all_to_all x4 -> x2, waiting for transfers between devices: 40 us -> 0.01 us  [the longest x1 0.01 us: local(): home = lax.all_to_all(out, 'seq', split_axis=0, concat_axis=0, tiled=True)]
    reduce_scatter x1, waiting for transfers between devices: 29.8 us -> 56 us  [local(): lax.psum_scatter(tap_grad.reshape(length, channels), 'dp', scatter_dimens...]
    squeeze x1 -> x0, other arithmetic: 24.5 us -> none  [local(): sig_real = signal_spectrum[0]]
    all_to_all x4 -> x2, starting transfers between devices: 37 us -> 20.2 us  [the longest x1 11.6 us: local(): both = lax.all_to_all(gates, 'seq', split_axis=0, concat_axis=0, tiled=True)]
    convert_element_type x5 -> x2, other arithmetic: 14.2 us -> 2.3 us  [the longest x1 1.63 us: local(): filter_grad = lax.psum_scatter(tap_grad.reshape(length, channels), 'dp',...]
  transfers between devices with their start and end apart: 6 -> 4, of which waited for: 4 -> 2; matrix products, arithmetic and copies ran while one was open for 24% -> 3% of each run, Pallas kernels for 0% -> 10%
where the time goes in v1:
time: 219 us; the launch traced here: 218 us
  waiting for transfers between devices  113 us (52%)
  Pallas kernels  60.2 us (27%)
  starting transfers between devices  20.3 us (9%)
  between operations  14.1 us (6%)
  local copies, waits for them, and re-layouts  8.56 us (4%)
  other arithmetic  2.3 us (1%)
    all_gather x1, waiting for transfers between devices, local(): lax.all_gather(long_filter.T.astype(jnp.bfloat16), 'dp', axis=0, tiled=True)  57 us
    reduce_scatter x1, waiting for transfers between devices, local(): lax.psum_scatter(tap_grad.reshape(length, channels), 'dp', scatter_dimens...  56 us
    pallas_call x1, Pallas kernels, local(): call(main_kernel, (packed, spectrum_shape), [pltpu.VMEM((2 * groups, toke...  22.6 us
    all_to_all x1, starting transfers between devices, local(): both = lax.all_to_all(gates, 'seq', split_axis=0, concat_axis=0, tiled=True)  11.6 us
    pallas_call x1, Pallas kernels, local(): call(tap_grad_kernel, jax.ShapeDtypeStruct((groups, tokens, channels), jn...  11.3 us
    pallas_call x1, Pallas kernels, local(): call(taps_kernel, spectrum_shape, [pltpu.VMEM((2 * groups, tokens, channe...  11.3 us
    all_to_all x1, starting transfers between devices, local(): home = lax.all_to_all(out, 'seq', split_axis=0, concat_axis=0, tiled=True)  8.58 us
    pallas_call x1, Pallas kernels, local(): call(ungate_kernel, (grad_shape, grad_shape, grad_shape), moved=8 * array...  7.63 us
  transfers between devices with their start and end apart: 4, of which 2 were waited for; matrix products, arithmetic and copies ran while one was open for 3% of the time, Pallas kernels for 10%

profile of v1, /device:TPU:2, one launch (start us, length us, event | category | flops | bytes accessed | tf_op | source)
XLA Modules:
  0.0 218.4 jit_solution(5113412363763641511)
XLA Ops:
  7.2 1.4 copy.16.bases_ref
  8.6 0.0 copy-start.2
  8.6 7.3 %shard_map.147 = bf16[32,256,128]{2,1,0:T(8,128)(2,1)} custom-call(bf16[1,128,4096]{2,1,0:T(8,128)(2,1)} %query_ref.1, bf16[1,128,4096]{2,1,0:T(8,128)(2,1)} %key_ref.3, bf16[1,128,4096]{2,1,0:T(8,128)(2,1)} %value_ref.3, bf16[1,128,4096]{2,1,0:T(8,128)(2,1)} %upstream_ref.3, s32[128,1]{1,0:T(8,128)} %copy.16.bases_ref, bf16[4,4096]{1,0:T(4,128)(2,1)} %rows_ref.3), custom_call_target="tpu_custom_call" | custom-call | bytes 6291456 | tf_op jit(solution)/shard_map/pallas_call | solution.py:232
  15.9 11.6 %all-to-all-start = ((bf16[32,256,128]{2,1,0:T(8,128)(2,1)}), bf16[32,256,128]{2,1,0:T(8,128)(2,1)S(1)}, u32[]{:S(2)}, u32[]{:S(2)}) async-start(bf16[32,256,128]{2,1,0:T(8,128)(2,1)} %shard_map.147), calls=%async_computation | async-start | bytes 4194304 | tf_op jit(solution)/shard_map/all_to_all | solution.py:240
  27.5 0.0 all-gather.2.cloned.1.call-start
  27.6 0.0 copy-done.2
  27.6 0.7 convert_bitcast_fusion.1
  28.2 0.0 all-gather.2.cloned.1.call-update
  28.3 57.0 %all-gather.2.cloned.1.call-done = bf16[4096,128]{0,1:T(8,128)(2,1)} async-done(((bf16[512,128]{0,1:T(8,128)(2,1)}), bf16[4096,128]{0,1:T(8,128)(2,1)}) %all-gather.2.cloned.1.call-update) | async-done | bytes 1048592 | tf_op jit(solution)/shard_map/all_gather | solution.py:242
  85.2 2.3 %copy.17 = bf16[4096,128]{1,0:T(8,128)(2,1)} copy(bf16[4096,128]{0,1:T(8,128)(2,1)} %all-gather.2.cloned.1.call-done) | data formatting | bytes 2097152 | tf_op jit(solution)/shard_map/all_gather | solution.py:242
  87.5 11.3 %shard_map.148.filter_ref = f32[32,256,128]{2,1,0:T(8,128)} custom-call(bf16[32,128,128]{2,1,0:T(8,128)(2,1)} %bitcast.9, bf16[16,512,256]{2,1,0:T(8,128)(2,1)} %constant.8.clone.ahead_ref, bf16[2,256,256]{2,1,0:T(8,128)(2,1)} %constant.9.clone.second_ref), custom_call_target="tpu_custom_call" | custom-call | flops 1073741824 | bytes 9437184 | tf_op jit(solution)/shard_map/pallas_call | solution.py:245
  98.7 0.0 all-to-all-done.both_ref
  98.7 1.3 copy-done.1
  100.1 22.6 %shard_map.149 = (bf16[32,256,128]{2,1,0:T(8,128)(2,1)}, f32[32,256,128]{2,1,0:T(8,128)}) custom-call(bf16[32,256,128]{2,1,0:T(8,128)(2,1)} %copy-done.1, f32[32,256,128]{2,1,0:T(8,128)} %shard_map.148.filter_ref, f32[1,128]{1,0:T(1,128)} %bitcast.11, bf16[16,512,256]{2,1,0:T(8,128)(2,1)} %constant.8.clone.ahead_ref, ...), custom_call_target="tpu_custom_call" | custom-call | flops 4294967296 | bytes 20971520 | tf_op jit(solution)/shard_map/pallas_call | solution.py:253
  122.7 8.6 %all-to-all-start.1 = ((bf16[32,256,128]{2,1,0:T(8,128)(2,1)}), bf16[32,256,128]{2,1,0:T(8,128)(2,1)S(1)}, u32[]{:S(2)}, u32[]{:S(2)}) async-start(bf16[32,256,128]{2,1,0:T(8,128)(2,1)} %get-tuple-element.9), calls=%async_computation.1 | async-start | bytes 4194304 | tf_op jit(solution)/shard_map/all_to_all | solution.py:260
  131.3 0.0 reduce-scatter.2.cloned.1.call-start
  131.3 11.3 %shard_map.151 = bf16[32,128,128]{2,1,0:T(8,128)(2,1)} custom-call(f32[32,256,128]{2,1,0:T(8,128)} %get-tuple-element.13.cross_ref, bf16[16,256,512]{2,1,0:T(8,128)(2,1)} %constant.10.clone.back_ref, bf16[2,256,256]{2,1,0:T(8,128)(2,1)} %constant.11.clone.undo_ref), custom_call_target="tpu_custom_call" | custom-call | flops 1073741824 | bytes 9437184 | tf_op jit(solution)/shard_map/pallas_call | solution.py:262
  142.7 2.3 %copy.19 = bf16[4096,128]{0,1:T(8,128)(2,1)} copy(bf16[4096,128]{1,0:T(8,128)(2,1)} %bitcast.8) | data formatting | bytes 2097152 | tf_op jit(solution)/shard_map/reshape | solution.py:270
  144.9 0.0 reduce-scatter.2.cloned.1.call-update
  145.0 56.0 %reduce-scatter.2.cloned.1.call-done = bf16[512,128]{0,1:T(8,128)(2,1)} async-done(((bf16[4096,128]{0,1:T(8,128)(2,1)}), bf16[512,128]{0,1:T(8,128)(2,1)}) %reduce-scatter.2.cloned.1.call-update) | async-done | bytes 131088 | tf_op jit(solution)/shard_map/reduce_scatter | solution.py:269
  201.0 1.6 convert_bitcast_fusion
  202.6 0.0 all-to-all-done.1.back_ref
  202.6 1.3 copy-done
  204.0 7.6 %shard_map.150 = (bf16[1,128,4096]{2,1,0:T(8,128)(2,1)}, bf16[1,128,4096]{2,1,0:T(8,128)(2,1)}, bf16[1,128,4096]{2,1,0:T(8,128)(2,1)}) custom-call(bf16[32,256,128]{2,1,0:T(8,128)(2,1)} %copy-done, bf16[1,128,4096]{2,1,0:T(8,128)(2,1)} %key_ref.3, bf16[1,128,4096]{2,1,0:T(8,128)(2,1)} %value_ref.3, bf16[1,128,4096]{2,1,0:T(8,128)(2,1)} %upstream_ref.3, ...), custom_call_target="tpu_custom_call" | custom-call | bytes 8388608 | tf_op jit(solution)/shard_map/pallas_call | solution.py:274
  (2 shorter events, 0.0 us)
Async XLA Ops:
  8.6 19.0 %copy-start.2 = (f32[128,512]{1,0:T(8,128)S(1)}, f32[128,512]{1,0:T(8,128)}, u32[]{:S(2)}) copy-start(f32[128,512]{1,0:T(8,128)} %param.18) | copy-start | bytes 786436
  15.9 82.9 %all-to-all-start = ((bf16[32,256,128]{2,1,0:T(8,128)(2,1)}), bf16[32,256,128]{2,1,0:T(8,128)(2,1)S(1)}, u32[]{:S(2)}, u32[]{:S(2)}) async-start(bf16[32,256,128]{2,1,0:T(8,128)(2,1)} %shard_map.147), calls=%async_computation | async-start | bytes 4194304 | tf_op jit(solution)/shard_map/all_to_all | solution.py:240
  27.5 57.7 %all-gather.2.cloned.1.call-start = ((), (), s32[]{:S(2)}) async-start(), calls=%async_computation.3 | async-start | bytes 1179648 | tf_op jit(solution)/shard_map/all_gather | solution.py:242
  98.7 1.3 copy-start.1
  122.7 79.9 %all-to-all-start.1 = ((bf16[32,256,128]{2,1,0:T(8,128)(2,1)}), bf16[32,256,128]{2,1,0:T(8,128)(2,1)S(1)}, u32[]{:S(2)}, u32[]{:S(2)}) async-start(bf16[32,256,128]{2,1,0:T(8,128)(2,1)} %get-tuple-element.9), calls=%async_computation.1 | async-start | bytes 4194304 | tf_op jit(solution)/shard_map/all_to_all | solution.py:260
  131.3 69.7 %reduce-scatter.2.cloned.1.call-start = ((), (), s32[]{:S(2)}) async-start(), calls=%async_computation.4 | async-start | bytes 1179648 | tf_op jit(solution)/shard_map/reduce_scatter | solution.py:269
  202.6 1.3 copy-start
Sparse Core Ops, SparseCore 0:
  30.7 54.4 all-gather.1
  145.1 55.8 reduce-scatter.1

commit v2 on v1

v2 whole, which is shorter than its diff:
```python
import math

import jax
import jax.numpy as jnp
import ml_dtypes
import numpy as np
from jax import lax
from jax.experimental import pallas as pl
from jax.experimental.pallas import tpu as pltpu
from jax.sharding import PartitionSpec as P

LANES = 128
SUB = 8
PIECES = 8
UNROLL = 8
MEGA = 1024 * 1024
VMEM = pltpu.VMEM
bf16 = jnp.bfloat16


def transform_tables(blocks, rows, scale):
    points = 2 * blocks * rows
    low = 2 * np.arange(blocks)[:, None, None] + 1
    point = np.arange(blocks)[None, None, :] * rows + np.arange(rows)[None, :, None]
    angle = math.pi / points * (low * point % (2 * points))
    first = np.stack([np.cos(angle), -np.sin(angle)], axis=1)
    first = first.reshape(2 * blocks, rows // SUB, SUB, blocks)
    ahead = np.einsum("mhaj,ab->hmajb", first, np.eye(SUB))
    ahead = ahead.reshape(rows // SUB, 2 * blocks * SUB, blocks * SUB)
    back = np.ascontiguousarray(np.swapaxes(ahead, 1, 2))

    row = np.arange(rows)
    angle = 2.0 * math.pi / rows * (row[:, None] * row[None, :] % rows)
    cosine, sine = np.cos(angle), np.sin(angle)
    second = np.block([[cosine, sine], [-sine, cosine]])
    undo = np.ascontiguousarray(second.T) * (2.0 / points * scale)
    return tuple(table.astype(ml_dtypes.bfloat16) for table in (ahead, back, second, undo))


def dot(left, right):
    return jnp.dot(left, right, preferred_element_type=jnp.float32)


def letters_of(bases_ref):
    count = bases_ref.shape[1]
    return jnp.transpose(jnp.broadcast_to(bases_ref[...], (count, count)))


def readout(letters, rows_ref, columns):
    rows = rows_ref[:, columns].astype(jnp.float32)
    picked = rows[0:1]
    for letter in range(1, rows.shape[0]):
        picked = jnp.where(letters == letter, rows[letter : letter + 1], picked)
    return picked


def gate_kernel(query, key, value, upstream, bases_ref, rows_ref, out_ref, held, sems):
    tokens, width = query.shape[1:]
    span = width // PIECES
    copies = []
    for piece in range(PIECES):
        columns = pl.ds(piece * span, span)
        row = []
        for which, source in enumerate((query, key, value, upstream)):
            copy = pltpu.make_async_copy(
                source.at[0, :, columns], held.at[which, :, columns], sems.at[which, piece]
            )
            copy.start()
            row.append(copy)
        copies.append(row)
    letters = letters_of(bases_ref)
    for piece in range(PIECES):
        for copy in copies[piece]:
            copy.wait()
        for block in range(piece * span // LANES, (piece + 1) * span // LANES):
            columns = slice(block * LANES, (block + 1) * LANES)
            query_rows, key_rows, value_rows, upstream_rows = (
                held[which, :, columns].astype(jnp.float32) for which in range(4)
            )
            out_grad = upstream_rows - readout(letters, rows_ref, columns)
            out_ref[block, :tokens, :] = (key_rows * value_rows).astype(bf16)
            out_ref[block, tokens:, :] = (out_grad * query_rows).astype(bf16)


def ungate_kernel(back_ref, key_ref, value_ref, upstream_ref, bases_ref, rows_ref, *rest):
    outs, (held, sems) = rest[:3], rest[3:]
    tokens, width = key_ref.shape[1:]
    span = width // PIECES
    letters = letters_of(bases_ref)
    copies = []
    for piece in range(PIECES):
        for block in range(piece * span // LANES, (piece + 1) * span // LANES):
            columns = slice(block * LANES, (block + 1) * LANES)
            conv = back_ref[block, :tokens, :].astype(jnp.float32)
            corr = back_ref[block, tokens:, :].astype(jnp.float32)
            out_grad = upstream_ref[0, :, columns].astype(jnp.float32) - readout(letters, rows_ref, columns)
            held[0, :, columns] = (out_grad * conv).astype(bf16)
            held[1, :, columns] = (corr * value_ref[0, :, columns].astype(jnp.float32)).astype(bf16)
            held[2, :, columns] = (corr * key_ref[0, :, columns].astype(jnp.float32)).astype(bf16)
        columns = pl.ds(piece * span, span)
        for which, target in enumerate(outs):
            copy = pltpu.make_async_copy(
                held.at[which, :, columns], target.at[0, :, columns], sems.at[which, piece]
            )
            copy.start()
            copies.append(copy)
    for copy in copies:
        copy.wait()


def turn_kernel(in_ref, out_ref):
    wide, high = out_ref.shape[0] // LANES, out_ref.shape[1] // LANES
    for row in range(wide):
        for column in range(high):
            rows, columns = slice(row * LANES, (row + 1) * LANES), slice(column * LANES, (column + 1) * LANES)
            out_ref[rows, columns] = jnp.transpose(in_ref[columns, rows].astype(jnp.float32)).astype(out_ref.dtype)


def first_stage(load, ahead_ref, mid_ref):
    for pair in range(ahead_ref.shape[0] // 2):
        both = load(pair)
        halves = []
        for part in range(2):
            piece = both[:, part * SUB : (part + 1) * SUB, :]
            piece = piece.reshape(piece.shape[0] * SUB, piece.shape[2]).astype(bf16)
            mid = dot(ahead_ref[2 * pair + part], piece)
            halves.append(mid.reshape(-1, SUB, mid.shape[1]))
        mid_ref[:, pair * 2 * SUB : (pair + 1) * 2 * SUB, :] = jnp.concatenate(halves, axis=1).astype(bf16)


def last_stage(back_ref, wide_ref, pair):
    halves = []
    for step in (2 * pair, 2 * pair + 1):
        piece = wide_ref[:, step * SUB : (step + 1) * SUB, :]
        piece = piece.reshape(piece.shape[0] * SUB, piece.shape[2]).astype(bf16)
        out = dot(back_ref[step], piece)
        halves.append(out.reshape(-1, SUB, out.shape[1]))
    return jnp.concatenate(halves, axis=1)


def for_groups(count, work):
    @pl.loop(0, count // UNROLL)
    def _(turn):
        for step in range(UNROLL):
            work(turn * UNROLL + step)


def group_of(ref, group):
    both = ref[pl.ds(2 * group, 2)]
    return both.reshape(2 * both.shape[1], both.shape[2])


def taps_kernel(taps_ref, ahead_ref, second_ref, spectrum_ref, mid_ref):
    def load(pair):
        return taps_ref[:, pair * 2 * SUB : (pair + 1) * 2 * SUB, :].astype(jnp.float32)

    first_stage(load, ahead_ref, mid_ref)

    def work(group):
        spectrum_ref[group] = dot(second_ref[...], group_of(mid_ref, group))

    for_groups(spectrum_ref.shape[0], work)


def times(left, right, conjugate):
    half = left.shape[0] // 2
    left_real, left_imag = left[:half], left[half:]
    right_real, right_imag = right[:half], right[half:]
    if conjugate:
        real = left_real * right_real + left_imag * right_imag
        imag = left_imag * right_real - left_real * right_imag
    else:
        real = left_real * right_real - left_imag * right_imag
        imag = left_imag * right_real + left_real * right_imag
    return jnp.concatenate([real, imag], axis=0)


def main_kernel(
    both_ref, filter_ref, skip_ref, ahead_ref, back_ref, second_ref, undo_ref, out_ref, cross_ref, mid_ref, wide_ref
):
    tokens = both_ref.shape[1] // 2

    def load(pair):
        rows = slice(pair * 2 * SUB, (pair + 1) * 2 * SUB)
        more = slice(tokens + pair * 2 * SUB, tokens + (pair + 1) * 2 * SUB)
        return jnp.concatenate([both_ref[:, rows, :], both_ref[:, more, :]], axis=2).astype(jnp.float32)

    first_stage(load, ahead_ref, mid_ref)

    def work(group):
        spectrum = dot(second_ref[...], group_of(mid_ref, group))
        gated, grad = spectrum[:, :LANES], spectrum[:, LANES:]
        taps = filter_ref[group]
        conv = times(gated, taps, False)
        corr = times(grad, taps, True)
        cross_ref[group] = times(grad, gated, True).astype(bf16)
        undone = dot(undo_ref[...], jnp.concatenate([conv, corr], axis=1).astype(bf16))
        wide_ref[pl.ds(2 * group, 2)] = undone.reshape(2, -1, undone.shape[1])

    for_groups(filter_ref.shape[0], work)

    skip = skip_ref[...]
    for pair in range(back_ref.shape[0] // 2):
        sums = last_stage(back_ref, wide_ref, pair)
        for part in range(2):
            rows = slice(part * tokens + pair * 2 * SUB, part * tokens + (pair + 1) * 2 * SUB)
            direct = skip * both_ref[:, rows, :].astype(jnp.float32)
            out_ref[:, rows, :] = (sums[:, :, part * LANES : (part + 1) * LANES] + direct).astype(bf16)


def tap_grad_kernel(cross_ref, back_ref, undo_ref, out_ref, wide_ref):
    def work(group):
        undone = dot(undo_ref[...], cross_ref[group])
        wide_ref[pl.ds(2 * group, 2)] = undone.reshape(2, -1, undone.shape[1])

    for_groups(cross_ref.shape[0], work)
    for pair in range(back_ref.shape[0] // 2):
        out_ref[:, pair * 2 * SUB : (pair + 1) * 2 * SUB, :] = last_stage(back_ref, wide_ref, pair).astype(bf16)


def call(kernel, args, outs, scratch, limit, far=(), flops=0, moved=0):
    args = [
        pltpu.with_memory_space_constraint(arg, pltpu.HBM if place in far else VMEM) for place, arg in enumerate(args)
    ]
    in_specs = [pl.BlockSpec(memory_space=pl.ANY if place in far else VMEM) for place in range(len(args))]
    near = [isinstance(out, jax.ShapeDtypeStruct) for out in outs]
    return pl.pallas_call(
        kernel,
        out_shape=tuple(out if plain else VMEM(*out) for out, plain in zip(outs, near)),
        in_specs=in_specs,
        out_specs=tuple(pl.BlockSpec(memory_space=pl.ANY if plain else VMEM) for plain in near),
        scratch_shapes=scratch,
        cost_estimate=pl.CostEstimate(flops=flops, bytes_accessed=moved, transcendentals=0),
        compiler_params=pltpu.CompilerParams(vmem_limit_bytes=limit * MEGA),
    )(*args)


def local(query, key_stream, value_stream, upstream, bases, base_rows, long_filter, skip_weight):
    groups = lax.axis_size("seq")
    tokens, width = query.shape[1:]
    length = tokens * groups
    channels = long_filter.shape[0]
    ahead, back, second, undo = transform_tables(groups, tokens, length ** (-0.5))
    packed = ((groups, 2 * tokens, channels), bf16)
    array_bytes = tokens * width * 2

    (turned,) = call(turn_kernel, (long_filter,), [(long_filter.shape[::-1], bf16)], [], 4)
    all_taps = lax.all_gather(turned, "dp", axis=0, tiled=True)
    (gates,) = call(
        gate_kernel,
        (query, key_stream, value_stream, upstream, bases, base_rows),
        [packed],
        [VMEM((4, tokens, width), bf16), pltpu.SemaphoreType.DMA((4, PIECES))],
        12,
        far=(0, 1, 2, 3),
        moved=6 * array_bytes,
    )
    both = lax.all_to_all(gates, "seq", split_axis=0, concat_axis=0, tiled=True)

    one_pass = 2 * 4 * length * 256 * channels
    (spectrum,) = call(
        taps_kernel,
        (all_taps.reshape(groups, tokens, channels), ahead, second),
        [((groups, 2 * tokens, channels), jnp.float32)],
        [VMEM((2 * groups, tokens, channels), bf16)],
        8,
        flops=one_pass,
        moved=array_bytes,
    )
    out, cross = call(
        main_kernel,
        (both, spectrum, skip_weight.reshape(1, channels), ahead, back, second, undo),
        [packed, packed],
        [VMEM((2 * groups, tokens, 2 * channels), bf16), VMEM((2 * groups, tokens, 2 * channels), jnp.float32)],
        20,
        flops=4 * one_pass,
        moved=array_bytes,
    )
    home = lax.all_to_all(out, "seq", split_axis=0, concat_axis=0, tiled=True)

    (tap_grad,) = call(
        tap_grad_kernel,
        (cross, back, undo),
        [((groups, tokens, channels), bf16)],
        [VMEM((2 * groups, tokens, channels), jnp.float32)],
        10,
        flops=one_pass,
        moved=array_bytes,
    )
    summed = lax.psum_scatter(tap_grad.reshape(length, channels), "dp", scatter_dimension=0, tiled=True)
    (filter_grad,) = call(turn_kernel, (summed,), [(long_filter.shape, jnp.float32)], [], 4)

    grad_shape = jax.ShapeDtypeStruct(query.shape, bf16)
    query_grad, key_grad, value_grad = call(
        ungate_kernel,
        (home, key_stream, value_stream, upstream, bases, base_rows),
        [grad_shape, grad_shape, grad_shape],
        [VMEM((3, tokens, width), bf16), pltpu.SemaphoreType.DMA((3, PIECES))],
        12,
        moved=6 * array_bytes,
    )
    return (query_grad, key_grad, value_grad, filter_grad)


def solution(mesh):
    return jax.shard_map(
        local,
        mesh=mesh,
        in_specs=(
            P("dp", "seq", None),
            P("dp", "seq", None),
            P("dp", "seq", None),
            P("dp", "seq", None),
            P("dp", "seq"),
            P(),
            P("seq", "dp"),
            P("seq"),
        ),
        out_specs=(
            P("dp", "seq", None),
            P("dp", "seq", None),
            P("dp", "seq", None),
            P("seq", "dp"),
        ),
        check_vma=False,
    )
```

time: 219 us -> 195 us (0.89)
  Pallas kernels: 60.2 us -> 21 us
  local copies, waits for them, and re-layouts: 8.56 us -> 23.8 us
  other arithmetic: 2.3 us -> 0 us
    pallas_call x5 -> x7, Pallas kernels: 60.2 us -> 21 us  [call(): pl.pallas_call(kernel, out_shape=tuple((out if plain else VMEM(*out) for...]
    unnamed x6 -> x45, local copies, waits for them, and re-layouts: 2.65 us -> 23.8 us
    reshape x2 -> x0, local copies, waits for them, and re-layouts: 3.65 us -> none  [the longest x1 2.26 us: local(): tap_grad.reshape(length, channels)]
    convert_element_type x2 -> x0, other arithmetic: 2.3 us -> none  [the longest x1 1.63 us: local(): filter_grad = lax.psum_scatter(tap_grad.reshape(length, channels), 'dp',...]
    all_gather x1 -> x0, local copies, waits for them, and re-layouts: 2.26 us -> none  [local(): lax.all_gather(long_filter.T.astype(jnp.bfloat16), 'dp', axis=0, tiled=True)]
  transfers between devices with their start and end apart: 4 -> 4, of which waited for: 2 -> 2; matrix products, arithmetic and copies ran while one was open for 3% -> 0% of each run, Pallas kernels for 10% -> 4%
where the time goes in v2:
time: 195 us; the launch traced here: 194 us
  waiting for transfers between devices  115 us (59%)
  local copies, waits for them, and re-layouts  23.8 us (12%)
  Pallas kernels  21 us (11%)
  starting transfers between devices  20.4 us (10%)
  between operations  14.2 us (7%)
    reduce_scatter x1, waiting for transfers between devices, local(): lax.psum_scatter(tap_grad.reshape(length, channels), 'dp', scatter_dimens...  57.8 us
    all_gather x1, waiting for transfers between devices, local(): all_taps = lax.all_gather(turned, 'dp', axis=0, tiled=True)  56.9 us
    unnamed x45, local copies, waits for them, and re-layouts  23.8 us
    pallas_call x7, Pallas kernels, call(): pl.pallas_call(kernel, out_shape=tuple((out if plain else VMEM(*out) for...  21 us
    all_to_all x1, starting transfers between devices, local(): both = lax.all_to_all(gates, 'seq', split_axis=0, concat_axis=0, tiled=True)  11.8 us
    all_to_all x1, starting transfers between devices, local(): home = lax.all_to_all(out, 'seq', split_axis=0, concat_axis=0, tiled=True)  8.56 us
  transfers between devices with their start and end apart: 4, of which 2 were waited for; matrix products, arithmetic and copies ran while one was open for 0% of the time, Pallas kernels for 4%

profile of v2, /device:TPU:2, one launch (start us, length us, event | category | flops | bytes accessed | tf_op | source)
XLA Modules:
  0.0 194.1 jit_solution(13613000298886349677)
XLA Ops:
  7.2 0.7 copy-done.16
  8.6 4.0 %shard_map.147 = bf16[32,256,128]{2,1,0:T(8,128)(2,1)} custom-call(bf16[1,128,4096]{2,1,0:T(8,128)(2,1)} %query.1, bf16[1,128,4096]{2,1,0:T(8,128)(2,1)} %key_ref.1, bf16[1,128,4096]{2,1,0:T(8,128)(2,1)} %value_ref.1, bf16[1,128,4096]{2,1,0:T(8,128)(2,1)} %upstream_ref.1, s32[1,128]{1,0:T(1,128)S(1)} %copy-done.19, bf16[4,4096]{1,0:T(4,128)(2,1)S(1)} %copy-done.16), custom_call_target="tpu_custom_call" | custom-call | bytes 6291456 | tf_op jit(solution)/shard_map/pallas_call | solution.py:227
  12.7 11.8 %all-to-all-start = ((bf16[32,256,128]{2,1,0:T(8,128)(2,1)}), bf16[32,256,128]{2,1,0:T(8,128)(2,1)S(1)}, u32[]{:S(2)}, u32[]{:S(2)}) async-start(bf16[32,256,128]{2,1,0:T(8,128)(2,1)} %shard_map.147), calls=%async_computation | async-start | bytes 4194304 | tf_op jit(solution)/shard_map/all_to_all | solution.py:258
  24.5 0.8 shard_map.148
  25.3 56.9 %all-gather.2.cloned.1.call-done = bf16[4096,128]{1,0:T(8,128)(2,1)} async-done(((bf16[512,128]{1,0:T(8,128)(2,1)}), bf16[4096,128]{1,0:T(8,128)(2,1)}) %all-gather.2.cloned.1.call-update) | async-done | bytes 1048592 | tf_op jit(solution)/shard_map/all_gather | solution.py:248
  82.1 2.2 %copy-done.2 = bf16[16,512,256]{2,1,0:T(8,128)(2,1)S(1)} copy-done((bf16[16,512,256]{2,1,0:T(8,128)(2,1)S(1)}, bf16[16,512,256]{2,1,0:T(8,128)(2,1)}, u32[]{:S(2)}) %copy-start.2) | copy-done | bytes 4194328
  84.3 1.2 copy-done.12
  85.5 3.0 %shard_map.149.filter_ref = f32[32,256,128]{2,1,0:T(8,128)S(1)} custom-call(bf16[32,128,128]{2,1,0:T(8,128)(2,1)S(1)} %bitcast.3, bf16[16,512,256]{2,1,0:T(8,128)(2,1)S(1)} %copy-done.2, bf16[256,256]{1,0:T(8,128)(2,1)S(1)} %copy-done.15), custom_call_target="tpu_custom_call" | custom-call | flops 1073741824 | bytes 1048576 | tf_op jit(solution)/shard_map/pallas_call | solution.py:227
  88.5 2.0 %copy-done.4 = f32[32,256,128]{2,1,0:T(8,128)} copy-done((f32[32,256,128]{2,1,0:T(8,128)}, f32[32,256,128]{2,1,0:T(8,128)S(1)}, u32[]{:S(2)}) %copy-start.4) | copy-done | bytes 4194328
  90.5 2.2 %copy-done = bf16[16,256,512]{2,1,0:T(8,128)(2,1)S(1)} copy-done((bf16[16,256,512]{2,1,0:T(8,128)(2,1)S(1)}, bf16[16,256,512]{2,1,0:T(8,128)(2,1)}, u32[]{:S(2)}) %copy-start) | copy-done | bytes 4194328
  92.7 2.2 %copy-done.3 = bf16[16,512,256]{2,1,0:T(8,128)(2,1)S(1)} copy-done((bf16[16,512,256]{2,1,0:T(8,128)(2,1)S(1)}, bf16[16,512,256]{2,1,0:T(8,128)(2,1)}, u32[]{:S(2)}) %copy-start.3) | copy-done | bytes 4194328
  94.9 2.2 %copy-done.5 = f32[32,256,128]{2,1,0:T(8,128)S(1)} copy-done((f32[32,256,128]{2,1,0:T(8,128)S(1)}, f32[32,256,128]{2,1,0:T(8,128)}, u32[]{:S(2)}) %copy-start.5) | copy-done | bytes 4194328
  97.1 6.5 %shard_map.150 = (bf16[32,256,128]{2,1,0:T(8,128)(2,1)S(1)}, bf16[32,256,128]{2,1,0:T(8,128)(2,1)S(1)}) custom-call(bf16[32,256,128]{2,1,0:T(8,128)(2,1)S(1)} %all-to-all-done.both_ref, f32[32,256,128]{2,1,0:T(8,128)S(1)} %copy-done.5, f32[1,128]{1,0:T(1,128)S(1)} %bitcast.4, bf16[16,512,256]{2,1,0:T(8,128)(2,1)S(1)} %copy-done.3, ...), custom_call_target="tpu_custom_call" | custom-call | flops 4294967296 | bytes 1048576 | tf_op jit(solution)/shard_map/pallas_call | solution.py:227
  103.6 1.3 copy-done.9
  104.9 1.3 copy-done.11
  106.2 8.6 %all-to-all-start.1 = ((bf16[32,256,128]{2,1,0:T(8,128)(2,1)}), bf16[32,256,128]{2,1,0:T(8,128)(2,1)S(1)}, u32[]{:S(2)}, u32[]{:S(2)}) async-start(bf16[32,256,128]{2,1,0:T(8,128)(2,1)} %copy-done.11), calls=%async_computation.1 | async-start | bytes 4194304 | tf_op jit(solution)/shard_map/all_to_all | solution.py:279
  114.8 2.2 %copy-done.1 = bf16[16,256,512]{2,1,0:T(8,128)(2,1)S(1)} copy-done((bf16[16,256,512]{2,1,0:T(8,128)(2,1)S(1)}, bf16[16,256,512]{2,1,0:T(8,128)(2,1)}, u32[]{:S(2)}) %copy-start.1) | copy-done | bytes 4194328
  117.0 1.6 copy-done.10
  118.6 4.0 %shard_map.152 = bf16[32,128,128]{2,1,0:T(8,128)(2,1)} custom-call(bf16[32,256,128]{2,1,0:T(8,128)(2,1)S(1)} %copy-done.10, bf16[16,256,512]{2,1,0:T(8,128)(2,1)S(1)} %copy-done.1, bf16[256,256]{1,0:T(8,128)(2,1)S(1)} %copy-done.14), custom_call_target="tpu_custom_call" | custom-call | flops 1073741824 | bytes 1048576 | tf_op jit(solution)/shard_map/pallas_call | solution.py:227
  122.6 57.8 %reduce-scatter.2.cloned.1.call-done.in_ref = bf16[512,128]{1,0:T(8,128)(2,1)} async-done(((bf16[4096,128]{1,0:T(8,128)(2,1)}), bf16[512,128]{1,0:T(8,128)(2,1)}) %reduce-scatter.2.cloned.1.call-update) | async-done | bytes 131088 | tf_op jit(solution)/shard_map/reduce_scatter | solution.py:290
  180.4 0.9 copy-done.18
  182.2 1.2 copy-done.7
  183.4 1.2 copy-done.8
  184.6 2.7 %shard_map.151 = (bf16[1,128,4096]{2,1,0:T(8,128)(2,1)}, bf16[1,128,4096]{2,1,0:T(8,128)(2,1)}, bf16[1,128,4096]{2,1,0:T(8,128)(2,1)}) custom-call(bf16[32,256,128]{2,1,0:T(8,128)(2,1)S(1)} %all-to-all-done.1.back_ref, bf16[1,128,4096]{2,1,0:T(8,128)(2,1)S(1)} %copy-done.6, bf16[1,128,4096]{2,1,0:T(8,128)(2,1)S(1)} %copy-done.7, ...), custom_call_target="tpu_custom_call" | custom-call | bytes 6291456 | tf_op jit(solution)/shard_map/pallas_call | solution.py:227
  (38 shorter events, 1.6 us)
Async XLA Ops:
  12.6 11.8 %copy-start.13 = (f32[128,512]{1,0:T(8,128)S(1)}, f32[128,512]{1,0:T(8,128)}, u32[]{:S(2)}) copy-start(f32[128,512]{1,0:T(8,128)} %in_ref.1) | copy-start | bytes 786436
  12.6 69.5 %copy-start.15 = (bf16[256,256]{1,0:T(8,128)(2,1)S(1)}, bf16[256,256]{1,0:T(8,128)(2,1)}, u32[]{:S(2)}) copy-start(bf16[256,256]{1,0:T(8,128)(2,1)} %constant.9.clone.second_ref) | copy-start | bytes 393220
  12.7 77.8 %all-to-all-start = ((bf16[32,256,128]{2,1,0:T(8,128)(2,1)}), bf16[32,256,128]{2,1,0:T(8,128)(2,1)S(1)}, u32[]{:S(2)}, u32[]{:S(2)}) async-start(bf16[32,256,128]{2,1,0:T(8,128)(2,1)} %shard_map.147), calls=%async_computation | async-start | bytes 4194304 | tf_op jit(solution)/shard_map/all_to_all | solution.py:258
  24.4 57.7 %all-gather.2.cloned.1.call-start = ((), (), s32[]{:S(2)}) async-start(), calls=%async_computation.3 | async-start | bytes 1179648 | tf_op jit(solution)/shard_map/all_gather | solution.py:248
  82.1 2.2 %copy-start.2 = (bf16[16,512,256]{2,1,0:T(8,128)(2,1)S(1)}, bf16[16,512,256]{2,1,0:T(8,128)(2,1)}, u32[]{:S(2)}) copy-start(bf16[16,512,256]{2,1,0:T(8,128)(2,1)} %constant.8.clone.ahead_ref) | copy-start | bytes 12582916
  84.3 1.2 copy-start.12
  85.5 4.9 %copy-start.14 = (bf16[256,256]{1,0:T(8,128)(2,1)S(1)}, bf16[256,256]{1,0:T(8,128)(2,1)}, u32[]{:S(2)}) copy-start(bf16[256,256]{1,0:T(8,128)(2,1)} %constant.11.clone.undo_ref) | copy-start | bytes 393220
  85.5 4.9 %copy-start.21 = (f32[128]{0:T(128)S(1)}, f32[128]{0:T(128)}, u32[]{:S(2)}) copy-start(f32[128]{0:T(128)} %param.19) | copy-start | bytes 1540
  88.5 2.0 %copy-start.4 = (f32[32,256,128]{2,1,0:T(8,128)}, f32[32,256,128]{2,1,0:T(8,128)S(1)}, u32[]{:S(2)}) copy-start(f32[32,256,128]{2,1,0:T(8,128)S(1)} %shard_map.149.filter_ref) | copy-start | bytes 12582916
  90.5 2.2 %copy-start = (bf16[16,256,512]{2,1,0:T(8,128)(2,1)S(1)}, bf16[16,256,512]{2,1,0:T(8,128)(2,1)}, u32[]{:S(2)}) copy-start(bf16[16,256,512]{2,1,0:T(8,128)(2,1)} %constant.10.clone.back_ref) | copy-start | bytes 12582916
  92.7 2.2 %copy-start.3 = (bf16[16,512,256]{2,1,0:T(8,128)(2,1)S(1)}, bf16[16,512,256]{2,1,0:T(8,128)(2,1)}, u32[]{:S(2)}) copy-start(bf16[16,512,256]{2,1,0:T(8,128)(2,1)} %constant.8.clone.ahead_ref) | copy-start | bytes 12582916
  94.9 2.2 %copy-start.5 = (f32[32,256,128]{2,1,0:T(8,128)S(1)}, f32[32,256,128]{2,1,0:T(8,128)}, u32[]{:S(2)}) copy-start(f32[32,256,128]{2,1,0:T(8,128)} %copy-done.4) | copy-start | bytes 12582916
  103.6 1.3 copy-start.9
  104.9 1.3 copy-start.11
  106.2 75.9 %all-to-all-start.1 = ((bf16[32,256,128]{2,1,0:T(8,128)(2,1)}), bf16[32,256,128]{2,1,0:T(8,128)(2,1)S(1)}, u32[]{:S(2)}, u32[]{:S(2)}) async-start(bf16[32,256,128]{2,1,0:T(8,128)(2,1)} %copy-done.11), calls=%async_computation.1 | async-start | bytes 4194304 | tf_op jit(solution)/shard_map/all_to_all | solution.py:279
  114.8 65.6 %reduce-scatter.2.cloned.1.call-start = ((), (), s32[]{:S(2)}) async-start(), calls=%async_computation.4 | async-start | bytes 1179648 | tf_op jit(solution)/shard_map/reduce_scatter | solution.py:290
  114.8 2.2 %copy-start.1 = (bf16[16,256,512]{2,1,0:T(8,128)(2,1)S(1)}, bf16[16,256,512]{2,1,0:T(8,128)(2,1)}, u32[]{:S(2)}) copy-start(bf16[16,256,512]{2,1,0:T(8,128)(2,1)} %constant.10.clone.back_ref) | copy-start | bytes 12582916
  117.0 1.6 copy-start.10
  118.6 63.5 %copy-start.17 = (bf16[4,4096]{1,0:T(4,128)(2,1)S(1)}, bf16[4,4096]{1,0:T(4,128)(2,1)}, u32[]{:S(2)}) copy-start(bf16[4,4096]{1,0:T(4,128)(2,1)} %rows_ref.3) | copy-start | bytes 98308
  118.6 63.5 %copy-start.20 = (s32[1,128]{1,0:T(1,128)S(1)}, s32[1,128]{1,0:T(1,128)}, u32[]{:S(2)}) copy-start(s32[1,128]{1,0:T(1,128)} %bases_ref.3) | copy-start | bytes 1540
  122.6 59.6 %copy-start.6 = (bf16[1,128,4096]{2,1,0:T(8,128)(2,1)S(1)}, bf16[1,128,4096]{2,1,0:T(8,128)(2,1)}, u32[]{:S(2)}) copy-start(bf16[1,128,4096]{2,1,0:T(8,128)(2,1)} %key_ref.1) | copy-start | bytes 3145732
  180.4 0.9 copy-start.18
  182.1 1.2 copy-start.7
  183.4 1.2 copy-start.8
  (2 other events, 1.4 us)
Sparse Core Ops, SparseCore 0:
  27.6 54.4 all-gather.1
  122.7 57.6 reduce-scatter.1

commit v3 on v2

v3 whole, which is shorter than its diff:
```python
import math

import jax
import jax.numpy as jnp
import ml_dtypes
import numpy as np
from jax import lax
from jax.experimental import pallas as pl
from jax.experimental.pallas import tpu as pltpu
from jax.sharding import PartitionSpec as P

LANES = 128
SUB = 8
PIECES = 8
UNROLL = 8
TABLE_PIECES = 4
Z_PAIRS = 2
Y_PLACES = 4
TAP_BLOCKS = 4
MEGA = 1024 * 1024
VMEM = pltpu.VMEM
bf16 = jnp.bfloat16


def transform_tables(blocks, rows, scale):
    points = 2 * blocks * rows
    low = 2 * np.arange(blocks)[:, None, None] + 1
    point = np.arange(blocks)[None, None, :] * rows + np.arange(rows)[None, :, None]
    angle = math.pi / points * (low * point % (2 * points))
    first = np.stack([np.cos(angle), -np.sin(angle)], axis=1)
    first = first.reshape(2 * blocks, rows // SUB, SUB, blocks)
    ahead = np.einsum("mhaj,ab->hmajb", first, np.eye(SUB))
    ahead = ahead.reshape(rows // SUB, 2 * blocks * SUB, blocks * SUB)
    back = np.ascontiguousarray(np.swapaxes(ahead, 1, 2))

    row = np.arange(rows)
    angle = 2.0 * math.pi / rows * (row[:, None] * row[None, :] % rows)
    cosine, sine = np.cos(angle), np.sin(angle)
    second = np.block([[cosine, sine], [-sine, cosine]])
    undo = np.ascontiguousarray(second.T) * (2.0 / points * scale)
    return tuple(table.astype(ml_dtypes.bfloat16) for table in (ahead, back, second, undo))


def dot(left, right):
    return jnp.dot(left, right, preferred_element_type=jnp.float32)


def letters_of(bases_ref):
    count = bases_ref.shape[1]
    return jnp.transpose(jnp.broadcast_to(bases_ref[...], (count, count)))


def readout(letters, rows_ref, columns):
    rows = rows_ref[:, columns].astype(jnp.float32)
    picked = rows[0:1]
    for letter in range(1, rows.shape[0]):
        picked = jnp.where(letters == letter, rows[letter : letter + 1], picked)
    return picked


def gate_kernel(query, key, value, upstream, bases_ref, rows_ref, out_ref, held, sems):
    tokens, width = query.shape[1:]
    span = width // PIECES
    copies = []
    for piece in range(PIECES):
        columns = pl.ds(piece * span, span)
        row = []
        for which, source in enumerate((query, key, value, upstream)):
            copy = pltpu.make_async_copy(
                source.at[0, :, columns], held.at[which, :, columns], sems.at[which, piece]
            )
            copy.start()
            row.append(copy)
        copies.append(row)
    letters = letters_of(bases_ref)
    for piece in range(PIECES):
        for copy in copies[piece]:
            copy.wait()
        for block in range(piece * span // LANES, (piece + 1) * span // LANES):
            columns = slice(block * LANES, (block + 1) * LANES)
            query_rows, key_rows, value_rows, upstream_rows = (
                held[which, :, columns].astype(jnp.float32) for which in range(4)
            )
            out_grad = upstream_rows - readout(letters, rows_ref, columns)
            out_ref[block, :tokens, :] = (key_rows * value_rows).astype(bf16)
            out_ref[block, tokens:, :] = (out_grad * query_rows).astype(bf16)


def ungate_kernel(back_ref, key, value, upstream, bases_ref, rows_ref, *rest):
    outs, (held, in_sems, made, out_sems) = rest[:3], rest[3:]
    tokens, width = key.shape[1:]
    span = width // PIECES
    arriving = []
    for piece in range(PIECES):
        columns = pl.ds(piece * span, span)
        row = []
        for which, source in enumerate((key, value, upstream)):
            copy = pltpu.make_async_copy(
                source.at[0, :, columns], held.at[which, :, columns], in_sems.at[which, piece]
            )
            copy.start()
            row.append(copy)
        arriving.append(row)
    letters = letters_of(bases_ref)
    leaving = []
    for piece in range(PIECES):
        for copy in arriving[piece]:
            copy.wait()
        for block in range(piece * span // LANES, (piece + 1) * span // LANES):
            columns = slice(block * LANES, (block + 1) * LANES)
            conv = back_ref[block, :tokens, :].astype(jnp.float32)
            corr = back_ref[block, tokens:, :].astype(jnp.float32)
            key_rows, value_rows, upstream_rows = (held[which, :, columns].astype(jnp.float32) for which in range(3))
            out_grad = upstream_rows - readout(letters, rows_ref, columns)
            made[0, :, columns] = (out_grad * conv).astype(bf16)
            made[1, :, columns] = (corr * value_rows).astype(bf16)
            made[2, :, columns] = (corr * key_rows).astype(bf16)
        columns = pl.ds(piece * span, span)
        for which, target in enumerate(outs):
            copy = pltpu.make_async_copy(
                made.at[which, :, columns], target.at[0, :, columns], out_sems.at[which, piece]
            )
            copy.start()
            leaving.append(copy)
    for copy in leaving:
        copy.wait()


def turn_kernel(in_ref, out_ref):
    blocks, rows, channels = out_ref.shape
    for block in range(blocks):
        out_ref[block] = jnp.transpose(in_ref[:, block * rows : (block + 1) * rows]).astype(bf16)


def first_stage(load, table, mid_ref):
    for pair in range(mid_ref.shape[1] // (2 * SUB)):
        both = load(pair)
        halves = []
        for part in range(2):
            piece = both[:, part * SUB : (part + 1) * SUB, :]
            piece = piece.reshape(piece.shape[0] * SUB, piece.shape[2]).astype(bf16)
            mid = dot(table(2 * pair + part), piece)
            halves.append(mid.reshape(-1, SUB, mid.shape[1]))
        mid_ref[:, pair * 2 * SUB : (pair + 1) * 2 * SUB, :] = jnp.concatenate(halves, axis=1).astype(bf16)


def last_stage(table, wide_ref, pair):
    halves = []
    for step in (2 * pair, 2 * pair + 1):
        piece = wide_ref[:, step * SUB : (step + 1) * SUB, :]
        piece = piece.reshape(piece.shape[0] * SUB, piece.shape[2]).astype(bf16)
        out = dot(table(step), piece)
        halves.append(out.reshape(-1, SUB, out.shape[1]))
    return jnp.concatenate(halves, axis=1)


def for_groups(count, work):
    @pl.loop(0, count // UNROLL)
    def _(turn):
        for step in range(UNROLL):
            work(turn * UNROLL + step)


def group_of(ref, group):
    both = ref[pl.ds(2 * group, 2)]
    return both.reshape(2 * both.shape[1], both.shape[2])


def times(left, right, conjugate):
    half = left.shape[0] // 2
    left_real, left_imag = left[:half], left[half:]
    right_real, right_imag = right[:half], right[half:]
    if conjugate:
        real = left_real * right_real + left_imag * right_imag
        imag = left_imag * right_real - left_real * right_imag
    else:
        real = left_real * right_real - left_imag * right_imag
        imag = left_imag * right_real + left_real * right_imag
    return jnp.concatenate([real, imag], axis=0)


def place():
    index = lax.axis_index("dp")
    return index // Y_PLACES, lax.rem(index, Y_PLACES)


def block_of(pair, turn):
    pair_here, place_here = place()
    owner = lax.rem(pair_here + pair, Z_PAIRS) * Y_PLACES + lax.rem(place_here + turn + Y_PLACES, Y_PLACES)
    return pl.ds(owner * TAP_BLOCKS, TAP_BLOCKS)


def middle_kernel(both_ref, *refs):
    taps_hbm, refs = refs[:Y_PLACES], refs[Y_PLACES:]
    (skip_ref, ahead_hbm, back_hbm, second_ref, undo_ref, out_ref), refs = refs[:6], refs[6:]
    tap_outs, refs = refs[:Y_PLACES], refs[Y_PLACES:]
    taps_ref, ahead_ref, back_ref, tap_mid_ref, mid_ref, spectrum_ref, cross_ref, wide_ref = refs[:8]
    taps_sems, ahead_sems, back_sems, out_sems = refs[8:]
    groups = both_ref.shape[0]
    tokens = both_ref.shape[1] // 2
    steps = ahead_ref.shape[0]
    pairs = steps // 2

    def chunk(pair):
        return slice(pair * 2 * SUB, (pair + 1) * 2 * SUB)

    tap_copies = []
    for turn in range(Y_PLACES):
        for pair in range(Z_PAIRS):
            target = taps_ref.at[block_of(pair, -turn)]
            tap_copies.append(pltpu.make_async_copy(taps_hbm[turn].at[pair], target, taps_sems.at[turn, pair]))
            tap_copies[-1].start()
    span = steps // TABLE_PIECES
    ahead_copies = []
    back_copies = []
    for source, target, sems, copies in (
        (ahead_hbm, ahead_ref, ahead_sems, ahead_copies),
        (back_hbm, back_ref, back_sems, back_copies),
    ):
        for piece in range(TABLE_PIECES):
            rows = pl.ds(piece * span, span)
            copies.append(pltpu.make_async_copy(source.at[rows], target.at[rows], sems.at[piece]))
            copies[-1].start()

    for copy in tap_copies:
        copy.wait()

    def load_taps(pair):
        return taps_ref[:, chunk(pair), :].astype(jnp.float32)

    def fresh_ahead(step):
        if step % span == 0:
            ahead_copies[step // span].wait()
        return ahead_ref[step]

    first_stage(load_taps, fresh_ahead, tap_mid_ref)

    def transform_taps(group):
        spectrum_ref[group] = dot(second_ref[...], group_of(tap_mid_ref, group))

    for_groups(groups, transform_taps)

    def load_both(pair):
        rows = chunk(pair)
        more = slice(tokens + rows.start, tokens + rows.stop)
        return jnp.concatenate([both_ref[:, rows, :], both_ref[:, more, :]], axis=2).astype(jnp.float32)

    first_stage(load_both, lambda step: ahead_ref[step], mid_ref)

    def work(group):
        spectrum = dot(second_ref[...], group_of(mid_ref, group))
        gated, grad = spectrum[:, :LANES], spectrum[:, LANES:]
        taps = spectrum_ref[group]
        conv = times(gated, taps, False)
        corr = times(grad, taps, True)
        cross_ref[group] = times(grad, gated, True).astype(bf16)
        undone = dot(undo_ref[...], jnp.concatenate([conv, corr], axis=1).astype(bf16))
        wide_ref[pl.ds(2 * group, 2)] = undone.reshape(2, -1, undone.shape[1])

    for_groups(groups, work)

    for copy in back_copies:
        copy.wait()

    def back_table(step):
        return back_ref[step]

    skip = skip_ref[...]
    for pair in range(pairs):
        sums = last_stage(back_table, wide_ref, pair)
        for part in range(2):
            rows = slice(part * tokens + pair * 2 * SUB, part * tokens + (pair + 1) * 2 * SUB)
            direct = skip * both_ref[:, rows, :].astype(jnp.float32)
            out_ref[:, rows, :] = (sums[:, :, part * LANES : (part + 1) * LANES] + direct).astype(bf16)

    def undo_cross(group):
        undone = dot(undo_ref[...], cross_ref[group])
        spectrum_wide[pl.ds(2 * group, 2)] = undone.reshape(2, -1, undone.shape[1])

    spectrum_wide = wide_ref.at[:, :, :LANES]
    for_groups(groups, undo_cross)
    for pair in range(pairs):
        taps_ref[:, chunk(pair), :] = last_stage(back_table, spectrum_wide, pair).astype(bf16)

    leaving = []
    for turn in range(Y_PLACES):
        for pair in range(Z_PAIRS):
            source = taps_ref.at[block_of(pair, turn)]
            leaving.append(pltpu.make_async_copy(source, tap_outs[turn].at[pair], out_sems.at[turn, pair]))
            leaving[-1].start()
    for copy in leaving:
        copy.wait()


def join_kernel(*refs):
    parts, (kept_ref, sent_ref) = refs[:-2], refs[-2:]
    total = parts[0][...].astype(jnp.float32)
    for part in parts[1:]:
        total = total + part[...].astype(jnp.float32)
    kept_ref[...] = total[0]
    sent_ref[...] = total[1].astype(bf16)


def finish_kernel(kept_ref, came_ref, out_ref):
    blocks, rows, channels = kept_ref.shape
    for block in range(blocks):
        total = kept_ref[block] + came_ref[block].astype(jnp.float32)
        out_ref[:, block * rows : (block + 1) * rows] = jnp.transpose(total)


def call(kernel, args, outs, scratch, limit, flops=0, moved=0):
    in_specs = []
    held = []
    for arg, space in args:
        held.append(arg if space in (None, pl.ANY) else pltpu.with_memory_space_constraint(arg, space))
        in_specs.append(pl.BlockSpec(memory_space=pl.ANY if space in (pl.ANY, pltpu.HBM) else VMEM))
    out_shape = []
    out_specs = []
    for shape, dtype, space in outs:
        out_shape.append(jax.ShapeDtypeStruct(shape, dtype) if space is None else space(shape, dtype))
        out_specs.append(pl.BlockSpec(memory_space=pl.ANY if space is pltpu.HBM else VMEM))
    return pl.pallas_call(
        kernel,
        out_shape=tuple(out_shape),
        in_specs=in_specs,
        out_specs=tuple(out_specs),
        scratch_shapes=scratch,
        cost_estimate=pl.CostEstimate(flops=flops, bytes_accessed=moved, transcendentals=0),
        compiler_params=pltpu.CompilerParams(vmem_limit_bytes=limit * MEGA),
    )(*held)


def along_dp(array, pairs, places):
    sources = [(pair, place) for pair in range(Z_PAIRS) for place in range(Y_PLACES)]
    moves = [
        (pair * Y_PLACES + place, (pair + pairs) % Z_PAIRS * Y_PLACES + (place + places) % Y_PLACES)
        for pair, place in sources
    ]
    return lax.ppermute(array, "dp", moves)


def exchange(array):
    always = lax.optimization_barrier(jnp.int32(1)) == 1
    return lax.cond(
        always,
        lambda whole: lax.all_to_all(whole, "seq", split_axis=0, concat_axis=0, tiled=True),
        lambda whole: whole,
        array,
    )


def local(query, key_stream, value_stream, upstream, bases, base_rows, long_filter, skip_weight):
    groups = lax.axis_size("seq")
    tokens, width = query.shape[1:]
    length = tokens * groups
    channels = long_filter.shape[0]
    ahead, back, second, undo = (jnp.asarray(table) for table in transform_tables(groups, tokens, length ** (-0.5)))
    array_bytes = tokens * width * 2
    far, free, dma = pltpu.HBM, None, pltpu.SemaphoreType.DMA
    steps = ahead.shape[0]
    packed = ((groups, 2 * tokens, channels), bf16, VMEM)
    tap_block = (TAP_BLOCKS, tokens, channels)
    tap_pair = ((Z_PAIRS,) + tap_block, bf16, far)

    (turned,) = call(turn_kernel, [(long_filter, free)], [(tap_block, bf16, free)], [], 4)
    other = along_dp(turned, 1, 0)
    (gates,) = call(
        gate_kernel,
        [(query, far), (key_stream, far), (value_stream, far), (upstream, far), (bases, free), (base_rows, free)],
        [packed],
        [VMEM((4, tokens, width), bf16), dma((4, PIECES))],
        12,
        moved=6 * array_bytes,
    )
    gates, own_taps = lax.optimization_barrier((gates, jnp.stack([turned, other])))
    taps = [own_taps] + [along_dp(own_taps, 0, turn) for turn in range(1, Y_PLACES)]
    both = exchange(gates)

    half_mid = (2 * groups, tokens, channels)
    wide_mid = (2 * groups, tokens, 2 * channels)
    spectra = (groups, 2 * tokens, channels)
    out, *tap_grads = call(
        middle_kernel,
        [(both, VMEM)]
        + [(part, pl.ANY) for part in taps]
        + [
            (skip_weight.reshape(1, channels), free),
            (ahead, far),
            (back, far),
            (second, free),
            (undo, free),
        ],
        [packed] + [tap_pair] * Y_PLACES,
        [
            VMEM((groups, tokens, channels), bf16),
            VMEM(ahead.shape, bf16),
            VMEM(back.shape, bf16),
            VMEM(half_mid, bf16),
            VMEM(wide_mid, bf16),
            VMEM(spectra, jnp.float32),
            VMEM(spectra, bf16),
            VMEM(wide_mid, jnp.float32),
            dma((Y_PLACES, Z_PAIRS)),
            dma((TABLE_PIECES,)),
            dma((TABLE_PIECES,)),
            dma((Y_PLACES, Z_PAIRS)),
        ],
        40,
        flops=2 * 24 * length * 256 * channels,
        moved=12 * array_bytes,
    )
    came = [along_dp(tap_grads[turn], 0, turn) for turn in range(1, Y_PLACES)]
    home, *came = lax.optimization_barrier((exchange(out), *came))

    kept, sent = call(
        join_kernel,
        [(part, free) for part in [tap_grads[0]] + came],
        [(tap_block, jnp.float32, free), (tap_block, bf16, free)],
        [],
        8,
    )
    last = along_dp(sent, 1, 0)
    grad = (query.shape, bf16, far)
    query_grad, key_grad, value_grad = call(
        ungate_kernel,
        [(home, VMEM), (key_stream, far), (value_stream, far), (upstream, far), (bases, free), (base_rows, free)],
        [grad, grad, grad],
        [
            VMEM((3, tokens, width), bf16),
            dma((3, PIECES)),
            VMEM((3, tokens, width), bf16),
            dma((3, PIECES)),
        ],
        16,
        moved=6 * array_bytes,
    )
    (filter_grad,) = call(finish_kernel, [(kept, free), (last, free)], [(long_filter.shape, jnp.float32, free)], [], 8)
    return (query_grad, key_grad, value_grad, filter_grad)


def solution(mesh):
    return jax.shard_map(
        local,
        mesh=mesh,
        in_specs=(
            P("dp", "seq", None),
            P("dp", "seq", None),
            P("dp", "seq", None),
            P("dp", "seq", None),
            P("dp", "seq"),
            P(),
            P("seq", "dp"),
            P("seq"),
        ),
        out_specs=(
            P("dp", "seq", None),
            P("dp", "seq", None),
            P("dp", "seq", None),
            P("seq", "dp"),
        ),
        check_vma=False,
    )
```

time: 195 us -> 164 us (0.84)
  blocking collectives: 0 us -> 117 us
  waiting for transfers between devices: 115 us -> 0.9 us
  local copies, waits for them, and re-layouts: 23.8 us -> 7.06 us
  between operations: 14.2 us -> 0.79 us
  starting transfers between devices: 20.4 us -> 11.4 us
  Pallas kernels: 21 us -> 25 us
    all_to_all x0 -> x2, blocking collectives: none -> 117 us  [exchange(): lax.all_to_all(whole, 'seq', split_axis=0, concat_axis=0, tiled=True)]
    reduce_scatter x1 -> x0, waiting for transfers between devices: 57.8 us -> none  [local(): lax.psum_scatter(tap_grad.reshape(length, channels), 'dp', scatter_dimens...]
    all_gather x1 -> x0, waiting for transfers between devices: 56.9 us -> none  [local(): all_taps = lax.all_gather(turned, 'dp', axis=0, tiled=True)]
    all_to_all x2 -> x0, starting transfers between devices: 20.3 us -> none  [the longest x1 11.8 us: local(): both = lax.all_to_all(gates, 'seq', split_axis=0, concat_axis=0, tiled=True)]
    unnamed x45 -> x22, local copies, waits for them, and re-layouts: 23.8 us -> 5.29 us
    ppermute x0 -> x8, starting transfers between devices: none -> 11.4 us  [along_dp(): return lax.ppermute(array, 'dp', moves)]
    pallas_call x7 -> x6, Pallas kernels: 21 us -> 25 us  [call(): pl.pallas_call(kernel, out_shape=tuple(out_shape), in_specs=in_specs, out...]
  transfers between devices with their start and end apart: 4 -> 8, of which waited for: 2 -> 1; matrix products, arithmetic and copies ran while one was open for 0% -> 0% of each run, Pallas kernels for 4% -> 4%
where the time goes in v3:
time: 164 us; the launch traced here: 162 us
  blocking collectives  117 us (71%)
  Pallas kernels  25 us (15%)
  starting transfers between devices  11.4 us (7%)
  local copies, waits for them, and re-layouts  7.06 us (4%)
    all_to_all x2, blocking collectives, exchange(): lax.all_to_all(whole, 'seq', split_axis=0, concat_axis=0, tiled=True)  117 us
    pallas_call x6, Pallas kernels, call(): pl.pallas_call(kernel, out_shape=tuple(out_shape), in_specs=in_specs, out...  25 us
    ppermute x8, starting transfers between devices, along_dp(): return lax.ppermute(array, 'dp', moves)  11.4 us
    unnamed x22, local copies, waits for them, and re-layouts  5.29 us
  transfers between devices with their start and end apart: 8, of which 1 were waited for; matrix products, arithmetic and copies ran while one was open for 0% of the time, Pallas kernels for 4%

profile of v3, /device:TPU:2, one launch (start us, length us, event | category | flops | bytes accessed | tf_op | source)
XLA Modules:
  0.0 162.2 jit_solution(3304727399964256685)
XLA Ops:
  0.6 0.9 copy-done.3
  1.7 2.0 %collective-permute-start = (bf16[4,128,128]{2,1,0:T(8,128)(2,1)S(1)}, bf16[4,128,128]{2,1,0:T(8,128)(2,1)S(1)}, u32[]{:S(2)}, u32[]{:S(2)}) collective-permute-start(bf16[4,128,128]{2,1,0:T(8,128)(2,1)S(1)} %shard_map.148), channel_id=1, source_target_pairs={{0,128},{32,160},{64,192},{96,224},{128,0},{160,32},{192,64},{224,... | collective-permute-start | bytes 393224 | tf_op jit(solution)/shard_map/ppermute | solution.py:339
  3.7 0.8 copy-done.5
  4.5 0.7 copy-done.7
  5.1 2.7 %shard_map.147 = bf16[32,256,128]{2,1,0:T(8,128)(2,1)S(1)} custom-call(bf16[1,128,4096]{2,1,0:T(8,128)(2,1)} %query.1, bf16[1,128,4096]{2,1,0:T(8,128)(2,1)} %key.3, bf16[1,128,4096]{2,1,0:T(8,128)(2,1)} %value.3, bf16[1,128,4096]{2,1,0:T(8,128)(2,1)} %upstream.3, s32[1,128]{1,0:T(1,128)S(1)} %copy-done.7, bf16[4,4096]{1,0:T(4,128)(2,1)S(1)} %copy-done.5), custom_call_target="tpu_custom_call" | custom-call | bytes 6291456 | tf_op jit(solution)/shard_map/pallas_call | solution.py:322
  7.8 3.1 %collective-permute-start.3 = (bf16[2,4,128,128]{3,2,1,0:T(8,128)(2,1)S(1)}, bf16[2,4,128,128]{3,2,1,0:T(8,128)(2,1)S(1)}, u32[]{:S(2)}, u32[]{:S(2)}) collective-permute-start(bf16[2,4,128,128]{3,2,1,0:T(8,128)(2,1)S(1)} %pad_maximum_fusion.refs_0_), channel_id=1, source_target_pairs={{0,96},{32,0},{64,32},{96,64},{128,224},{160,128},{192,160},{224,1... | collective-permute-start | bytes 786440 | tf_op jit(solution)/shard_map/ppermute | solution.py:339
  10.9 0.6 collective-permute-start.2
  11.6 1.0 collective-permute-start.1
  12.5 59.2 %conditional.2 = (bf16[32,256,128]{2,1,0:T(8,128)(2,1)S(1)}) conditional(s32[]{:T(128)} %convert_element_type.4, bf16[32,256,128]{2,1,0:T(8,128)(2,1)S(1)} %shard_map.147, bf16[32,256,128]{2,1,0:T(8,128)(2,1)S(1)} %shard_map.147), branch_computations={%region_0.0_spmd, %region_1.0_spmd} | conditional | bytes 8388616 | solution.py:344
  12.5 0.1 copy.20
  12.7 59.0 %all_to_all.8 = bf16[32,256,128]{2,1,0:T(8,128)(2,1)S(1)} all-to-all(bf16[32,256,128]{2,1,0:T(8,128)(2,1)S(1)} %copy.20), channel_id=1, replica_groups=mesh['dp'=8,'seq'=32] {'seq'}, dimensions={0} | all-to-all | bytes 4194304 | tf_op jit(solution)/shard_map/cond/branch_1_fun/all_to_all | solution.py:346
  71.8 17.5 %shard_map.149 = (bf16[32,256,128]{2,1,0:T(8,128)(2,1)S(1)}, bf16[2,4,128,128]{3,2,1,0:T(8,128)(2,1)}, bf16[2,4,128,128]{3,2,1,0:T(8,128)(2,1)}, bf16[2,4,128,12...) custom-call(bf16[32,256,128]{2,1,0:T(8,128)(2,1)S(1)} %get-tuple-element.46.both_ref, ...), custom_call_target="tpu_custom_call" | custom-call | flops 6442450944 | bytes 12582912 | tf_op jit(solution)/shard_map/pallas_call | solution.py:322
  89.3 1.3 copy-done
  90.6 1.9 %collective-permute-start.4 = (bf16[2,4,128,128]{3,2,1,0:T(8,128)(2,1)}, bf16[2,4,128,128]{3,2,1,0:T(8,128)(2,1)S(1)}, u32[]{:S(2)}, u32[]{:S(2)}) collective-permute-start(bf16[2,4,128,128]{3,2,1,0:T(8,128)(2,1)} %get-tuple-element.33), channel_id=1, source_target_pairs={{0,32},{32,64},{64,96},{96,0},{128,160},{160,192},{192,224},{224,1... | collective-permute-start | bytes 786440 | tf_op jit(solution)/shard_map/ppermute | solution.py:339
  92.5 1.8 %collective-permute-start.5 = (bf16[2,4,128,128]{3,2,1,0:T(8,128)(2,1)}, bf16[2,4,128,128]{3,2,1,0:T(8,128)(2,1)S(1)}, u32[]{:S(2)}, u32[]{:S(2)}) collective-permute-start(bf16[2,4,128,128]{3,2,1,0:T(8,128)(2,1)} %get-tuple-element.34), channel_id=1, source_target_pairs={{0,64},{32,96},{64,0},{96,32},{128,192},{160,224},{192,128},{224,1... | collective-permute-start | bytes 786440 | tf_op jit(solution)/shard_map/ppermute | solution.py:339
  94.3 0.8 collective-permute-start.6
  95.2 59.6 %conditional.3 = (bf16[32,256,128]{2,1,0:T(8,128)(2,1)}) conditional(s32[]{:T(128)} %convert_element_type.4, bf16[32,256,128]{2,1,0:T(8,128)(2,1)} %copy-done, bf16[32,256,128]{2,1,0:T(8,128)(2,1)} %copy-done), branch_computations={%region_2.0_spmd, %region_3.0_spmd} | conditional | bytes 12582948 | solution.py:344
  95.2 1.6 %copy-done.2 = bf16[32,256,128]{2,1,0:T(8,128)(2,1)S(1)} copy-done((bf16[32,256,128]{2,1,0:T(8,128)(2,1)S(1)}, bf16[32,256,128]{2,1,0:T(8,128)(2,1)}, u32[]{:S(2)}) %copy-start.2) | copy-done | bytes 2097176 | tf_op jit(solution)/shard_map/cond
  96.8 58.0 %all_to_all.9 = bf16[32,256,128]{2,1,0:T(8,128)(2,1)} all-to-all(bf16[32,256,128]{2,1,0:T(8,128)(2,1)S(1)} %copy-done.2), channel_id=1, replica_groups=mesh['dp'=8,'seq'=32] {'seq'}, dimensions={0} | all-to-all | bytes 4194304 | tf_op jit(solution)/shard_map/cond/branch_1_fun/all_to_all | solution.py:346
  154.8 0.1 shard_map.151
  155.1 1.6 copy-done.1
  156.7 3.8 %shard_map.150 = (bf16[1,128,4096]{2,1,0:T(8,128)(2,1)}, bf16[1,128,4096]{2,1,0:T(8,128)(2,1)}, bf16[1,128,4096]{2,1,0:T(8,128)(2,1)}) custom-call(bf16[32,256,128]{2,1,0:T(8,128)(2,1)S(1)} %copy-done.1, bf16[1,128,4096]{2,1,0:T(8,128)(2,1)} %key.3, bf16[1,128,4096]{2,1,0:T(8,128)(2,1)} %value.3, bf16[1,128,4096]{2,1,0:T(8,128)(2,1)} %upstream.3, ...), custom_call_target="tpu_custom_call" | custom-call | bytes 6291456 | tf_op jit(solution)/shard_map/pallas_call | solution.py:322
  160.5 0.9 collective-permute-done.7.came_ref
  161.4 0.8 shard_map.152
  (28 shorter events, 0.3 us)
Async XLA Ops:
  0.6 1.0 copy-start.3
  1.7 6.1 %collective-permute-start = (bf16[4,128,128]{2,1,0:T(8,128)(2,1)S(1)}, bf16[4,128,128]{2,1,0:T(8,128)(2,1)S(1)}, u32[]{:S(2)}, u32[]{:S(2)}) collective-permute-start(bf16[4,128,128]{2,1,0:T(8,128)(2,1)S(1)} %shard_map.148), channel_id=1, source_target_pairs={{0,128},{32,160},{64,192},{96,224},{128,0},{160,32},{192,64},{224,... | collective-permute-start | bytes 393224 | tf_op jit(solution)/shard_map/ppermute | solution.py:339
  3.7 0.8 copy-start.5
  4.5 0.7 copy-start.7
  7.8 63.9 %collective-permute-start.3 = (bf16[2,4,128,128]{3,2,1,0:T(8,128)(2,1)S(1)}, bf16[2,4,128,128]{3,2,1,0:T(8,128)(2,1)S(1)}, u32[]{:S(2)}, u32[]{:S(2)}) collective-permute-start(bf16[2,4,128,128]{3,2,1,0:T(8,128)(2,1)S(1)} %pad_maximum_fusion.refs_0_), channel_id=1, source_target_pairs={{0,96},{32,0},{64,32},{96,64},{128,224},{160,128},{192,160},{224,1... | collective-permute-start | bytes 786440 | tf_op jit(solution)/shard_map/ppermute | solution.py:339
  10.9 60.8 %collective-permute-start.2 = (bf16[2,4,128,128]{3,2,1,0:T(8,128)(2,1)S(1)}, bf16[2,4,128,128]{3,2,1,0:T(8,128)(2,1)S(1)}, u32[]{:S(2)}, u32[]{:S(2)}) collective-permute-start(bf16[2,4,128,128]{3,2,1,0:T(8,128)(2,1)S(1)} %pad_maximum_fusion.refs_0_), channel_id=1, source_target_pairs={{0,64},{32,96},{64,0},{96,32},{128,192},{160,224},{192,128},{224,1... | collective-permute-start | bytes 786440 | tf_op jit(solution)/shard_map/ppermute | solution.py:339
  11.6 60.2 %collective-permute-start.1 = (bf16[2,4,128,128]{3,2,1,0:T(8,128)(2,1)S(1)}, bf16[2,4,128,128]{3,2,1,0:T(8,128)(2,1)S(1)}, u32[]{:S(2)}, u32[]{:S(2)}) collective-permute-start(bf16[2,4,128,128]{3,2,1,0:T(8,128)(2,1)S(1)} %pad_maximum_fusion.refs_0_), channel_id=1, source_target_pairs={{0,32},{32,64},{64,96},{96,0},{128,160},{160,192},{192,224},{224,1... | collective-permute-start | bytes 786440 | tf_op jit(solution)/shard_map/ppermute | solution.py:339
  12.5 59.2 %copy-start.9 = (f32[128]{0:T(128)S(1)}, f32[128]{0:T(128)}, u32[]{:S(2)}) copy-start(f32[128]{0:T(128)} %param.23) | copy-start | bytes 1540
  12.5 59.2 %copy-start.10 = (bf16[256,256]{1,0:T(8,128)(2,1)S(1)}, bf16[256,256]{1,0:T(8,128)(2,1)}, u32[]{:S(2)}) copy-start(bf16[256,256]{1,0:T(8,128)(2,1)} %constant.13.clone.refs_8_) | copy-start | bytes 393220
  12.5 59.2 %copy-start.11 = (bf16[256,256]{1,0:T(8,128)(2,1)S(1)}, bf16[256,256]{1,0:T(8,128)(2,1)}, u32[]{:S(2)}) copy-start(bf16[256,256]{1,0:T(8,128)(2,1)} %constant.12.clone.refs_7_) | copy-start | bytes 393220
  89.3 1.3 copy-start
  90.6 64.2 %collective-permute-start.4 = (bf16[2,4,128,128]{3,2,1,0:T(8,128)(2,1)}, bf16[2,4,128,128]{3,2,1,0:T(8,128)(2,1)S(1)}, u32[]{:S(2)}, u32[]{:S(2)}) collective-permute-start(bf16[2,4,128,128]{3,2,1,0:T(8,128)(2,1)} %get-tuple-element.33), channel_id=1, source_target_pairs={{0,32},{32,64},{64,96},{96,0},{128,160},{160,192},{192,224},{224,1... | collective-permute-start | bytes 786440 | tf_op jit(solution)/shard_map/ppermute | solution.py:339
  92.5 62.3 %collective-permute-start.5 = (bf16[2,4,128,128]{3,2,1,0:T(8,128)(2,1)}, bf16[2,4,128,128]{3,2,1,0:T(8,128)(2,1)S(1)}, u32[]{:S(2)}, u32[]{:S(2)}) collective-permute-start(bf16[2,4,128,128]{3,2,1,0:T(8,128)(2,1)} %get-tuple-element.34), channel_id=1, source_target_pairs={{0,64},{32,96},{64,0},{96,32},{128,192},{160,224},{192,128},{224,1... | collective-permute-start | bytes 786440 | tf_op jit(solution)/shard_map/ppermute | solution.py:339
  94.3 60.5 %collective-permute-start.6 = (bf16[2,4,128,128]{3,2,1,0:T(8,128)(2,1)}, bf16[2,4,128,128]{3,2,1,0:T(8,128)(2,1)S(1)}, u32[]{:S(2)}, u32[]{:S(2)}) collective-permute-start(bf16[2,4,128,128]{3,2,1,0:T(8,128)(2,1)} %get-tuple-element.35), channel_id=1, source_target_pairs={{0,96},{32,0},{64,32},{96,64},{128,224},{160,128},{192,160},{224,1... | collective-permute-start | bytes 786440 | tf_op jit(solution)/shard_map/ppermute | solution.py:339
  95.2 59.7 %copy-start.4 = (bf16[2,4,128,128]{3,2,1,0:T(8,128)(2,1)S(1)}, bf16[2,4,128,128]{3,2,1,0:T(8,128)(2,1)}, u32[]{:S(2)}) copy-start(bf16[2,4,128,128]{3,2,1,0:T(8,128)(2,1)} %get-tuple-element.40.refs_0_) | copy-start | bytes 786436
  95.2 59.9 %copy-start.6 = (bf16[4,4096]{1,0:T(4,128)(2,1)S(1)}, bf16[4,4096]{1,0:T(4,128)(2,1)}, u32[]{:S(2)}) copy-start(bf16[4,4096]{1,0:T(4,128)(2,1)} %rows_ref.3) | copy-start | bytes 98308
  95.2 59.9 %copy-start.8 = (s32[1,128]{1,0:T(1,128)S(1)}, s32[1,128]{1,0:T(1,128)}, u32[]{:S(2)}) copy-start(s32[1,128]{1,0:T(1,128)} %bases_ref.3) | copy-start | bytes 1540
  95.2 1.6 %copy-start.2 = (bf16[32,256,128]{2,1,0:T(8,128)(2,1)S(1)}, bf16[32,256,128]{2,1,0:T(8,128)(2,1)}, u32[]{:S(2)}) copy-start(bf16[32,256,128]{2,1,0:T(8,128)(2,1)} %param.3) | copy-start | bytes 6291460 | tf_op jit(solution)/shard_map/cond
  155.0 6.4 %collective-permute-start.7 = (bf16[4,128,128]{2,1,0:T(8,128)(2,1)S(1)}, bf16[4,128,128]{2,1,0:T(8,128)(2,1)S(1)}, u32[]{:S(2)}, u32[]{:S(2)}) collective-permute-start(bf16[4,128,128]{2,1,0:T(8,128)(2,1)S(1)} %get-tuple-element.45), channel_id=1, source_target_pairs={{0,128},{32,160},{64,192},{96,224},{128,0},{160,32},{192,64},{224,... | collective-permute-start | bytes 393224 | tf_op jit(solution)/shard_map/ppermute | solution.py:339
  155.1 1.6 copy-start.1

commit v4 on v3

--- a/solution.py
+++ b/solution.py
@@ -12,11 +12,10 @@
 LANES = 128
 SUB = 8
 PIECES = 8
-UNROLL = 8
-TABLE_PIECES = 4
 Z_PAIRS = 2
 Y_PLACES = 4
 TAP_BLOCKS = 4
+TABLE_PIECES = 2
 MEGA = 1024 * 1024
 VMEM = pltpu.VMEM
 bf16 = jnp.bfloat16
@@ -58,8 +57,14 @@
     return picked
 
 
-def gate_kernel(query, key, value, upstream, bases_ref, rows_ref, out_ref, held, sems):
+def gate_kernel(query, key, value, upstream, bases, rows, out_ref, held, bases_ref, rows_ref, sems, small_sems):
     tokens, width = query.shape[1:]
+    small = [
+        pltpu.make_async_copy(bases, bases_ref, small_sems.at[0]),
+        pltpu.make_async_copy(rows, rows_ref, small_sems.at[1]),
+    ]
+    for copy in small:
+        copy.start()
     span = width // PIECES
     copies = []
     for piece in range(PIECES):
@@ -72,6 +77,8 @@
             copy.start()
             row.append(copy)
         copies.append(row)
+    for copy in small:
+        copy.wait()
     letters = letters_of(bases_ref)
     for piece in range(PIECES):
         for copy in copies[piece]:
@@ -126,10 +133,19 @@
         copy.wait()
 
 
-def turn_kernel(in_ref, out_ref):
-    blocks, rows, channels = out_ref.shape
-    for block in range(blocks):
-        out_ref[block] = jnp.transpose(in_ref[:, block * rows : (block + 1) * rows]).astype(bf16)
+def turn_kernel(taps_hbm, out_ref, held, sems):
+    copies = []
+    for block in range(held.shape[0]):
+        columns = pl.ds(block * LANES, LANES)
+        copies.append(pltpu.make_async_copy(taps_hbm.at[:, columns], held.at[block], sems.at[block]))
+        copies[-1].start()
+    for block, copy in enumerate(copies):
+        copy.wait()
+        out_ref[block] = jnp.transpose(held[block]).astype(bf16)
+
+
+def chunk(pair, first=0):
+    return slice(first + pair * 2 * SUB, first + (pair + 1) * 2 * SUB)
 
 
 def first_stage(load, table, mid_ref):
@@ -141,7 +157,7 @@
             piece = piece.reshape(piece.shape[0] * SUB, piece.shape[2]).astype(bf16)
             mid = dot(table(2 * pair + part), piece)
             halves.append(mid.reshape(-1, SUB, mid.shape[1]))
-        mid_ref[:, pair * 2 * SUB : (pair + 1) * 2 * SUB, :] = jnp.concatenate(halves, axis=1).astype(bf16)
+        mid_ref[:, chunk(pair), :] = jnp.concatenate(halves, axis=1).astype(bf16)
 
 
 def last_stage(table, wide_ref, pair):
@@ -152,18 +168,6 @@
         out = dot(table(step), piece)
         halves.append(out.reshape(-1, SUB, out.shape[1]))
     return jnp.concatenate(halves, axis=1)
-
-
-def for_groups(count, work):
-    @pl.loop(0, count // UNROLL)
-    def _(turn):
-        for step in range(UNROLL):
-            work(turn * UNROLL + step)
-
-
-def group_of(ref, group):
-    both = ref[pl.ds(2 * group, 2)]
-    return both.reshape(2 * both.shape[1], both.shape[2])
 
 
 def times(left, right, conjugate):
@@ -184,121 +188,104 @@
     return index // Y_PLACES, lax.rem(index, Y_PLACES)
 
 
-def block_of(pair, turn):
-    pair_here, place_here = place()
-    owner = lax.rem(pair_here + pair, Z_PAIRS) * Y_PLACES + lax.rem(place_here + turn + Y_PLACES, Y_PLACES)
-    return pl.ds(owner * TAP_BLOCKS, TAP_BLOCKS)
-
-
-def middle_kernel(both_ref, *refs):
+def place_at(turn):
+    return lax.rem(place()[1] + turn + Y_PLACES, Y_PLACES)
+
+
+def middle_kernel(both_hbm, *refs):
     taps_hbm, refs = refs[:Y_PLACES], refs[Y_PLACES:]
     (skip_ref, ahead_hbm, back_hbm, second_ref, undo_ref, out_ref), refs = refs[:6], refs[6:]
     tap_outs, refs = refs[:Y_PLACES], refs[Y_PLACES:]
-    taps_ref, ahead_ref, back_ref, tap_mid_ref, mid_ref, spectrum_ref, cross_ref, wide_ref = refs[:8]
-    taps_sems, ahead_sems, back_sems, out_sems = refs[8:]
+    both_ref, taps_ref, mid_ref, wide_ref, ahead_ref, back_ref = refs[:6]
+    both_sem, taps_sems, out_sems, ahead_sems, back_sem = refs[6:]
     groups = both_ref.shape[0]
     tokens = both_ref.shape[1] // 2
     steps = ahead_ref.shape[0]
-    pairs = steps // 2
-
-    def chunk(pair):
-        return slice(pair * 2 * SUB, (pair + 1) * 2 * SUB)
-
-    tap_copies = []
-    for turn in range(Y_PLACES):
-        for pair in range(Z_PAIRS):
-            target = taps_ref.at[block_of(pair, -turn)]
-            tap_copies.append(pltpu.make_async_copy(taps_hbm[turn].at[pair], target, taps_sems.at[turn, pair]))
-            tap_copies[-1].start()
     span = steps // TABLE_PIECES
     ahead_copies = []
-    back_copies = []
-    for source, target, sems, copies in (
-        (ahead_hbm, ahead_ref, ahead_sems, ahead_copies),
-        (back_hbm, back_ref, back_sems, back_copies),
-    ):
-        for piece in range(TABLE_PIECES):
-            rows = pl.ds(piece * span, span)
-            copies.append(pltpu.make_async_copy(source.at[rows], target.at[rows], sems.at[piece]))
-            copies[-1].start()
-
-    for copy in tap_copies:
+    for piece in range(TABLE_PIECES):
+        rows = pl.ds(piece * span, span)
+        ahead_copies.append(pltpu.make_async_copy(ahead_hbm.at[rows], ahead_ref.at[rows], ahead_sems.at[piece]))
+    back_copy = pltpu.make_async_copy(back_hbm, back_ref, back_sem)
+    ahead_copies[0].start()
+    arriving = [pltpu.make_async_copy(both_hbm, both_ref, both_sem)]
+    arriving[-1].start()
+    for turn in range(Y_PLACES):
+        arriving.append(
+            pltpu.make_async_copy(taps_hbm[turn], taps_ref.at[:, place_at(-turn)], taps_sems.at[turn])
+        )
+        arriving[-1].start()
+    for copy in ahead_copies[1:] + [back_copy]:
+        copy.start()
+    for copy in arriving:
         copy.wait()
 
-    def load_taps(pair):
-        return taps_ref[:, chunk(pair), :].astype(jnp.float32)
+    def load(pair):
+        filt = taps_ref[:, :, :, chunk(pair), :].reshape(groups, 2 * SUB, LANES)
+        parts = [both_ref[:, chunk(pair), :], both_ref[:, chunk(pair, tokens), :], filt]
+        return jnp.concatenate(parts, axis=2).astype(jnp.float32)
 
     def fresh_ahead(step):
         if step % span == 0:
             ahead_copies[step // span].wait()
         return ahead_ref[step]
 
-    first_stage(load_taps, fresh_ahead, tap_mid_ref)
-
-    def transform_taps(group):
-        spectrum_ref[group] = dot(second_ref[...], group_of(tap_mid_ref, group))
-
-    for_groups(groups, transform_taps)
-
-    def load_both(pair):
-        rows = chunk(pair)
-        more = slice(tokens + rows.start, tokens + rows.stop)
-        return jnp.concatenate([both_ref[:, rows, :], both_ref[:, more, :]], axis=2).astype(jnp.float32)
-
-    first_stage(load_both, lambda step: ahead_ref[step], mid_ref)
-
-    def work(group):
-        spectrum = dot(second_ref[...], group_of(mid_ref, group))
-        gated, grad = spectrum[:, :LANES], spectrum[:, LANES:]
-        taps = spectrum_ref[group]
-        conv = times(gated, taps, False)
-        corr = times(grad, taps, True)
-        cross_ref[group] = times(grad, gated, True).astype(bf16)
-        undone = dot(undo_ref[...], jnp.concatenate([conv, corr], axis=1).astype(bf16))
-        wide_ref[pl.ds(2 * group, 2)] = undone.reshape(2, -1, undone.shape[1])
-
-    for_groups(groups, work)
-
-    for copy in back_copies:
-        copy.wait()
-
-    def back_table(step):
-        return back_ref[step]
+    first_stage(load, fresh_ahead, mid_ref)
+
+    def group_of(group, columns):
+        both = mid_ref[2 * group : 2 * group + 2, :, columns]
+        return both.reshape(2 * tokens, both.shape[2])
+
+    second, undo = second_ref[...], undo_ref[...]
+    signals, taps = slice(0, 2 * LANES), slice(2 * LANES, 3 * LANES)
+    for pair in range(groups // 2):
+        here = (2 * pair, 2 * pair + 1)
+        filters = dot(second, jnp.concatenate([group_of(group, taps) for group in here], axis=1))
+        crosses = []
+        for which, group in enumerate(here):
+            spectrum = dot(second, group_of(group, signals))
+            gated, grad = spectrum[:, :LANES], spectrum[:, LANES:]
+            filt = filters[:, which * LANES : (which + 1) * LANES]
+            product = jnp.concatenate([times(gated, filt, False), times(grad, filt, True)], axis=1)
+            undone = dot(undo, product.astype(bf16))
+            wide_ref[2 * group : 2 * group + 2, :, signals] = undone.reshape(2, tokens, 2 * LANES)
+            crosses.append(times(grad, gated, True))
+        undone = dot(undo, jnp.concatenate(crosses, axis=1).astype(bf16))
+        for which, group in enumerate(here):
+            part = undone[:, which * LANES : (which + 1) * LANES]
+            wide_ref[2 * group : 2 * group + 2, :, taps] = part.reshape(2, tokens, LANES)
 
     skip = skip_ref[...]
-    for pair in range(pairs):
-        sums = last_stage(back_table, wide_ref, pair)
+
+    back_copy.wait()
+
+    for pair in range(steps // 2):
+        sums = last_stage(lambda step: back_ref[step], wide_ref, pair)
         for part in range(2):
-            rows = slice(part * tokens + pair * 2 * SUB, part * tokens + (pair + 1) * 2 * SUB)
+            rows = chunk(pair, part * tokens)
             direct = skip * both_ref[:, rows, :].astype(jnp.float32)
             out_ref[:, rows, :] = (sums[:, :, part * LANES : (part + 1) * LANES] + direct).astype(bf16)
-
-    def undo_cross(group):
-        undone = dot(undo_ref[...], cross_ref[group])
-        spectrum_wide[pl.ds(2 * group, 2)] = undone.reshape(2, -1, undone.shape[1])
-
-    spectrum_wide = wide_ref.at[:, :, :LANES]
-    for_groups(groups, undo_cross)
-    for pair in range(pairs):
-        taps_ref[:, chunk(pair), :] = last_stage(back_table, spectrum_wide, pair).astype(bf16)
+        tap_grad = sums[:, :, taps].astype(bf16)
+        taps_ref[:, :, :, chunk(pair), :] = tap_grad.reshape(taps_ref.shape[:3] + (2 * SUB, LANES))
 
     leaving = []
     for turn in range(Y_PLACES):
-        for pair in range(Z_PAIRS):
-            source = taps_ref.at[block_of(pair, turn)]
-            leaving.append(pltpu.make_async_copy(source, tap_outs[turn].at[pair], out_sems.at[turn, pair]))
-            leaving[-1].start()
+        leaving.append(
+            pltpu.make_async_copy(taps_ref.at[:, place_at(turn)], tap_outs[turn], out_sems.at[turn])
+        )
+        leaving[-1].start()
     for copy in leaving:
         copy.wait()
 
 
 def join_kernel(*refs):
     parts, (kept_ref, sent_ref) = refs[:-2], refs[-2:]
-    total = parts[0][...].astype(jnp.float32)
-    for part in parts[1:]:
-        total = total + part[...].astype(jnp.float32)
-    kept_ref[...] = total[0]
-    sent_ref[...] = total[1].astype(bf16)
+    here = place()[0]
+    for pair, out_ref in ((here, kept_ref), (Z_PAIRS - 1 - here, sent_ref)):
+        total = parts[0][pair].astype(jnp.float32)
+        for part in parts[1:]:
+            total = total + part[pair].astype(jnp.float32)
+        out_ref[...] = total.astype(out_ref.dtype)
 
 
 def finish_kernel(kept_ref, came_ref, out_ref):
@@ -339,14 +326,55 @@
     return lax.ppermute(array, "dp", moves)
 
 
-def exchange(array):
+def exchange(array, other=lambda whole: whole):
     always = lax.optimization_barrier(jnp.int32(1)) == 1
     return lax.cond(
         always,
         lambda whole: lax.all_to_all(whole, "seq", split_axis=0, concat_axis=0, tiled=True),
-        lambda whole: whole,
+        other,
         array,
     )
+
+
+def middle(both, taps, skip):
+    groups, both_rows, channels = both.shape
+    tokens = both_rows // 2
+    length = groups * tokens
+    ahead, back, second, undo = (jnp.asarray(table) for table in transform_tables(groups, tokens, length ** (-0.5)))
+    steps = ahead.shape[0]
+    far, free, dma = pltpu.HBM, None, pltpu.SemaphoreType.DMA
+    tap_pair = (taps[0].shape, bf16, far)
+    wide = (2 * groups, tokens, 3 * channels)
+    out, *tap_grads = call(
+        middle_kernel,
+        [(both, pl.ANY)]
+        + [(part, pl.ANY) for part in taps]
+        + [
+            (skip, free),
+            (ahead, far),
+            (back, far),
+            (second, free),
+            (undo, free),
+        ],
+        [(both.shape, bf16, VMEM)] + [tap_pair] * Y_PLACES,
+        [
+            VMEM(both.shape, bf16),
+            VMEM((Z_PAIRS, Y_PLACES) + taps[0].shape[1:], bf16),
+            VMEM(wide, bf16),
+            VMEM(wide, jnp.float32),
+            VMEM(ahead.shape, bf16),
+            VMEM(back.shape, bf16),
+            dma(()),
+            dma((Y_PLACES,)),
+            dma((Y_PLACES,)),
+            dma((TABLE_PIECES,)),
+            dma(()),
+        ],
+        32,
+        flops=2 * 24 * length * 256 * channels,
+        moved=24 * length * channels,
+    )
+    return out, tap_grads
 
 
 def local(query, key_stream, value_stream, upstream, bases, base_rows, long_filter, skip_weight):
@@ -354,63 +382,41 @@
     tokens, width = query.shape[1:]
     length = tokens * groups
     channels = long_filter.shape[0]
-    ahead, back, second, undo = (jnp.asarray(table) for table in transform_tables(groups, tokens, length ** (-0.5)))
     array_bytes = tokens * width * 2
     far, free, dma = pltpu.HBM, None, pltpu.SemaphoreType.DMA
-    steps = ahead.shape[0]
     packed = ((groups, 2 * tokens, channels), bf16, VMEM)
     tap_block = (TAP_BLOCKS, tokens, channels)
-    tap_pair = ((Z_PAIRS,) + tap_block, bf16, far)
-
-    (turned,) = call(turn_kernel, [(long_filter, free)], [(tap_block, bf16, free)], [], 4)
+
+    (turned,) = call(
+        turn_kernel,
+        [(long_filter, far)],
+        [(tap_block, bf16, free)],
+        [VMEM((TAP_BLOCKS, channels, tokens), jnp.float32), dma((TAP_BLOCKS,))],
+        4,
+    )
     other = along_dp(turned, 1, 0)
     (gates,) = call(
         gate_kernel,
-        [(query, far), (key_stream, far), (value_stream, far), (upstream, far), (bases, free), (base_rows, free)],
+        [(query, far), (key_stream, far), (value_stream, far), (upstream, far), (bases, far), (base_rows, far)],
         [packed],
-        [VMEM((4, tokens, width), bf16), dma((4, PIECES))],
+        [
+            VMEM((4, tokens, width), bf16),
+            VMEM(bases.shape, bases.dtype),
+            VMEM(base_rows.shape, bf16),
+            dma((4, PIECES)),
+            dma((2,)),
+        ],
         12,
         moved=6 * array_bytes,
     )
-    gates, own_taps = lax.optimization_barrier((gates, jnp.stack([turned, other])))
+    own_taps = jnp.where(place()[0] == 0, jnp.stack([turned, other]), jnp.stack([other, turned]))
+    gates, own_taps = lax.optimization_barrier((gates, own_taps))
     taps = [own_taps] + [along_dp(own_taps, 0, turn) for turn in range(1, Y_PLACES)]
     both = exchange(gates)
 
-    half_mid = (2 * groups, tokens, channels)
-    wide_mid = (2 * groups, tokens, 2 * channels)
-    spectra = (groups, 2 * tokens, channels)
-    out, *tap_grads = call(
-        middle_kernel,
-        [(both, VMEM)]
-        + [(part, pl.ANY) for part in taps]
-        + [
-            (skip_weight.reshape(1, channels), free),
-            (ahead, far),
-            (back, far),
-            (second, free),
-            (undo, free),
-        ],
-        [packed] + [tap_pair] * Y_PLACES,
-        [
-            VMEM((groups, tokens, channels), bf16),
-            VMEM(ahead.shape, bf16),
-            VMEM(back.shape, bf16),
-            VMEM(half_mid, bf16),
-            VMEM(wide_mid, bf16),
-            VMEM(spectra, jnp.float32),
-            VMEM(spectra, bf16),
-            VMEM(wide_mid, jnp.float32),
-            dma((Y_PLACES, Z_PAIRS)),
-            dma((TABLE_PIECES,)),
-            dma((TABLE_PIECES,)),
-            dma((Y_PLACES, Z_PAIRS)),
-        ],
-        40,
-        flops=2 * 24 * length * 256 * channels,
-        moved=12 * array_bytes,
-    )
+    out, tap_grads = middle(both, taps, skip_weight.reshape(1, channels))
     came = [along_dp(tap_grads[turn], 0, turn) for turn in range(1, Y_PLACES)]
-    home, *came = lax.optimization_barrier((exchange(out), *came))
+    home, *came = lax.optimization_barrier((exchange(out, lambda whole: whole + whole), *came))
 
     kept, sent = call(
         join_kernel,

time: 164 us -> 156 us (0.951)
  local copies, waits for them, and re-layouts: 7.06 us -> 0.16 us
  Pallas kernels: 25 us -> 23 us
    unnamed x22 -> x12, local copies, waits for them, and re-layouts: 5.29 us -> 0.02 us
    pallas_call x6, Pallas kernels: 25 us -> 23 us  [call(): pl.pallas_call(kernel, out_shape=tuple(out_shape), in_specs=in_specs, out...]
  transfers between devices with their start and end apart: 8 -> 8, of which waited for: 1 -> 1; matrix products, arithmetic and copies ran while one was open for 0% -> 0% of each run, Pallas kernels for 4% -> 5%
where the time goes in v4:
time: 156 us; the launch traced here: 155 us
  blocking collectives  117 us (75%)
  Pallas kernels  23 us (15%)
  starting transfers between devices  11.5 us (7%)
  waiting for transfers between devices  2.52 us (2%)
    all_to_all x2, blocking collectives, exchange(): lax.all_to_all(whole, 'seq', split_axis=0, concat_axis=0, tiled=True)  117 us
    pallas_call x6, Pallas kernels, call(): pl.pallas_call(kernel, out_shape=tuple(out_shape), in_specs=in_specs, out...  23 us
    ppermute x8, starting transfers between devices, along_dp(): return lax.ppermute(array, 'dp', moves)  11.5 us
  transfers between devices with their start and end apart: 8, of which 1 were waited for; matrix products, arithmetic and copies ran while one was open for 0% of the time, Pallas kernels for 5%

profile of v4, /device:TPU:2, one launch (start us, length us, event | category | flops | bytes accessed | tf_op | source)
XLA Modules:
  0.0 155.5 jit_solution(12445654510123902982)
XLA Ops:
  0.6 1.3 shard_map.148
  1.9 2.0 %collective-permute-start = (bf16[4,128,128]{2,1,0:T(8,128)(2,1)S(1)}, bf16[4,128,128]{2,1,0:T(8,128)(2,1)S(1)}, u32[]{:S(2)}, u32[]{:S(2)}) collective-permute-start(bf16[4,128,128]{2,1,0:T(8,128)(2,1)S(1)} %shard_map.148), channel_id=1, source_target_pairs={{0,128},{32,160},{64,192},{96,224},{128,0},{160,32},{192,64},{224,... | collective-permute-start | bytes 393224 | tf_op jit(solution)/shard_map/ppermute | solution.py:326
  3.9 3.6 %shard_map.147 = bf16[32,256,128]{2,1,0:T(8,128)(2,1)S(1)} custom-call(bf16[1,128,4096]{2,1,0:T(8,128)(2,1)} %query.1, bf16[1,128,4096]{2,1,0:T(8,128)(2,1)} %key.3, bf16[1,128,4096]{2,1,0:T(8,128)(2,1)} %value.3, bf16[1,128,4096]{2,1,0:T(8,128)(2,1)} %upstream.3, s32[1,128]{1,0:T(1,128)} %bases_ref.1, bf16[4,4096]{1,0:T(4,128)(2,1)} %rows_ref.1), custom_call_target="tpu_custom_call" | custom-call | bytes 6291456 | tf_op jit(solution)/shard_map/pallas_call | solution.py:309
  7.5 0.0 collective-permute-done
  7.6 3.1 %collective-permute-start.3 = (bf16[2,4,128,128]{3,2,1,0:T(8,128)(2,1)S(1)}, bf16[2,4,128,128]{3,2,1,0:T(8,128)(2,1)S(1)}, u32[]{:S(2)}, u32[]{:S(2)}) collective-permute-start(bf16[2,4,128,128]{3,2,1,0:T(8,128)(2,1)S(1)} %maximum_select_fusion.refs_0_), channel_id=1, source_target_pairs={{0,96},{32,0},{64,32},{96,64},{128,224},{160,128},{192,160},{224,1... | collective-permute-start | bytes 786440 | tf_op jit(solution)/shard_map/ppermute | solution.py:326
  10.7 0.6 collective-permute-start.2
  11.3 1.0 collective-permute-start.1
  12.3 59.7 %conditional.2 = (bf16[32,256,128]{2,1,0:T(8,128)(2,1)S(1)}) conditional(s32[]{:T(128)} %convert_element_type.4, bf16[32,256,128]{2,1,0:T(8,128)(2,1)S(1)} %shard_map.147, bf16[32,256,128]{2,1,0:T(8,128)(2,1)S(1)} %shard_map.147), branch_computations={%region_0.1_spmd, %region_1.2_spmd} | conditional | bytes 8388616 | solution.py:331
  12.3 0.1 copy.20
  12.4 59.5 %all_to_all.8 = bf16[32,256,128]{2,1,0:T(8,128)(2,1)S(1)} all-to-all(bf16[32,256,128]{2,1,0:T(8,128)(2,1)S(1)} %copy.20), channel_id=1, replica_groups=mesh['dp'=8,'seq'=32] {'seq'}, dimensions={0} | all-to-all | bytes 4194304 | tf_op jit(solution)/shard_map/cond/branch_1_fun/all_to_all | solution.py:333
  71.9 0.0 collective-permute-done.3.refs_3_
  72.0 13.3 %shard_map.149 = (bf16[32,256,128]{2,1,0:T(8,128)(2,1)S(1)}, bf16[2,4,128,128]{3,2,1,0:T(8,128)(2,1)}, bf16[2,4,128,128]{3,2,1,0:T(8,128)(2,1)}, bf16[2,4,128,12...) custom-call(bf16[32,256,128]{2,1,0:T(8,128)(2,1)S(1)} %get-tuple-element.46.both_hbm, ...), custom_call_target="tpu_custom_call" | custom-call | flops 6442450944 | bytes 12582912 | tf_op jit(solution)/shard_map/pallas_call | solution.py:309
  85.3 2.0 %collective-permute-start.4 = (bf16[2,4,128,128]{3,2,1,0:T(8,128)(2,1)}, bf16[2,4,128,128]{3,2,1,0:T(8,128)(2,1)S(1)}, u32[]{:S(2)}, u32[]{:S(2)}) collective-permute-start(bf16[2,4,128,128]{3,2,1,0:T(8,128)(2,1)} %get-tuple-element.33), channel_id=1, source_target_pairs={{0,32},{32,64},{64,96},{96,0},{128,160},{160,192},{192,224},{224,1... | collective-permute-start | bytes 786440 | tf_op jit(solution)/shard_map/ppermute | solution.py:326
  87.3 1.8 %collective-permute-start.5 = (bf16[2,4,128,128]{3,2,1,0:T(8,128)(2,1)}, bf16[2,4,128,128]{3,2,1,0:T(8,128)(2,1)S(1)}, u32[]{:S(2)}, u32[]{:S(2)}) collective-permute-start(bf16[2,4,128,128]{3,2,1,0:T(8,128)(2,1)} %get-tuple-element.34), channel_id=1, source_target_pairs={{0,64},{32,96},{64,0},{96,32},{128,192},{160,224},{192,128},{224,1... | collective-permute-start | bytes 786440 | tf_op jit(solution)/shard_map/ppermute | solution.py:326
  89.1 0.9 collective-permute-start.6
  90.1 58.0 %conditional.3 = (bf16[32,256,128]{2,1,0:T(8,128)(2,1)S(1)}) conditional(s32[]{:T(128)} %convert_element_type.4, bf16[32,256,128]{2,1,0:T(8,128)(2,1)S(1)} %get-tuple-element.32, bf16[32,256,128]{2,1,0:T(8,128)(2,1)S(1)} %get-tuple-element.32), branch_computations={%region_2.3_spmd, %region_3.4_spmd} | conditional | bytes 6291464 | solution.py:331
  90.1 58.0 %all_to_all.9 = bf16[32,256,128]{2,1,0:T(8,128)(2,1)S(1)} all-to-all(bf16[32,256,128]{2,1,0:T(8,128)(2,1)S(1)} %param.3), channel_id=1, replica_groups=mesh['dp'=8,'seq'=32] {'seq'}, dimensions={0} | all-to-all | bytes 4194304 | tf_op jit(solution)/shard_map/cond/branch_1_fun/all_to_all | solution.py:333
  148.0 0.0 collective-permute-done.5.refs_2_
  148.0 0.0 collective-permute-done.6.refs_3_
  148.1 0.1 shard_map.151
  148.2 0.1 collective-permute-start.7
  148.3 3.8 %shard_map.150 = (bf16[1,128,4096]{2,1,0:T(8,128)(2,1)}, bf16[1,128,4096]{2,1,0:T(8,128)(2,1)}, bf16[1,128,4096]{2,1,0:T(8,128)(2,1)}) custom-call(bf16[32,256,128]{2,1,0:T(8,128)(2,1)S(1)} %get-tuple-element.47.back_ref, bf16[1,128,4096]{2,1,0:T(8,128)(2,1)} %key.3, bf16[1,128,4096]{2,1,0:T(8,128)(2,1)} %value.3, bf16[1,128,4096]{2,1,0:T(8,128)(2,1)} %upstream.3, ...), custom_call_target="tpu_custom_call" | custom-call | bytes 6291456 | tf_op jit(solution)/shard_map/pallas_call | solution.py:309
  152.1 2.5 %collective-permute-done.7.came_ref = bf16[4,128,128]{2,1,0:T(8,128)(2,1)S(1)} collective-permute-done((bf16[4,128,128]{2,1,0:T(8,128)(2,1)S(1)}, bf16[4,128,128]{2,1,0:T(8,128)(2,1)S(1)}, u32[]{:S(2)}, u32[]{:S(2)}) %collective-permute-start.7) | collective-permute-done | bytes 131104 | tf_op jit(solution)/shard_map/ppermute | solution.py:326
  154.6 0.8 shard_map.152
  (16 shorter events, 0.1 us)
Async XLA Ops:
  1.9 5.6 %collective-permute-start = (bf16[4,128,128]{2,1,0:T(8,128)(2,1)S(1)}, bf16[4,128,128]{2,1,0:T(8,128)(2,1)S(1)}, u32[]{:S(2)}, u32[]{:S(2)}) collective-permute-start(bf16[4,128,128]{2,1,0:T(8,128)(2,1)S(1)} %shard_map.148), channel_id=1, source_target_pairs={{0,128},{32,160},{64,192},{96,224},{128,0},{160,32},{192,64},{224,... | collective-permute-start | bytes 393224 | tf_op jit(solution)/shard_map/ppermute | solution.py:326
  7.6 64.4 %collective-permute-start.3 = (bf16[2,4,128,128]{3,2,1,0:T(8,128)(2,1)S(1)}, bf16[2,4,128,128]{3,2,1,0:T(8,128)(2,1)S(1)}, u32[]{:S(2)}, u32[]{:S(2)}) collective-permute-start(bf16[2,4,128,128]{3,2,1,0:T(8,128)(2,1)S(1)} %maximum_select_fusion.refs_0_), channel_id=1, source_target_pairs={{0,96},{32,0},{64,32},{96,64},{128,224},{160,128},{192,160},{224,1... | collective-permute-start | bytes 786440 | tf_op jit(solution)/shard_map/ppermute | solution.py:326
  10.7 61.3 %collective-permute-start.2 = (bf16[2,4,128,128]{3,2,1,0:T(8,128)(2,1)S(1)}, bf16[2,4,128,128]{3,2,1,0:T(8,128)(2,1)S(1)}, u32[]{:S(2)}, u32[]{:S(2)}) collective-permute-start(bf16[2,4,128,128]{3,2,1,0:T(8,128)(2,1)S(1)} %maximum_select_fusion.refs_0_), channel_id=1, source_target_pairs={{0,64},{32,96},{64,0},{96,32},{128,192},{160,224},{192,128},{224,1... | collective-permute-start | bytes 786440 | tf_op jit(solution)/shard_map/ppermute | solution.py:326
  11.3 60.6 %collective-permute-start.1 = (bf16[2,4,128,128]{3,2,1,0:T(8,128)(2,1)S(1)}, bf16[2,4,128,128]{3,2,1,0:T(8,128)(2,1)S(1)}, u32[]{:S(2)}, u32[]{:S(2)}) collective-permute-start(bf16[2,4,128,128]{3,2,1,0:T(8,128)(2,1)S(1)} %maximum_select_fusion.refs_0_), channel_id=1, source_target_pairs={{0,32},{32,64},{64,96},{96,0},{128,160},{160,192},{192,224},{224,1... | collective-permute-start | bytes 786440 | tf_op jit(solution)/shard_map/ppermute | solution.py:326
  12.3 59.7 %copy-start.3 = (f32[128]{0:T(128)S(1)}, f32[128]{0:T(128)}, u32[]{:S(2)}) copy-start(f32[128]{0:T(128)} %param.23) | copy-start | bytes 1540
  12.3 59.7 %copy-start.4 = (bf16[256,256]{1,0:T(8,128)(2,1)S(1)}, bf16[256,256]{1,0:T(8,128)(2,1)}, u32[]{:S(2)}) copy-start(bf16[256,256]{1,0:T(8,128)(2,1)} %constant.35.clone.refs_8_) | copy-start | bytes 393220
  12.3 59.7 %copy-start.5 = (bf16[256,256]{1,0:T(8,128)(2,1)S(1)}, bf16[256,256]{1,0:T(8,128)(2,1)}, u32[]{:S(2)}) copy-start(bf16[256,256]{1,0:T(8,128)(2,1)} %constant.34.clone.refs_7_) | copy-start | bytes 393220
  85.3 62.7 %collective-permute-start.4 = (bf16[2,4,128,128]{3,2,1,0:T(8,128)(2,1)}, bf16[2,4,128,128]{3,2,1,0:T(8,128)(2,1)S(1)}, u32[]{:S(2)}, u32[]{:S(2)}) collective-permute-start(bf16[2,4,128,128]{3,2,1,0:T(8,128)(2,1)} %get-tuple-element.33), channel_id=1, source_target_pairs={{0,32},{32,64},{64,96},{96,0},{128,160},{160,192},{192,224},{224,1... | collective-permute-start | bytes 786440 | tf_op jit(solution)/shard_map/ppermute | solution.py:326
  87.3 60.7 %collective-permute-start.5 = (bf16[2,4,128,128]{3,2,1,0:T(8,128)(2,1)}, bf16[2,4,128,128]{3,2,1,0:T(8,128)(2,1)S(1)}, u32[]{:S(2)}, u32[]{:S(2)}) collective-permute-start(bf16[2,4,128,128]{3,2,1,0:T(8,128)(2,1)} %get-tuple-element.34), channel_id=1, source_target_pairs={{0,64},{32,96},{64,0},{96,32},{128,192},{160,224},{192,128},{224,1... | collective-permute-start | bytes 786440 | tf_op jit(solution)/shard_map/ppermute | solution.py:326
  89.1 58.9 %collective-permute-start.6 = (bf16[2,4,128,128]{3,2,1,0:T(8,128)(2,1)}, bf16[2,4,128,128]{3,2,1,0:T(8,128)(2,1)S(1)}, u32[]{:S(2)}, u32[]{:S(2)}) collective-permute-start(bf16[2,4,128,128]{3,2,1,0:T(8,128)(2,1)} %get-tuple-element.35), channel_id=1, source_target_pairs={{0,96},{32,0},{64,32},{96,64},{128,224},{160,128},{192,160},{224,1... | collective-permute-start | bytes 786440 | tf_op jit(solution)/shard_map/ppermute | solution.py:326
  90.1 58.0 %copy-start = (bf16[2,4,128,128]{3,2,1,0:T(8,128)(2,1)S(1)}, bf16[2,4,128,128]{3,2,1,0:T(8,128)(2,1)}, u32[]{:S(2)}) copy-start(bf16[2,4,128,128]{3,2,1,0:T(8,128)(2,1)} %get-tuple-element.40.refs_0_) | copy-start | bytes 786436
  90.1 58.2 %copy-start.1 = (bf16[4,4096]{1,0:T(4,128)(2,1)S(1)}, bf16[4,4096]{1,0:T(4,128)(2,1)}, u32[]{:S(2)}) copy-start(bf16[4,4096]{1,0:T(4,128)(2,1)} %rows_ref.1) | copy-start | bytes 98308
  90.1 58.2 %copy-start.2 = (s32[1,128]{1,0:T(1,128)S(1)}, s32[1,128]{1,0:T(1,128)}, u32[]{:S(2)}) copy-start(s32[1,128]{1,0:T(1,128)} %bases_ref.1) | copy-start | bytes 1540
  148.2 6.4 %collective-permute-start.7 = (bf16[4,128,128]{2,1,0:T(8,128)(2,1)S(1)}, bf16[4,128,128]{2,1,0:T(8,128)(2,1)S(1)}, u32[]{:S(2)}, u32[]{:S(2)}) collective-permute-start(bf16[4,128,128]{2,1,0:T(8,128)(2,1)S(1)} %get-tuple-element.45), channel_id=1, source_target_pairs={{0,128},{32,160},{64,192},{96,224},{128,0},{160,32},{192,64},{224,... | collective-permute-start | bytes 393224 | tf_op jit(solution)/shard_map/ppermute | solution.py:326

commit v5 on v4

--- a/solution.py
+++ b/solution.py
@@ -11,7 +11,7 @@
 
 LANES = 128
 SUB = 8
-PIECES = 8
+PIECES = 4
 Z_PAIRS = 2
 Y_PLACES = 4
 TAP_BLOCKS = 4
@@ -59,74 +59,73 @@
 
 def gate_kernel(query, key, value, upstream, bases, rows, out_ref, held, bases_ref, rows_ref, sems, small_sems):
     tokens, width = query.shape[1:]
+    span = tokens // PIECES
     small = [
         pltpu.make_async_copy(bases, bases_ref, small_sems.at[0]),
         pltpu.make_async_copy(rows, rows_ref, small_sems.at[1]),
     ]
-    for copy in small:
-        copy.start()
-    span = width // PIECES
     copies = []
     for piece in range(PIECES):
-        columns = pl.ds(piece * span, span)
-        row = []
+        part = pl.ds(piece * span, span)
+        copies.append([])
         for which, source in enumerate((query, key, value, upstream)):
-            copy = pltpu.make_async_copy(
-                source.at[0, :, columns], held.at[which, :, columns], sems.at[which, piece]
+            copies[-1].append(
+                pltpu.make_async_copy(source.at[0, part], held.at[which, part], sems.at[which, piece])
             )
-            copy.start()
-            row.append(copy)
-        copies.append(row)
+            copies[-1][-1].start()
+        if piece == 0:
+            for copy in small:
+                copy.start()
     for copy in small:
         copy.wait()
     letters = letters_of(bases_ref)
     for piece in range(PIECES):
+        part = slice(piece * span, (piece + 1) * span)
+        here = letters[part]
         for copy in copies[piece]:
             copy.wait()
-        for block in range(piece * span // LANES, (piece + 1) * span // LANES):
+        for block in range(width // LANES):
             columns = slice(block * LANES, (block + 1) * LANES)
             query_rows, key_rows, value_rows, upstream_rows = (
-                held[which, :, columns].astype(jnp.float32) for which in range(4)
+                held[which, part, columns].astype(jnp.float32) for which in range(4)
             )
-            out_grad = upstream_rows - readout(letters, rows_ref, columns)
-            out_ref[block, :tokens, :] = (key_rows * value_rows).astype(bf16)
-            out_ref[block, tokens:, :] = (out_grad * query_rows).astype(bf16)
+            out_grad = upstream_rows - readout(here, rows_ref, columns)
+            out_ref[block, part, :] = (key_rows * value_rows).astype(bf16)
+            out_ref[block, tokens + part.start : tokens + part.stop, :] = (out_grad * query_rows).astype(bf16)
 
 
 def ungate_kernel(back_ref, key, value, upstream, bases_ref, rows_ref, *rest):
     outs, (held, in_sems, made, out_sems) = rest[:3], rest[3:]
     tokens, width = key.shape[1:]
-    span = width // PIECES
+    span = tokens // PIECES
     arriving = []
     for piece in range(PIECES):
-        columns = pl.ds(piece * span, span)
-        row = []
+        part = pl.ds(piece * span, span)
+        arriving.append([])
         for which, source in enumerate((key, value, upstream)):
-            copy = pltpu.make_async_copy(
-                source.at[0, :, columns], held.at[which, :, columns], in_sems.at[which, piece]
+            arriving[-1].append(
+                pltpu.make_async_copy(source.at[0, part], held.at[which, part], in_sems.at[which, piece])
             )
-            copy.start()
-            row.append(copy)
-        arriving.append(row)
+            arriving[-1][-1].start()
     letters = letters_of(bases_ref)
     leaving = []
     for piece in range(PIECES):
+        part = slice(piece * span, (piece + 1) * span)
+        here = letters[part]
         for copy in arriving[piece]:
             copy.wait()
-        for block in range(piece * span // LANES, (piece + 1) * span // LANES):
+        for block in range(width // LANES):
             columns = slice(block * LANES, (block + 1) * LANES)
-            conv = back_ref[block, :tokens, :].astype(jnp.float32)
-            corr = back_ref[block, tokens:, :].astype(jnp.float32)
-            key_rows, value_rows, upstream_rows = (held[which, :, columns].astype(jnp.float32) for which in range(3))
-            out_grad = upstream_rows - readout(letters, rows_ref, columns)
-            made[0, :, columns] = (out_grad * conv).astype(bf16)
-            made[1, :, columns] = (corr * value_rows).astype(bf16)
-            made[2, :, columns] = (corr * key_rows).astype(bf16)
-        columns = pl.ds(piece * span, span)
+            conv = back_ref[block, part, :].astype(jnp.float32)
+            corr = back_ref[block, tokens + part.start : tokens + part.stop, :].astype(jnp.float32)
+            key_rows, value_rows, upstream_rows = (held[which, part, columns].astype(jnp.float32) for which in range(3))
+            out_grad = upstream_rows - readout(here, rows_ref, columns)
+            made[0, part, columns] = (out_grad * conv).astype(bf16)
+            made[1, part, columns] = (corr * value_rows).astype(bf16)
+            made[2, part, columns] = (corr * key_rows).astype(bf16)
+        part = pl.ds(piece * span, span)
         for which, target in enumerate(outs):
-            copy = pltpu.make_async_copy(
-                made.at[which, :, columns], target.at[0, :, columns], out_sems.at[which, piece]
-            )
+            copy = pltpu.make_async_copy(made.at[which, part], target.at[0, part], out_sems.at[which, piece])
             copy.start()
             leaving.append(copy)
     for copy in leaving:
@@ -160,10 +159,10 @@
         mid_ref[:, chunk(pair), :] = jnp.concatenate(halves, axis=1).astype(bf16)
 
 
-def last_stage(table, wide_ref, pair):
+def last_stage(table, wide_ref, pair, columns):
     halves = []
     for step in (2 * pair, 2 * pair + 1):
-        piece = wide_ref[:, step * SUB : (step + 1) * SUB, :]
+        piece = wide_ref[:, step * SUB : (step + 1) * SUB, columns]
         piece = piece.reshape(piece.shape[0] * SUB, piece.shape[2]).astype(bf16)
         out = dot(table(step), piece)
         halves.append(out.reshape(-1, SUB, out.shape[1]))
@@ -260,20 +259,20 @@
     back_copy.wait()
 
     for pair in range(steps // 2):
-        sums = last_stage(lambda step: back_ref[step], wide_ref, pair)
-        for part in range(2):
-            rows = chunk(pair, part * tokens)
-            direct = skip * both_ref[:, rows, :].astype(jnp.float32)
-            out_ref[:, rows, :] = (sums[:, :, part * LANES : (part + 1) * LANES] + direct).astype(bf16)
-        tap_grad = sums[:, :, taps].astype(bf16)
+        tap_grad = last_stage(lambda step: back_ref[step], wide_ref, pair, taps).astype(bf16)
         taps_ref[:, :, :, chunk(pair), :] = tap_grad.reshape(taps_ref.shape[:3] + (2 * SUB, LANES))
-
     leaving = []
     for turn in range(Y_PLACES):
         leaving.append(
             pltpu.make_async_copy(taps_ref.at[:, place_at(turn)], tap_outs[turn], out_sems.at[turn])
         )
         leaving[-1].start()
+    for pair in range(steps // 2):
+        sums = last_stage(lambda step: back_ref[step], wide_ref, pair, signals)
+        for part in range(2):
+            rows = chunk(pair, part * tokens)
+            direct = skip * both_ref[:, rows, :].astype(jnp.float32)
+            out_ref[:, rows, :] = (sums[:, :, part * LANES : (part + 1) * LANES] + direct).astype(bf16)
     for copy in leaving:
         copy.wait()
 
@@ -377,28 +376,13 @@
     return out, tap_grads
 
 
-def local(query, key_stream, value_stream, upstream, bases, base_rows, long_filter, skip_weight):
-    groups = lax.axis_size("seq")
+def gate(query, key_stream, value_stream, upstream, bases, base_rows, channels):
     tokens, width = query.shape[1:]
-    length = tokens * groups
-    channels = long_filter.shape[0]
-    array_bytes = tokens * width * 2
-    far, free, dma = pltpu.HBM, None, pltpu.SemaphoreType.DMA
-    packed = ((groups, 2 * tokens, channels), bf16, VMEM)
-    tap_block = (TAP_BLOCKS, tokens, channels)
-
-    (turned,) = call(
-        turn_kernel,
-        [(long_filter, far)],
-        [(tap_block, bf16, free)],
-        [VMEM((TAP_BLOCKS, channels, tokens), jnp.float32), dma((TAP_BLOCKS,))],
-        4,
-    )
-    other = along_dp(turned, 1, 0)
+    far, dma = pltpu.HBM, pltpu.SemaphoreType.DMA
     (gates,) = call(
         gate_kernel,
         [(query, far), (key_stream, far), (value_stream, far), (upstream, far), (bases, far), (base_rows, far)],
-        [packed],
+        [((width // channels, 2 * tokens, channels), bf16, VMEM)],
         [
             VMEM((4, tokens, width), bf16),
             VMEM(bases.shape, bases.dtype),
@@ -407,27 +391,16 @@
             dma((2,)),
         ],
         12,
-        moved=6 * array_bytes,
-    )
-    own_taps = jnp.where(place()[0] == 0, jnp.stack([turned, other]), jnp.stack([other, turned]))
-    gates, own_taps = lax.optimization_barrier((gates, own_taps))
-    taps = [own_taps] + [along_dp(own_taps, 0, turn) for turn in range(1, Y_PLACES)]
-    both = exchange(gates)
-
-    out, tap_grads = middle(both, taps, skip_weight.reshape(1, channels))
-    came = [along_dp(tap_grads[turn], 0, turn) for turn in range(1, Y_PLACES)]
-    home, *came = lax.optimization_barrier((exchange(out, lambda whole: whole + whole), *came))
-
-    kept, sent = call(
-        join_kernel,
-        [(part, free) for part in [tap_grads[0]] + came],
-        [(tap_block, jnp.float32, free), (tap_block, bf16, free)],
-        [],
-        8,
-    )
-    last = along_dp(sent, 1, 0)
-    grad = (query.shape, bf16, far)
-    query_grad, key_grad, value_grad = call(
+        moved=12 * tokens * width,
+    )
+    return gates
+
+
+def ungate(home, key_stream, value_stream, upstream, bases, base_rows):
+    tokens, width = key_stream.shape[1:]
+    far, free, dma = pltpu.HBM, None, pltpu.SemaphoreType.DMA
+    grad = (key_stream.shape, bf16, far)
+    return call(
         ungate_kernel,
         [(home, VMEM), (key_stream, far), (value_stream, far), (upstream, far), (bases, free), (base_rows, free)],
         [grad, grad, grad],
@@ -438,8 +411,45 @@
             dma((3, PIECES)),
         ],
         16,
-        moved=6 * array_bytes,
-    )
+        moved=12 * tokens * width,
+    )
+
+
+def local(query, key_stream, value_stream, upstream, bases, base_rows, long_filter, skip_weight):
+    groups = lax.axis_size("seq")
+    tokens, width = query.shape[1:]
+    length = tokens * groups
+    channels = long_filter.shape[0]
+    far, free, dma = pltpu.HBM, None, pltpu.SemaphoreType.DMA
+    tap_block = (TAP_BLOCKS, tokens, channels)
+
+    (turned,) = call(
+        turn_kernel,
+        [(long_filter, far)],
+        [(tap_block, bf16, free)],
+        [VMEM((TAP_BLOCKS, channels, tokens), jnp.float32), dma((TAP_BLOCKS,))],
+        4,
+    )
+    other = along_dp(turned, 1, 0)
+    gates = gate(query, key_stream, value_stream, upstream, bases, base_rows, channels)
+    own_taps = jnp.where(place()[0] == 0, jnp.stack([turned, other]), jnp.stack([other, turned]))
+    gates, own_taps = lax.optimization_barrier((gates, own_taps))
+    taps = [own_taps] + [along_dp(own_taps, 0, turn) for turn in range(1, Y_PLACES)]
+    both = exchange(gates)
+
+    out, tap_grads = middle(both, taps, skip_weight.reshape(1, channels))
+    came = [along_dp(tap_grads[turn], 0, turn) for turn in range(1, Y_PLACES)]
+    home, *came = lax.optimization_barrier((exchange(out, lambda whole: whole + whole), *came))
+
+    kept, sent = call(
+        join_kernel,
+        [(part, free) for part in [tap_grads[0]] + came],
+        [(tap_block, jnp.float32, free), (tap_block, bf16, free)],
+        [],
+        8,
+    )
+    last = along_dp(sent, 1, 0)
+    query_grad, key_grad, value_grad = ungate(home, key_stream, value_stream, upstream, bases, base_rows)
     (filter_grad,) = call(finish_kernel, [(kept, free), (last, free)], [(long_filter.shape, jnp.float32, free)], [], 8)
     return (query_grad, key_grad, value_grad, filter_grad)
 

time: 156 us -> 155 us (level)
  Pallas kernels: 23 us -> 21 us
    pallas_call x6, Pallas kernels: 23 us -> 21 us  [call(): pl.pallas_call(kernel, out_shape=tuple(out_shape), in_specs=in_specs, out...]
  transfers between devices with their start and end apart: 8 -> 8, of which waited for: 1 -> 2; matrix products, arithmetic and copies ran while one was open for 0% -> 0% of each run, Pallas kernels for 5% -> 4%
where the time goes in v5:
time: 155 us; the launch traced here: 154 us
  blocking collectives  118 us (76%)
  Pallas kernels  21 us (14%)
  starting transfers between devices  11.5 us (7%)
  waiting for transfers between devices  3.27 us (2%)
    all_to_all x2, blocking collectives, exchange(): lax.all_to_all(whole, 'seq', split_axis=0, concat_axis=0, tiled=True)  118 us
    pallas_call x6, Pallas kernels, call(): pl.pallas_call(kernel, out_shape=tuple(out_shape), in_specs=in_specs, out...  21 us
    ppermute x8, starting transfers between devices, along_dp(): return lax.ppermute(array, 'dp', moves)  11.5 us
    ppermute x8, waiting for transfers between devices, along_dp(): return lax.ppermute(array, 'dp', moves)  3.27 us
  transfers between devices with their start and end apart: 8, of which 2 were waited for; matrix products, arithmetic and copies ran while one was open for 0% of the time, Pallas kernels for 4%

profile of v5, /device:TPU:2, one launch (start us, length us, event | category | flops | bytes accessed | tf_op | source)
XLA Modules:
  0.0 154.3 jit_solution(926110048219876637)
XLA Ops:
  0.6 1.3 shard_map.148
  1.9 2.0 %collective-permute-start = (bf16[4,128,128]{2,1,0:T(8,128)(2,1)S(1)}, bf16[4,128,128]{2,1,0:T(8,128)(2,1)S(1)}, u32[]{:S(2)}, u32[]{:S(2)}) collective-permute-start(bf16[4,128,128]{2,1,0:T(8,128)(2,1)S(1)} %shard_map.148), channel_id=1, source_target_pairs={{0,128},{32,160},{64,192},{96,224},{128,0},{160,32},{192,64},{224,... | collective-permute-start | bytes 393224 | tf_op jit(solution)/shard_map/ppermute | solution.py:325
  3.9 3.1 %shard_map.147 = bf16[32,256,128]{2,1,0:T(8,128)(2,1)S(1)} custom-call(bf16[1,128,4096]{2,1,0:T(8,128)(2,1)} %query.1, bf16[1,128,4096]{2,1,0:T(8,128)(2,1)} %key.3, bf16[1,128,4096]{2,1,0:T(8,128)(2,1)} %value.3, bf16[1,128,4096]{2,1,0:T(8,128)(2,1)} %upstream.3, s32[1,128]{1,0:T(1,128)} %bases_ref.1, bf16[4,4096]{1,0:T(4,128)(2,1)} %rows_ref.1), custom_call_target="tpu_custom_call" | custom-call | bytes 6291456 | tf_op jit(solution)/shard_map/pallas_call | solution.py:308
  7.0 0.4 collective-permute-done
  7.5 3.1 %collective-permute-start.3 = (bf16[2,4,128,128]{3,2,1,0:T(8,128)(2,1)S(1)}, bf16[2,4,128,128]{3,2,1,0:T(8,128)(2,1)S(1)}, u32[]{:S(2)}, u32[]{:S(2)}) collective-permute-start(bf16[2,4,128,128]{3,2,1,0:T(8,128)(2,1)S(1)} %maximum_select_fusion.refs_0_), channel_id=1, source_target_pairs={{0,96},{32,0},{64,32},{96,64},{128,224},{160,128},{192,160},{224,1... | collective-permute-start | bytes 786440 | tf_op jit(solution)/shard_map/ppermute | solution.py:325
  10.5 0.6 collective-permute-start.2
  11.2 1.0 collective-permute-start.1
  12.2 59.8 %conditional.2 = (bf16[32,256,128]{2,1,0:T(8,128)(2,1)S(1)}) conditional(s32[]{:T(128)} %convert_element_type.4, bf16[32,256,128]{2,1,0:T(8,128)(2,1)S(1)} %shard_map.147, bf16[32,256,128]{2,1,0:T(8,128)(2,1)S(1)} %shard_map.147), branch_computations={%region_0.1_spmd, %region_1.2_spmd} | conditional | bytes 8388616 | solution.py:330
  12.2 0.1 copy.20
  12.3 59.6 %all_to_all.8 = bf16[32,256,128]{2,1,0:T(8,128)(2,1)S(1)} all-to-all(bf16[32,256,128]{2,1,0:T(8,128)(2,1)S(1)} %copy.20), channel_id=1, replica_groups=mesh['dp'=8,'seq'=32] {'seq'}, dimensions={0} | all-to-all | bytes 4194304 | tf_op jit(solution)/shard_map/cond/branch_1_fun/all_to_all | solution.py:332
  71.9 0.0 collective-permute-done.3.refs_3_
  71.9 0.0 collective-permute-done.2.refs_2_
  72.0 12.2 %shard_map.149 = (bf16[32,256,128]{2,1,0:T(8,128)(2,1)S(1)}, bf16[2,4,128,128]{3,2,1,0:T(8,128)(2,1)}, bf16[2,4,128,128]{3,2,1,0:T(8,128)(2,1)}, bf16[2,4,128,12...) custom-call(bf16[32,256,128]{2,1,0:T(8,128)(2,1)S(1)} %get-tuple-element.46.both_hbm, ...), custom_call_target="tpu_custom_call" | custom-call | flops 6442450944 | bytes 12582912 | tf_op jit(solution)/shard_map/pallas_call | solution.py:308
  84.2 2.0 %collective-permute-start.4 = (bf16[2,4,128,128]{3,2,1,0:T(8,128)(2,1)}, bf16[2,4,128,128]{3,2,1,0:T(8,128)(2,1)S(1)}, u32[]{:S(2)}, u32[]{:S(2)}) collective-permute-start(bf16[2,4,128,128]{3,2,1,0:T(8,128)(2,1)} %get-tuple-element.33), channel_id=1, source_target_pairs={{0,32},{32,64},{64,96},{96,0},{128,160},{160,192},{192,224},{224,1... | collective-permute-start | bytes 786440 | tf_op jit(solution)/shard_map/ppermute | solution.py:325
  86.2 1.8 %collective-permute-start.5 = (bf16[2,4,128,128]{3,2,1,0:T(8,128)(2,1)}, bf16[2,4,128,128]{3,2,1,0:T(8,128)(2,1)S(1)}, u32[]{:S(2)}, u32[]{:S(2)}) collective-permute-start(bf16[2,4,128,128]{3,2,1,0:T(8,128)(2,1)} %get-tuple-element.34), channel_id=1, source_target_pairs={{0,64},{32,96},{64,0},{96,32},{128,192},{160,224},{192,128},{224,1... | collective-permute-start | bytes 786440 | tf_op jit(solution)/shard_map/ppermute | solution.py:325
  88.0 0.9 collective-permute-start.6
  88.9 58.0 %conditional.3 = (bf16[32,256,128]{2,1,0:T(8,128)(2,1)S(1)}) conditional(s32[]{:T(128)} %convert_element_type.4, bf16[32,256,128]{2,1,0:T(8,128)(2,1)S(1)} %get-tuple-element.32, bf16[32,256,128]{2,1,0:T(8,128)(2,1)S(1)} %get-tuple-element.32), branch_computations={%region_2.3_spmd, %region_3.4_spmd} | conditional | bytes 6291464 | solution.py:330
  88.9 58.0 %all_to_all.9 = bf16[32,256,128]{2,1,0:T(8,128)(2,1)S(1)} all-to-all(bf16[32,256,128]{2,1,0:T(8,128)(2,1)S(1)} %param.3), channel_id=1, replica_groups=mesh['dp'=8,'seq'=32] {'seq'}, dimensions={0} | all-to-all | bytes 4194304 | tf_op jit(solution)/shard_map/cond/branch_1_fun/all_to_all | solution.py:332
  146.9 0.0 collective-permute-done.6.refs_3_
  146.9 0.1 shard_map.151
  147.1 0.1 collective-permute-start.7
  147.2 3.5 %shard_map.150 = (bf16[1,128,4096]{2,1,0:T(8,128)(2,1)}, bf16[1,128,4096]{2,1,0:T(8,128)(2,1)}, bf16[1,128,4096]{2,1,0:T(8,128)(2,1)}) custom-call(bf16[32,256,128]{2,1,0:T(8,128)(2,1)S(1)} %get-tuple-element.47.back_ref, bf16[1,128,4096]{2,1,0:T(8,128)(2,1)} %key.3, bf16[1,128,4096]{2,1,0:T(8,128)(2,1)} %value.3, bf16[1,128,4096]{2,1,0:T(8,128)(2,1)} %upstream.3, ...), custom_call_target="tpu_custom_call" | custom-call | bytes 6291456 | tf_op jit(solution)/shard_map/pallas_call | solution.py:308
  150.7 2.8 %collective-permute-done.7.came_ref = bf16[4,128,128]{2,1,0:T(8,128)(2,1)S(1)} collective-permute-done((bf16[4,128,128]{2,1,0:T(8,128)(2,1)S(1)}, bf16[4,128,128]{2,1,0:T(8,128)(2,1)S(1)}, u32[]{:S(2)}, u32[]{:S(2)}) %collective-permute-start.7) | collective-permute-done | bytes 131104 | tf_op jit(solution)/shard_map/ppermute | solution.py:325
  153.5 0.8 shard_map.152
  (16 shorter events, 0.1 us)
Async XLA Ops:
  1.9 5.5 %collective-permute-start = (bf16[4,128,128]{2,1,0:T(8,128)(2,1)S(1)}, bf16[4,128,128]{2,1,0:T(8,128)(2,1)S(1)}, u32[]{:S(2)}, u32[]{:S(2)}) collective-permute-start(bf16[4,128,128]{2,1,0:T(8,128)(2,1)S(1)} %shard_map.148), channel_id=1, source_target_pairs={{0,128},{32,160},{64,192},{96,224},{128,0},{160,32},{192,64},{224,... | collective-permute-start | bytes 393224 | tf_op jit(solution)/shard_map/ppermute | solution.py:325
  7.5 64.5 %collective-permute-start.3 = (bf16[2,4,128,128]{3,2,1,0:T(8,128)(2,1)S(1)}, bf16[2,4,128,128]{3,2,1,0:T(8,128)(2,1)S(1)}, u32[]{:S(2)}, u32[]{:S(2)}) collective-permute-start(bf16[2,4,128,128]{3,2,1,0:T(8,128)(2,1)S(1)} %maximum_select_fusion.refs_0_), channel_id=1, source_target_pairs={{0,96},{32,0},{64,32},{96,64},{128,224},{160,128},{192,160},{224,1... | collective-permute-start | bytes 786440 | tf_op jit(solution)/shard_map/ppermute | solution.py:325
  10.5 61.4 %collective-permute-start.2 = (bf16[2,4,128,128]{3,2,1,0:T(8,128)(2,1)S(1)}, bf16[2,4,128,128]{3,2,1,0:T(8,128)(2,1)S(1)}, u32[]{:S(2)}, u32[]{:S(2)}) collective-permute-start(bf16[2,4,128,128]{3,2,1,0:T(8,128)(2,1)S(1)} %maximum_select_fusion.refs_0_), channel_id=1, source_target_pairs={{0,64},{32,96},{64,0},{96,32},{128,192},{160,224},{192,128},{224,1... | collective-permute-start | bytes 786440 | tf_op jit(solution)/shard_map/ppermute | solution.py:325
  11.2 60.8 %collective-permute-start.1 = (bf16[2,4,128,128]{3,2,1,0:T(8,128)(2,1)S(1)}, bf16[2,4,128,128]{3,2,1,0:T(8,128)(2,1)S(1)}, u32[]{:S(2)}, u32[]{:S(2)}) collective-permute-start(bf16[2,4,128,128]{3,2,1,0:T(8,128)(2,1)S(1)} %maximum_select_fusion.refs_0_), channel_id=1, source_target_pairs={{0,32},{32,64},{64,96},{96,0},{128,160},{160,192},{192,224},{224,1... | collective-permute-start | bytes 786440 | tf_op jit(solution)/shard_map/ppermute | solution.py:325
  12.1 59.8 %copy-start.3 = (f32[128]{0:T(128)S(1)}, f32[128]{0:T(128)}, u32[]{:S(2)}) copy-start(f32[128]{0:T(128)} %param.23) | copy-start | bytes 1540
  12.1 59.8 %copy-start.4 = (bf16[256,256]{1,0:T(8,128)(2,1)S(1)}, bf16[256,256]{1,0:T(8,128)(2,1)}, u32[]{:S(2)}) copy-start(bf16[256,256]{1,0:T(8,128)(2,1)} %constant.35.clone.refs_8_) | copy-start | bytes 393220
  12.2 59.8 %copy-start.5 = (bf16[256,256]{1,0:T(8,128)(2,1)S(1)}, bf16[256,256]{1,0:T(8,128)(2,1)}, u32[]{:S(2)}) copy-start(bf16[256,256]{1,0:T(8,128)(2,1)} %constant.34.clone.refs_7_) | copy-start | bytes 393220
  84.2 62.7 %collective-permute-start.4 = (bf16[2,4,128,128]{3,2,1,0:T(8,128)(2,1)}, bf16[2,4,128,128]{3,2,1,0:T(8,128)(2,1)S(1)}, u32[]{:S(2)}, u32[]{:S(2)}) collective-permute-start(bf16[2,4,128,128]{3,2,1,0:T(8,128)(2,1)} %get-tuple-element.33), channel_id=1, source_target_pairs={{0,32},{32,64},{64,96},{96,0},{128,160},{160,192},{192,224},{224,1... | collective-permute-start | bytes 786440 | tf_op jit(solution)/shard_map/ppermute | solution.py:325
  86.2 60.7 %collective-permute-start.5 = (bf16[2,4,128,128]{3,2,1,0:T(8,128)(2,1)}, bf16[2,4,128,128]{3,2,1,0:T(8,128)(2,1)S(1)}, u32[]{:S(2)}, u32[]{:S(2)}) collective-permute-start(bf16[2,4,128,128]{3,2,1,0:T(8,128)(2,1)} %get-tuple-element.34), channel_id=1, source_target_pairs={{0,64},{32,96},{64,0},{96,32},{128,192},{160,224},{192,128},{224,1... | collective-permute-start | bytes 786440 | tf_op jit(solution)/shard_map/ppermute | solution.py:325
  88.0 58.9 %collective-permute-start.6 = (bf16[2,4,128,128]{3,2,1,0:T(8,128)(2,1)}, bf16[2,4,128,128]{3,2,1,0:T(8,128)(2,1)S(1)}, u32[]{:S(2)}, u32[]{:S(2)}) collective-permute-start(bf16[2,4,128,128]{3,2,1,0:T(8,128)(2,1)} %get-tuple-element.35), channel_id=1, source_target_pairs={{0,96},{32,0},{64,32},{96,64},{128,224},{160,128},{192,160},{224,1... | collective-permute-start | bytes 786440 | tf_op jit(solution)/shard_map/ppermute | solution.py:325
  88.9 58.0 %copy-start = (bf16[2,4,128,128]{3,2,1,0:T(8,128)(2,1)S(1)}, bf16[2,4,128,128]{3,2,1,0:T(8,128)(2,1)}, u32[]{:S(2)}) copy-start(bf16[2,4,128,128]{3,2,1,0:T(8,128)(2,1)} %get-tuple-element.40.refs_0_) | copy-start | bytes 786436
  88.9 58.2 %copy-start.1 = (bf16[4,4096]{1,0:T(4,128)(2,1)S(1)}, bf16[4,4096]{1,0:T(4,128)(2,1)}, u32[]{:S(2)}) copy-start(bf16[4,4096]{1,0:T(4,128)(2,1)} %rows_ref.1) | copy-start | bytes 98308
  88.9 58.2 %copy-start.2 = (s32[1,128]{1,0:T(1,128)S(1)}, s32[1,128]{1,0:T(1,128)}, u32[]{:S(2)}) copy-start(s32[1,128]{1,0:T(1,128)} %bases_ref.1) | copy-start | bytes 1540
  147.1 6.4 %collective-permute-start.7 = (bf16[4,128,128]{2,1,0:T(8,128)(2,1)S(1)}, bf16[4,128,128]{2,1,0:T(8,128)(2,1)S(1)}, u32[]{:S(2)}, u32[]{:S(2)}) collective-permute-start(bf16[4,128,128]{2,1,0:T(8,128)(2,1)S(1)} %get-tuple-element.45), channel_id=1, source_target_pairs={{0,128},{32,160},{64,192},{96,224},{128,0},{160,32},{192,64},{224,... | collective-permute-start | bytes 393224 | tf_op jit(solution)/shard_map/ppermute | solution.py:325

commit v6 on v5

--- a/solution.py
+++ b/solution.py
@@ -237,18 +237,27 @@
 
     second, undo = second_ref[...], undo_ref[...]
     signals, taps = slice(0, 2 * LANES), slice(2 * LANES, 3 * LANES)
+    def spectra_of(pair):
+        here = (2 * pair, 2 * pair + 1)
+        filters = dot(second, jnp.concatenate([group_of(group, taps) for group in here], axis=1))
+        return [dot(second, group_of(group, signals)) for group in here], filters
+
+    ready = spectra_of(0)
     for pair in range(groups // 2):
         here = (2 * pair, 2 * pair + 1)
-        filters = dot(second, jnp.concatenate([group_of(group, taps) for group in here], axis=1))
+        spectra, filters = ready
+        products = []
         crosses = []
+        for which in range(2):
+            gated, grad = spectra[which][:, :LANES], spectra[which][:, LANES:]
+            filt = filters[:, which * LANES : (which + 1) * LANES]
+            products.append(jnp.concatenate([times(gated, filt, False), times(grad, filt, True)], axis=1).astype(bf16))
+            crosses.append(times(grad, gated, True))
+        if pair + 1 < groups // 2:
+            ready = spectra_of(pair + 1)
         for which, group in enumerate(here):
-            spectrum = dot(second, group_of(group, signals))
-            gated, grad = spectrum[:, :LANES], spectrum[:, LANES:]
-            filt = filters[:, which * LANES : (which + 1) * LANES]
-            product = jnp.concatenate([times(gated, filt, False), times(grad, filt, True)], axis=1)
-            undone = dot(undo, product.astype(bf16))
+            undone = dot(undo, products[which])
             wide_ref[2 * group : 2 * group + 2, :, signals] = undone.reshape(2, tokens, 2 * LANES)
-            crosses.append(times(grad, gated, True))
         undone = dot(undo, jnp.concatenate(crosses, axis=1).astype(bf16))
         for which, group in enumerate(here):
             part = undone[:, which * LANES : (which + 1) * LANES]

time: 155 us -> 153 us (0.987)
  Pallas kernels: 21 us -> 19 us
    pallas_call x6, Pallas kernels: 21 us -> 19 us  [call(): pl.pallas_call(kernel, out_shape=tuple(out_shape), in_specs=in_specs, out...]
where the time goes in v6:
time: 153 us; the launch traced here: 152 us
  blocking collectives  118 us (77%)
  Pallas kernels  19 us (12%)
  starting transfers between devices  11.5 us (8%)
  waiting for transfers between devices  3.24 us (2%)
    all_to_all x2, blocking collectives, exchange(): lax.all_to_all(whole, 'seq', split_axis=0, concat_axis=0, tiled=True)  118 us
    pallas_call x6, Pallas kernels, call(): pl.pallas_call(kernel, out_shape=tuple(out_shape), in_specs=in_specs, out...  19 us
    ppermute x8, starting transfers between devices, along_dp(): return lax.ppermute(array, 'dp', moves)  11.5 us
    ppermute x8, waiting for transfers between devices, along_dp(): return lax.ppermute(array, 'dp', moves)  3.24 us
  transfers between devices with their start and end apart: 8, of which 2 were waited for; matrix products, arithmetic and copies ran while one was open for 0% of the time, Pallas kernels for 4%

profile of v6, /device:TPU:2, one launch (start us, length us, event | category | flops | bytes accessed | tf_op | source)
XLA Modules:
  0.0 152.3 jit_solution(16126246669238348777)
XLA Ops:
  0.6 1.3 shard_map.148
  1.9 2.0 %collective-permute-start = (bf16[4,128,128]{2,1,0:T(8,128)(2,1)S(1)}, bf16[4,128,128]{2,1,0:T(8,128)(2,1)S(1)}, u32[]{:S(2)}, u32[]{:S(2)}) collective-permute-start(bf16[4,128,128]{2,1,0:T(8,128)(2,1)S(1)} %shard_map.148), channel_id=1, source_target_pairs={{0,128},{32,160},{64,192},{96,224},{128,0},{160,32},{192,64},{224,... | collective-permute-start | bytes 393224 | tf_op jit(solution)/shard_map/ppermute | solution.py:334
  3.9 3.1 %shard_map.147 = bf16[32,256,128]{2,1,0:T(8,128)(2,1)S(1)} custom-call(bf16[1,128,4096]{2,1,0:T(8,128)(2,1)} %query.1, bf16[1,128,4096]{2,1,0:T(8,128)(2,1)} %key.3, bf16[1,128,4096]{2,1,0:T(8,128)(2,1)} %value.3, bf16[1,128,4096]{2,1,0:T(8,128)(2,1)} %upstream.3, s32[1,128]{1,0:T(1,128)} %bases_ref.1, bf16[4,4096]{1,0:T(4,128)(2,1)} %rows_ref.1), custom_call_target="tpu_custom_call" | custom-call | bytes 6291456 | tf_op jit(solution)/shard_map/pallas_call | solution.py:317
  7.0 0.4 collective-permute-done
  7.5 3.1 %collective-permute-start.3 = (bf16[2,4,128,128]{3,2,1,0:T(8,128)(2,1)S(1)}, bf16[2,4,128,128]{3,2,1,0:T(8,128)(2,1)S(1)}, u32[]{:S(2)}, u32[]{:S(2)}) collective-permute-start(bf16[2,4,128,128]{3,2,1,0:T(8,128)(2,1)S(1)} %maximum_select_fusion.refs_0_), channel_id=1, source_target_pairs={{0,96},{32,0},{64,32},{96,64},{128,224},{160,128},{192,160},{224,1... | collective-permute-start | bytes 786440 | tf_op jit(solution)/shard_map/ppermute | solution.py:334
  10.5 0.6 collective-permute-start.2
  11.2 1.0 collective-permute-start.1
  12.2 59.8 %conditional.2 = (bf16[32,256,128]{2,1,0:T(8,128)(2,1)S(1)}) conditional(s32[]{:T(128)} %convert_element_type.4, bf16[32,256,128]{2,1,0:T(8,128)(2,1)S(1)} %shard_map.147, bf16[32,256,128]{2,1,0:T(8,128)(2,1)S(1)} %shard_map.147), branch_computations={%region_0.1_spmd, %region_1.2_spmd} | conditional | bytes 8388616 | solution.py:339
  12.2 0.1 copy.20
  12.3 59.6 %all_to_all.8 = bf16[32,256,128]{2,1,0:T(8,128)(2,1)S(1)} all-to-all(bf16[32,256,128]{2,1,0:T(8,128)(2,1)S(1)} %copy.20), channel_id=1, replica_groups=mesh['dp'=8,'seq'=32] {'seq'}, dimensions={0} | all-to-all | bytes 4194304 | tf_op jit(solution)/shard_map/cond/branch_1_fun/all_to_all | solution.py:341
  71.9 0.0 collective-permute-done.3.refs_3_
  71.9 0.0 collective-permute-done.2.refs_2_
  72.0 10.2 %shard_map.149 = (bf16[32,256,128]{2,1,0:T(8,128)(2,1)S(1)}, bf16[2,4,128,128]{3,2,1,0:T(8,128)(2,1)}, bf16[2,4,128,128]{3,2,1,0:T(8,128)(2,1)}, bf16[2,4,128,12...) custom-call(bf16[32,256,128]{2,1,0:T(8,128)(2,1)S(1)} %get-tuple-element.46.both_hbm, ...), custom_call_target="tpu_custom_call" | custom-call | flops 6442450944 | bytes 12582912 | tf_op jit(solution)/shard_map/pallas_call | solution.py:317
  82.2 2.0 %collective-permute-start.4 = (bf16[2,4,128,128]{3,2,1,0:T(8,128)(2,1)}, bf16[2,4,128,128]{3,2,1,0:T(8,128)(2,1)S(1)}, u32[]{:S(2)}, u32[]{:S(2)}) collective-permute-start(bf16[2,4,128,128]{3,2,1,0:T(8,128)(2,1)} %get-tuple-element.33), channel_id=1, source_target_pairs={{0,32},{32,64},{64,96},{96,0},{128,160},{160,192},{192,224},{224,1... | collective-permute-start | bytes 786440 | tf_op jit(solution)/shard_map/ppermute | solution.py:334
  84.2 1.9 %collective-permute-start.5 = (bf16[2,4,128,128]{3,2,1,0:T(8,128)(2,1)}, bf16[2,4,128,128]{3,2,1,0:T(8,128)(2,1)S(1)}, u32[]{:S(2)}, u32[]{:S(2)}) collective-permute-start(bf16[2,4,128,128]{3,2,1,0:T(8,128)(2,1)} %get-tuple-element.34), channel_id=1, source_target_pairs={{0,64},{32,96},{64,0},{96,32},{128,192},{160,224},{192,128},{224,1... | collective-permute-start | bytes 786440 | tf_op jit(solution)/shard_map/ppermute | solution.py:334
  86.0 0.9 collective-permute-start.6
  86.9 58.0 %conditional.3 = (bf16[32,256,128]{2,1,0:T(8,128)(2,1)S(1)}) conditional(s32[]{:T(128)} %convert_element_type.4, bf16[32,256,128]{2,1,0:T(8,128)(2,1)S(1)} %get-tuple-element.32, bf16[32,256,128]{2,1,0:T(8,128)(2,1)S(1)} %get-tuple-element.32), branch_computations={%region_2.3_spmd, %region_3.4_spmd} | conditional | bytes 6291464 | solution.py:339
  86.9 58.0 %all_to_all.9 = bf16[32,256,128]{2,1,0:T(8,128)(2,1)S(1)} all-to-all(bf16[32,256,128]{2,1,0:T(8,128)(2,1)S(1)} %param.3), channel_id=1, replica_groups=mesh['dp'=8,'seq'=32] {'seq'}, dimensions={0} | all-to-all | bytes 4194304 | tf_op jit(solution)/shard_map/cond/branch_1_fun/all_to_all | solution.py:341
  144.9 0.0 collective-permute-done.6.refs_3_
  145.0 0.1 shard_map.151
  145.1 0.1 collective-permute-start.7
  145.2 3.5 %shard_map.150 = (bf16[1,128,4096]{2,1,0:T(8,128)(2,1)}, bf16[1,128,4096]{2,1,0:T(8,128)(2,1)}, bf16[1,128,4096]{2,1,0:T(8,128)(2,1)}) custom-call(bf16[32,256,128]{2,1,0:T(8,128)(2,1)S(1)} %get-tuple-element.47.back_ref, bf16[1,128,4096]{2,1,0:T(8,128)(2,1)} %key.3, bf16[1,128,4096]{2,1,0:T(8,128)(2,1)} %value.3, bf16[1,128,4096]{2,1,0:T(8,128)(2,1)} %upstream.3, ...), custom_call_target="tpu_custom_call" | custom-call | bytes 6291456 | tf_op jit(solution)/shard_map/pallas_call | solution.py:317
  148.7 2.8 %collective-permute-done.7.came_ref = bf16[4,128,128]{2,1,0:T(8,128)(2,1)S(1)} collective-permute-done((bf16[4,128,128]{2,1,0:T(8,128)(2,1)S(1)}, bf16[4,128,128]{2,1,0:T(8,128)(2,1)S(1)}, u32[]{:S(2)}, u32[]{:S(2)}) %collective-permute-start.7) | collective-permute-done | bytes 131104 | tf_op jit(solution)/shard_map/ppermute | solution.py:334
  151.5 0.8 shard_map.152
  (16 shorter events, 0.1 us)
Async XLA Ops:
  1.9 5.5 %collective-permute-start = (bf16[4,128,128]{2,1,0:T(8,128)(2,1)S(1)}, bf16[4,128,128]{2,1,0:T(8,128)(2,1)S(1)}, u32[]{:S(2)}, u32[]{:S(2)}) collective-permute-start(bf16[4,128,128]{2,1,0:T(8,128)(2,1)S(1)} %shard_map.148), channel_id=1, source_target_pairs={{0,128},{32,160},{64,192},{96,224},{128,0},{160,32},{192,64},{224,... | collective-permute-start | bytes 393224 | tf_op jit(solution)/shard_map/ppermute | solution.py:334
  7.5 64.5 %collective-permute-start.3 = (bf16[2,4,128,128]{3,2,1,0:T(8,128)(2,1)S(1)}, bf16[2,4,128,128]{3,2,1,0:T(8,128)(2,1)S(1)}, u32[]{:S(2)}, u32[]{:S(2)}) collective-permute-start(bf16[2,4,128,128]{3,2,1,0:T(8,128)(2,1)S(1)} %maximum_select_fusion.refs_0_), channel_id=1, source_target_pairs={{0,96},{32,0},{64,32},{96,64},{128,224},{160,128},{192,160},{224,1... | collective-permute-start | bytes 786440 | tf_op jit(solution)/shard_map/ppermute | solution.py:334
  10.5 61.4 %collective-permute-start.2 = (bf16[2,4,128,128]{3,2,1,0:T(8,128)(2,1)S(1)}, bf16[2,4,128,128]{3,2,1,0:T(8,128)(2,1)S(1)}, u32[]{:S(2)}, u32[]{:S(2)}) collective-permute-start(bf16[2,4,128,128]{3,2,1,0:T(8,128)(2,1)S(1)} %maximum_select_fusion.refs_0_), channel_id=1, source_target_pairs={{0,64},{32,96},{64,0},{96,32},{128,192},{160,224},{192,128},{224,1... | collective-permute-start | bytes 786440 | tf_op jit(solution)/shard_map/ppermute | solution.py:334
  11.2 60.8 %collective-permute-start.1 = (bf16[2,4,128,128]{3,2,1,0:T(8,128)(2,1)S(1)}, bf16[2,4,128,128]{3,2,1,0:T(8,128)(2,1)S(1)}, u32[]{:S(2)}, u32[]{:S(2)}) collective-permute-start(bf16[2,4,128,128]{3,2,1,0:T(8,128)(2,1)S(1)} %maximum_select_fusion.refs_0_), channel_id=1, source_target_pairs={{0,32},{32,64},{64,96},{96,0},{128,160},{160,192},{192,224},{224,1... | collective-permute-start | bytes 786440 | tf_op jit(solution)/shard_map/ppermute | solution.py:334
  12.1 59.8 %copy-start.3 = (f32[128]{0:T(128)S(1)}, f32[128]{0:T(128)}, u32[]{:S(2)}) copy-start(f32[128]{0:T(128)} %param.23) | copy-start | bytes 1540
  12.1 59.8 %copy-start.4 = (bf16[256,256]{1,0:T(8,128)(2,1)S(1)}, bf16[256,256]{1,0:T(8,128)(2,1)}, u32[]{:S(2)}) copy-start(bf16[256,256]{1,0:T(8,128)(2,1)} %constant.35.clone.refs_8_) | copy-start | bytes 393220
  12.2 59.8 %copy-start.5 = (bf16[256,256]{1,0:T(8,128)(2,1)S(1)}, bf16[256,256]{1,0:T(8,128)(2,1)}, u32[]{:S(2)}) copy-start(bf16[256,256]{1,0:T(8,128)(2,1)} %constant.34.clone.refs_7_) | copy-start | bytes 393220
  82.2 62.7 %collective-permute-start.4 = (bf16[2,4,128,128]{3,2,1,0:T(8,128)(2,1)}, bf16[2,4,128,128]{3,2,1,0:T(8,128)(2,1)S(1)}, u32[]{:S(2)}, u32[]{:S(2)}) collective-permute-start(bf16[2,4,128,128]{3,2,1,0:T(8,128)(2,1)} %get-tuple-element.33), channel_id=1, source_target_pairs={{0,32},{32,64},{64,96},{96,0},{128,160},{160,192},{192,224},{224,1... | collective-permute-start | bytes 786440 | tf_op jit(solution)/shard_map/ppermute | solution.py:334
  84.2 60.8 %collective-permute-start.5 = (bf16[2,4,128,128]{3,2,1,0:T(8,128)(2,1)}, bf16[2,4,128,128]{3,2,1,0:T(8,128)(2,1)S(1)}, u32[]{:S(2)}, u32[]{:S(2)}) collective-permute-start(bf16[2,4,128,128]{3,2,1,0:T(8,128)(2,1)} %get-tuple-element.34), channel_id=1, source_target_pairs={{0,64},{32,96},{64,0},{96,32},{128,192},{160,224},{192,128},{224,1... | collective-permute-start | bytes 786440 | tf_op jit(solution)/shard_map/ppermute | solution.py:334
  86.0 58.9 %collective-permute-start.6 = (bf16[2,4,128,128]{3,2,1,0:T(8,128)(2,1)}, bf16[2,4,128,128]{3,2,1,0:T(8,128)(2,1)S(1)}, u32[]{:S(2)}, u32[]{:S(2)}) collective-permute-start(bf16[2,4,128,128]{3,2,1,0:T(8,128)(2,1)} %get-tuple-element.35), channel_id=1, source_target_pairs={{0,96},{32,0},{64,32},{96,64},{128,224},{160,128},{192,160},{224,1... | collective-permute-start | bytes 786440 | tf_op jit(solution)/shard_map/ppermute | solution.py:334
  86.9 58.0 %copy-start = (bf16[2,4,128,128]{3,2,1,0:T(8,128)(2,1)S(1)}, bf16[2,4,128,128]{3,2,1,0:T(8,128)(2,1)}, u32[]{:S(2)}) copy-start(bf16[2,4,128,128]{3,2,1,0:T(8,128)(2,1)} %get-tuple-element.40.refs_0_) | copy-start | bytes 786436
  86.9 58.3 %copy-start.1 = (bf16[4,4096]{1,0:T(4,128)(2,1)S(1)}, bf16[4,4096]{1,0:T(4,128)(2,1)}, u32[]{:S(2)}) copy-start(bf16[4,4096]{1,0:T(4,128)(2,1)} %rows_ref.1) | copy-start | bytes 98308
  86.9 58.3 %copy-start.2 = (s32[1,128]{1,0:T(1,128)S(1)}, s32[1,128]{1,0:T(1,128)}, u32[]{:S(2)}) copy-start(s32[1,128]{1,0:T(1,128)} %bases_ref.1) | copy-start | bytes 1540
  145.1 6.4 %collective-permute-start.7 = (bf16[4,128,128]{2,1,0:T(8,128)(2,1)S(1)}, bf16[4,128,128]{2,1,0:T(8,128)(2,1)S(1)}, u32[]{:S(2)}, u32[]{:S(2)}) collective-permute-start(bf16[4,128,128]{2,1,0:T(8,128)(2,1)S(1)} %get-tuple-element.45), channel_id=1, source_target_pairs={{0,128},{32,160},{64,192},{96,224},{128,0},{160,32},{192,64},{224,... | collective-permute-start | bytes 393224 | tf_op jit(solution)/shard_map/ppermute | solution.py:334

commit v7 on v6

--- a/solution.py
+++ b/solution.py
@@ -11,6 +11,7 @@
 
 LANES = 128
 SUB = 8
+GATE_PIECES = 2
 PIECES = 4
 Z_PAIRS = 2
 Y_PLACES = 4
@@ -59,13 +60,13 @@
 
 def gate_kernel(query, key, value, upstream, bases, rows, out_ref, held, bases_ref, rows_ref, sems, small_sems):
     tokens, width = query.shape[1:]
-    span = tokens // PIECES
+    span = tokens // GATE_PIECES
     small = [
         pltpu.make_async_copy(bases, bases_ref, small_sems.at[0]),
         pltpu.make_async_copy(rows, rows_ref, small_sems.at[1]),
     ]
     copies = []
-    for piece in range(PIECES):
+    for piece in range(GATE_PIECES):
         part = pl.ds(piece * span, span)
         copies.append([])
         for which, source in enumerate((query, key, value, upstream)):
@@ -79,7 +80,7 @@
     for copy in small:
         copy.wait()
     letters = letters_of(bases_ref)
-    for piece in range(PIECES):
+    for piece in range(GATE_PIECES):
         part = slice(piece * span, (piece + 1) * span)
         here = letters[part]
         for copy in copies[piece]:
@@ -132,15 +133,12 @@
         copy.wait()
 
 
-def turn_kernel(taps_hbm, out_ref, held, sems):
-    copies = []
-    for block in range(held.shape[0]):
-        columns = pl.ds(block * LANES, LANES)
-        copies.append(pltpu.make_async_copy(taps_hbm.at[:, columns], held.at[block], sems.at[block]))
-        copies[-1].start()
-    for block, copy in enumerate(copies):
-        copy.wait()
-        out_ref[block] = jnp.transpose(held[block]).astype(bf16)
+def turn_kernel(taps_hbm, out_ref, held, sem):
+    copy = pltpu.make_async_copy(taps_hbm, held, sem)
+    copy.start()
+    copy.wait()
+    for block in range(out_ref.shape[0]):
+        out_ref[block] = jnp.transpose(held[:, block * LANES : (block + 1) * LANES]).astype(bf16)
 
 
 def chunk(pair, first=0):
@@ -396,7 +394,7 @@
             VMEM((4, tokens, width), bf16),
             VMEM(bases.shape, bases.dtype),
             VMEM(base_rows.shape, bf16),
-            dma((4, PIECES)),
+            dma((4, GATE_PIECES)),
             dma((2,)),
         ],
         12,
@@ -436,7 +434,7 @@
         turn_kernel,
         [(long_filter, far)],
         [(tap_block, bf16, free)],
-        [VMEM((TAP_BLOCKS, channels, tokens), jnp.float32), dma((TAP_BLOCKS,))],
+        [VMEM(long_filter.shape, jnp.float32), dma(())],
         4,
     )
     other = along_dp(turned, 1, 0)

time: 153 us -> 153 us (level)
  no operation moved by 1% of the time
where the time goes in v7:
time: 153 us; the launch traced here: 152 us
  blocking collectives  118 us (77%)
  Pallas kernels  18.7 us (12%)
  starting transfers between devices  11.5 us (8%)
  waiting for transfers between devices  3.32 us (2%)
    all_to_all x2, blocking collectives, exchange(): lax.all_to_all(whole, 'seq', split_axis=0, concat_axis=0, tiled=True)  118 us
    pallas_call x6, Pallas kernels, call(): pl.pallas_call(kernel, out_shape=tuple(out_shape), in_specs=in_specs, out...  18.7 us
    ppermute x8, starting transfers between devices, along_dp(): return lax.ppermute(array, 'dp', moves)  11.5 us
    ppermute x8, waiting for transfers between devices, along_dp(): return lax.ppermute(array, 'dp', moves)  3.32 us
  transfers between devices with their start and end apart: 8, of which 2 were waited for; matrix products, arithmetic and copies ran while one was open for 0% of the time, Pallas kernels for 4%

profile of v7, /device:TPU:2, one launch (start us, length us, event | category | flops | bytes accessed | tf_op | source)
XLA Modules:
  0.0 152.0 jit_solution(3413054865714415425)
XLA Ops:
  0.6 1.1 shard_map.148
  1.7 2.0 %collective-permute-start = (bf16[4,128,128]{2,1,0:T(8,128)(2,1)S(1)}, bf16[4,128,128]{2,1,0:T(8,128)(2,1)S(1)}, u32[]{:S(2)}, u32[]{:S(2)}) collective-permute-start(bf16[4,128,128]{2,1,0:T(8,128)(2,1)S(1)} %shard_map.148), channel_id=1, source_target_pairs={{0,128},{32,160},{64,192},{96,224},{128,0},{160,32},{192,64},{224,... | collective-permute-start | bytes 393224 | tf_op jit(solution)/shard_map/ppermute | solution.py:332
  3.7 3.0 %shard_map.147 = bf16[32,256,128]{2,1,0:T(8,128)(2,1)S(1)} custom-call(bf16[1,128,4096]{2,1,0:T(8,128)(2,1)} %query.1, bf16[1,128,4096]{2,1,0:T(8,128)(2,1)} %key.3, bf16[1,128,4096]{2,1,0:T(8,128)(2,1)} %value.3, bf16[1,128,4096]{2,1,0:T(8,128)(2,1)} %upstream.3, s32[1,128]{1,0:T(1,128)} %bases_ref.1, bf16[4,4096]{1,0:T(4,128)(2,1)} %rows_ref.1), custom_call_target="tpu_custom_call" | custom-call | bytes 6291456 | tf_op jit(solution)/shard_map/pallas_call | solution.py:315
  6.7 0.5 collective-permute-done
  7.2 3.1 %collective-permute-start.3 = (bf16[2,4,128,128]{3,2,1,0:T(8,128)(2,1)S(1)}, bf16[2,4,128,128]{3,2,1,0:T(8,128)(2,1)S(1)}, u32[]{:S(2)}, u32[]{:S(2)}) collective-permute-start(bf16[2,4,128,128]{3,2,1,0:T(8,128)(2,1)S(1)} %maximum_select_fusion.refs_0_), channel_id=1, source_target_pairs={{0,96},{32,0},{64,32},{96,64},{128,224},{160,128},{192,160},{224,1... | collective-permute-start | bytes 786440 | tf_op jit(solution)/shard_map/ppermute | solution.py:332
  10.3 0.6 collective-permute-start.2
  11.0 1.0 collective-permute-start.1
  11.9 59.8 %conditional.2 = (bf16[32,256,128]{2,1,0:T(8,128)(2,1)S(1)}) conditional(s32[]{:T(128)} %convert_element_type.4, bf16[32,256,128]{2,1,0:T(8,128)(2,1)S(1)} %shard_map.147, bf16[32,256,128]{2,1,0:T(8,128)(2,1)S(1)} %shard_map.147), branch_computations={%region_0.1_spmd, %region_1.2_spmd} | conditional | bytes 8388616 | solution.py:337
  11.9 0.1 copy.20
  12.1 59.6 %all_to_all.8 = bf16[32,256,128]{2,1,0:T(8,128)(2,1)S(1)} all-to-all(bf16[32,256,128]{2,1,0:T(8,128)(2,1)S(1)} %copy.20), channel_id=1, replica_groups=mesh['dp'=8,'seq'=32] {'seq'}, dimensions={0} | all-to-all | bytes 4194304 | tf_op jit(solution)/shard_map/cond/branch_1_fun/all_to_all | solution.py:339
  71.7 0.0 collective-permute-done.2.refs_2_
  71.7 0.0 collective-permute-done.1.refs_1_
  71.8 10.2 %shard_map.149 = (bf16[32,256,128]{2,1,0:T(8,128)(2,1)S(1)}, bf16[2,4,128,128]{3,2,1,0:T(8,128)(2,1)}, bf16[2,4,128,128]{3,2,1,0:T(8,128)(2,1)}, bf16[2,4,128,12...) custom-call(bf16[32,256,128]{2,1,0:T(8,128)(2,1)S(1)} %get-tuple-element.46.both_hbm, ...), custom_call_target="tpu_custom_call" | custom-call | flops 6442450944 | bytes 12582912 | tf_op jit(solution)/shard_map/pallas_call | solution.py:315
  82.0 1.9 %collective-permute-start.4 = (bf16[2,4,128,128]{3,2,1,0:T(8,128)(2,1)}, bf16[2,4,128,128]{3,2,1,0:T(8,128)(2,1)S(1)}, u32[]{:S(2)}, u32[]{:S(2)}) collective-permute-start(bf16[2,4,128,128]{3,2,1,0:T(8,128)(2,1)} %get-tuple-element.33), channel_id=1, source_target_pairs={{0,32},{32,64},{64,96},{96,0},{128,160},{160,192},{192,224},{224,1... | collective-permute-start | bytes 786440 | tf_op jit(solution)/shard_map/ppermute | solution.py:332
  83.9 1.8 %collective-permute-start.5 = (bf16[2,4,128,128]{3,2,1,0:T(8,128)(2,1)}, bf16[2,4,128,128]{3,2,1,0:T(8,128)(2,1)S(1)}, u32[]{:S(2)}, u32[]{:S(2)}) collective-permute-start(bf16[2,4,128,128]{3,2,1,0:T(8,128)(2,1)} %get-tuple-element.34), channel_id=1, source_target_pairs={{0,64},{32,96},{64,0},{96,32},{128,192},{160,224},{192,128},{224,1... | collective-permute-start | bytes 786440 | tf_op jit(solution)/shard_map/ppermute | solution.py:332
  85.8 0.9 collective-permute-start.6
  86.7 57.9 %conditional.3 = (bf16[32,256,128]{2,1,0:T(8,128)(2,1)S(1)}) conditional(s32[]{:T(128)} %convert_element_type.4, bf16[32,256,128]{2,1,0:T(8,128)(2,1)S(1)} %get-tuple-element.32, bf16[32,256,128]{2,1,0:T(8,128)(2,1)S(1)} %get-tuple-element.32), branch_computations={%region_2.3_spmd, %region_3.4_spmd} | conditional | bytes 6291464 | solution.py:337
  86.7 57.9 %all_to_all.9 = bf16[32,256,128]{2,1,0:T(8,128)(2,1)S(1)} all-to-all(bf16[32,256,128]{2,1,0:T(8,128)(2,1)S(1)} %param.3), channel_id=1, replica_groups=mesh['dp'=8,'seq'=32] {'seq'}, dimensions={0} | all-to-all | bytes 4194304 | tf_op jit(solution)/shard_map/cond/branch_1_fun/all_to_all | solution.py:339
  144.6 0.0 collective-permute-done.4.refs_1_
  144.6 0.1 shard_map.151
  144.8 0.1 collective-permute-start.7
  144.9 3.5 %shard_map.150 = (bf16[1,128,4096]{2,1,0:T(8,128)(2,1)}, bf16[1,128,4096]{2,1,0:T(8,128)(2,1)}, bf16[1,128,4096]{2,1,0:T(8,128)(2,1)}) custom-call(bf16[32,256,128]{2,1,0:T(8,128)(2,1)S(1)} %get-tuple-element.47.back_ref, bf16[1,128,4096]{2,1,0:T(8,128)(2,1)} %key.3, bf16[1,128,4096]{2,1,0:T(8,128)(2,1)} %value.3, bf16[1,128,4096]{2,1,0:T(8,128)(2,1)} %upstream.3, ...), custom_call_target="tpu_custom_call" | custom-call | bytes 6291456 | tf_op jit(solution)/shard_map/pallas_call | solution.py:315
  148.4 2.8 %collective-permute-done.7.came_ref = bf16[4,128,128]{2,1,0:T(8,128)(2,1)S(1)} collective-permute-done((bf16[4,128,128]{2,1,0:T(8,128)(2,1)S(1)}, bf16[4,128,128]{2,1,0:T(8,128)(2,1)S(1)}, u32[]{:S(2)}, u32[]{:S(2)}) %collective-permute-start.7) | collective-permute-done | bytes 131104 | tf_op jit(solution)/shard_map/ppermute | solution.py:332
  151.2 0.8 shard_map.152
  (16 shorter events, 0.1 us)
Async XLA Ops:
  1.7 5.5 %collective-permute-start = (bf16[4,128,128]{2,1,0:T(8,128)(2,1)S(1)}, bf16[4,128,128]{2,1,0:T(8,128)(2,1)S(1)}, u32[]{:S(2)}, u32[]{:S(2)}) collective-permute-start(bf16[4,128,128]{2,1,0:T(8,128)(2,1)S(1)} %shard_map.148), channel_id=1, source_target_pairs={{0,128},{32,160},{64,192},{96,224},{128,0},{160,32},{192,64},{224,... | collective-permute-start | bytes 393224 | tf_op jit(solution)/shard_map/ppermute | solution.py:332
  7.2 64.5 %collective-permute-start.3 = (bf16[2,4,128,128]{3,2,1,0:T(8,128)(2,1)S(1)}, bf16[2,4,128,128]{3,2,1,0:T(8,128)(2,1)S(1)}, u32[]{:S(2)}, u32[]{:S(2)}) collective-permute-start(bf16[2,4,128,128]{3,2,1,0:T(8,128)(2,1)S(1)} %maximum_select_fusion.refs_0_), channel_id=1, source_target_pairs={{0,96},{32,0},{64,32},{96,64},{128,224},{160,128},{192,160},{224,1... | collective-permute-start | bytes 786440 | tf_op jit(solution)/shard_map/ppermute | solution.py:332
  10.3 61.4 %collective-permute-start.2 = (bf16[2,4,128,128]{3,2,1,0:T(8,128)(2,1)S(1)}, bf16[2,4,128,128]{3,2,1,0:T(8,128)(2,1)S(1)}, u32[]{:S(2)}, u32[]{:S(2)}) collective-permute-start(bf16[2,4,128,128]{3,2,1,0:T(8,128)(2,1)S(1)} %maximum_select_fusion.refs_0_), channel_id=1, source_target_pairs={{0,64},{32,96},{64,0},{96,32},{128,192},{160,224},{192,128},{224,1... | collective-permute-start | bytes 786440 | tf_op jit(solution)/shard_map/ppermute | solution.py:332
  11.0 60.8 %collective-permute-start.1 = (bf16[2,4,128,128]{3,2,1,0:T(8,128)(2,1)S(1)}, bf16[2,4,128,128]{3,2,1,0:T(8,128)(2,1)S(1)}, u32[]{:S(2)}, u32[]{:S(2)}) collective-permute-start(bf16[2,4,128,128]{3,2,1,0:T(8,128)(2,1)S(1)} %maximum_select_fusion.refs_0_), channel_id=1, source_target_pairs={{0,32},{32,64},{64,96},{96,0},{128,160},{160,192},{192,224},{224,1... | collective-permute-start | bytes 786440 | tf_op jit(solution)/shard_map/ppermute | solution.py:332
  11.9 59.8 %copy-start.3 = (f32[128]{0:T(128)S(1)}, f32[128]{0:T(128)}, u32[]{:S(2)}) copy-start(f32[128]{0:T(128)} %param.23) | copy-start | bytes 1540
  11.9 59.8 %copy-start.4 = (bf16[256,256]{1,0:T(8,128)(2,1)S(1)}, bf16[256,256]{1,0:T(8,128)(2,1)}, u32[]{:S(2)}) copy-start(bf16[256,256]{1,0:T(8,128)(2,1)} %constant.35.clone.refs_8_) | copy-start | bytes 393220
  11.9 59.8 %copy-start.5 = (bf16[256,256]{1,0:T(8,128)(2,1)S(1)}, bf16[256,256]{1,0:T(8,128)(2,1)}, u32[]{:S(2)}) copy-start(bf16[256,256]{1,0:T(8,128)(2,1)} %constant.34.clone.refs_7_) | copy-start | bytes 393220
  82.0 62.6 %collective-permute-start.4 = (bf16[2,4,128,128]{3,2,1,0:T(8,128)(2,1)}, bf16[2,4,128,128]{3,2,1,0:T(8,128)(2,1)S(1)}, u32[]{:S(2)}, u32[]{:S(2)}) collective-permute-start(bf16[2,4,128,128]{3,2,1,0:T(8,128)(2,1)} %get-tuple-element.33), channel_id=1, source_target_pairs={{0,32},{32,64},{64,96},{96,0},{128,160},{160,192},{192,224},{224,1... | collective-permute-start | bytes 786440 | tf_op jit(solution)/shard_map/ppermute | solution.py:332
  83.9 60.7 %collective-permute-start.5 = (bf16[2,4,128,128]{3,2,1,0:T(8,128)(2,1)}, bf16[2,4,128,128]{3,2,1,0:T(8,128)(2,1)S(1)}, u32[]{:S(2)}, u32[]{:S(2)}) collective-permute-start(bf16[2,4,128,128]{3,2,1,0:T(8,128)(2,1)} %get-tuple-element.34), channel_id=1, source_target_pairs={{0,64},{32,96},{64,0},{96,32},{128,192},{160,224},{192,128},{224,1... | collective-permute-start | bytes 786440 | tf_op jit(solution)/shard_map/ppermute | solution.py:332
  85.8 58.8 %collective-permute-start.6 = (bf16[2,4,128,128]{3,2,1,0:T(8,128)(2,1)}, bf16[2,4,128,128]{3,2,1,0:T(8,128)(2,1)S(1)}, u32[]{:S(2)}, u32[]{:S(2)}) collective-permute-start(bf16[2,4,128,128]{3,2,1,0:T(8,128)(2,1)} %get-tuple-element.35), channel_id=1, source_target_pairs={{0,96},{32,0},{64,32},{96,64},{128,224},{160,128},{192,160},{224,1... | collective-permute-start | bytes 786440 | tf_op jit(solution)/shard_map/ppermute | solution.py:332
  86.7 57.9 %copy-start = (bf16[2,4,128,128]{3,2,1,0:T(8,128)(2,1)S(1)}, bf16[2,4,128,128]{3,2,1,0:T(8,128)(2,1)}, u32[]{:S(2)}) copy-start(bf16[2,4,128,128]{3,2,1,0:T(8,128)(2,1)} %get-tuple-element.40.refs_0_) | copy-start | bytes 786436
  86.7 58.2 %copy-start.1 = (bf16[4,4096]{1,0:T(4,128)(2,1)S(1)}, bf16[4,4096]{1,0:T(4,128)(2,1)}, u32[]{:S(2)}) copy-start(bf16[4,4096]{1,0:T(4,128)(2,1)} %rows_ref.1) | copy-start | bytes 98308
  86.7 58.2 %copy-start.2 = (s32[1,128]{1,0:T(1,128)S(1)}, s32[1,128]{1,0:T(1,128)}, u32[]{:S(2)}) copy-start(s32[1,128]{1,0:T(1,128)} %bases_ref.1) | copy-start | bytes 1540
  144.8 6.4 %collective-permute-start.7 = (bf16[4,128,128]{2,1,0:T(8,128)(2,1)S(1)}, bf16[4,128,128]{2,1,0:T(8,128)(2,1)S(1)}, u32[]{:S(2)}, u32[]{:S(2)}) collective-permute-start(bf16[4,128,128]{2,1,0:T(8,128)(2,1)S(1)} %get-tuple-element.45), channel_id=1, source_target_pairs={{0,128},{32,160},{64,192},{96,224},{128,0},{160,32},{192,64},{224,... | collective-permute-start | bytes 393224 | tf_op jit(solution)/shard_map/ppermute | solution.py:332

commit v8 on v7

--- a/solution.py
+++ b/solution.py
@@ -445,7 +445,7 @@
     both = exchange(gates)
 
     out, tap_grads = middle(both, taps, skip_weight.reshape(1, channels))
-    came = [along_dp(tap_grads[turn], 0, turn) for turn in range(1, Y_PLACES)]
+    came = [along_dp(tap_grads[turn], 0, turn) for turn in (2, 1, 3)]
     home, *came = lax.optimization_barrier((exchange(out, lambda whole: whole + whole), *came))
 
     kept, sent = call(

time: 153 us -> 153 us (level)
  no operation moved by 1% of the time
where the time goes in v8:
time: 153 us
  blocking collectives  118 us (77%)
  Pallas kernels  18.7 us (12%)
  starting transfers between devices  12 us (8%)
  waiting for transfers between devices  3.33 us (2%)
    all_to_all x2, blocking collectives, exchange(): lax.all_to_all(whole, 'seq', split_axis=0, concat_axis=0, tiled=True)  118 us
    pallas_call x6, Pallas kernels, call(): pl.pallas_call(kernel, out_shape=tuple(out_shape), in_specs=in_specs, out...  18.7 us
    ppermute x8, starting transfers between devices, along_dp(): return lax.ppermute(array, 'dp', moves)  12 us
    ppermute x8, waiting for transfers between devices, along_dp(): return lax.ppermute(array, 'dp', moves)  3.33 us
  transfers between devices with their start and end apart: 8, of which 2 were waited for; matrix products, arithmetic and copies ran while one was open for 0% of the time, Pallas kernels for 4%

profile of v8, /device:TPU:2, one launch (start us, length us, event | category | flops | bytes accessed | tf_op | source)
XLA Modules:
  0.0 152.7 jit_solution(8435831871035517370)
XLA Ops:
  0.6 1.1 shard_map.148
  1.7 2.0 %collective-permute-start = (bf16[4,128,128]{2,1,0:T(8,128)(2,1)S(1)}, bf16[4,128,128]{2,1,0:T(8,128)(2,1)S(1)}, u32[]{:S(2)}, u32[]{:S(2)}) collective-permute-start(bf16[4,128,128]{2,1,0:T(8,128)(2,1)S(1)} %shard_map.148), channel_id=1, source_target_pairs={{0,128},{32,160},{64,192},{96,224},{128,0},{160,32},{192,64},{224,... | collective-permute-start | bytes 393224 | tf_op jit(solution)/shard_map/ppermute | solution.py:332
  3.7 3.0 %shard_map.147 = bf16[32,256,128]{2,1,0:T(8,128)(2,1)S(1)} custom-call(bf16[1,128,4096]{2,1,0:T(8,128)(2,1)} %query.1, bf16[1,128,4096]{2,1,0:T(8,128)(2,1)} %key.3, bf16[1,128,4096]{2,1,0:T(8,128)(2,1)} %value.3, bf16[1,128,4096]{2,1,0:T(8,128)(2,1)} %upstream.3, s32[1,128]{1,0:T(1,128)} %bases_ref.1, bf16[4,4096]{1,0:T(4,128)(2,1)} %rows_ref.1), custom_call_target="tpu_custom_call" | custom-call | bytes 6291456 | tf_op jit(solution)/shard_map/pallas_call | solution.py:315
  6.7 0.5 collective-permute-done
  7.2 3.1 %collective-permute-start.3 = (bf16[2,4,128,128]{3,2,1,0:T(8,128)(2,1)S(1)}, bf16[2,4,128,128]{3,2,1,0:T(8,128)(2,1)S(1)}, u32[]{:S(2)}, u32[]{:S(2)}) collective-permute-start(bf16[2,4,128,128]{3,2,1,0:T(8,128)(2,1)S(1)} %maximum_select_fusion.refs_0_), channel_id=1, source_target_pairs={{0,96},{32,0},{64,32},{96,64},{128,224},{160,128},{192,160},{224,1... | collective-permute-start | bytes 786440 | tf_op jit(solution)/shard_map/ppermute | solution.py:332
  10.3 0.6 collective-permute-start.2
  11.0 1.0 collective-permute-start.1
  11.9 59.8 %conditional.2 = (bf16[32,256,128]{2,1,0:T(8,128)(2,1)S(1)}) conditional(s32[]{:T(128)} %convert_element_type.4, bf16[32,256,128]{2,1,0:T(8,128)(2,1)S(1)} %shard_map.147, bf16[32,256,128]{2,1,0:T(8,128)(2,1)S(1)} %shard_map.147), branch_computations={%region_0.1_spmd, %region_1.2_spmd} | conditional | bytes 8388616 | solution.py:337
  11.9 0.1 copy.20
  12.1 59.6 %all_to_all.8 = bf16[32,256,128]{2,1,0:T(8,128)(2,1)S(1)} all-to-all(bf16[32,256,128]{2,1,0:T(8,128)(2,1)S(1)} %copy.20), channel_id=1, replica_groups=mesh['dp'=8,'seq'=32] {'seq'}, dimensions={0} | all-to-all | bytes 4194304 | tf_op jit(solution)/shard_map/cond/branch_1_fun/all_to_all | solution.py:339
  71.7 0.0 collective-permute-done.3.refs_3_
  71.7 0.0 collective-permute-done.2.refs_2_
  71.7 0.0 collective-permute-done.1.refs_1_
  71.8 10.2 %shard_map.149 = (bf16[32,256,128]{2,1,0:T(8,128)(2,1)S(1)}, bf16[2,4,128,128]{3,2,1,0:T(8,128)(2,1)}, bf16[2,4,128,128]{3,2,1,0:T(8,128)(2,1)}, bf16[2,4,128,12...) custom-call(bf16[32,256,128]{2,1,0:T(8,128)(2,1)S(1)} %get-tuple-element.46.both_hbm, ...), custom_call_target="tpu_custom_call" | custom-call | flops 6442450944 | bytes 12582912 | tf_op jit(solution)/shard_map/pallas_call | solution.py:315
  82.0 2.0 %collective-permute-start.4 = (bf16[2,4,128,128]{3,2,1,0:T(8,128)(2,1)}, bf16[2,4,128,128]{3,2,1,0:T(8,128)(2,1)S(1)}, u32[]{:S(2)}, u32[]{:S(2)}) collective-permute-start(bf16[2,4,128,128]{3,2,1,0:T(8,128)(2,1)} %get-tuple-element.33), channel_id=1, source_target_pairs={{0,64},{32,96},{64,0},{96,32},{128,192},{160,224},{192,128},{224,1... | collective-permute-start | bytes 786440 | tf_op jit(solution)/shard_map/ppermute | solution.py:332
  84.0 1.2 collective-permute-start.5
  85.2 2.1 %collective-permute-start.6 = (bf16[2,4,128,128]{3,2,1,0:T(8,128)(2,1)}, bf16[2,4,128,128]{3,2,1,0:T(8,128)(2,1)S(1)}, u32[]{:S(2)}, u32[]{:S(2)}) collective-permute-start(bf16[2,4,128,128]{3,2,1,0:T(8,128)(2,1)} %get-tuple-element.35), channel_id=1, source_target_pairs={{0,96},{32,0},{64,32},{96,64},{128,224},{160,128},{192,160},{224,1... | collective-permute-start | bytes 786440 | tf_op jit(solution)/shard_map/ppermute | solution.py:332
  87.3 58.0 %conditional.3 = (bf16[32,256,128]{2,1,0:T(8,128)(2,1)S(1)}) conditional(s32[]{:T(128)} %convert_element_type.4, bf16[32,256,128]{2,1,0:T(8,128)(2,1)S(1)} %get-tuple-element.32, bf16[32,256,128]{2,1,0:T(8,128)(2,1)S(1)} %get-tuple-element.32), branch_computations={%region_2.3_spmd, %region_3.4_spmd} | conditional | bytes 6291464 | solution.py:337
  87.3 58.0 %all_to_all.9 = bf16[32,256,128]{2,1,0:T(8,128)(2,1)S(1)} all-to-all(bf16[32,256,128]{2,1,0:T(8,128)(2,1)S(1)} %param.3), channel_id=1, replica_groups=mesh['dp'=8,'seq'=32] {'seq'}, dimensions={0} | all-to-all | bytes 4194304 | tf_op jit(solution)/shard_map/cond/branch_1_fun/all_to_all | solution.py:339
  145.2 0.1 shard_map.151
  145.4 0.1 collective-permute-start.7
  145.5 3.5 %shard_map.150 = (bf16[1,128,4096]{2,1,0:T(8,128)(2,1)}, bf16[1,128,4096]{2,1,0:T(8,128)(2,1)}, bf16[1,128,4096]{2,1,0:T(8,128)(2,1)}) custom-call(bf16[32,256,128]{2,1,0:T(8,128)(2,1)S(1)} %get-tuple-element.47.back_ref, bf16[1,128,4096]{2,1,0:T(8,128)(2,1)} %key.3, bf16[1,128,4096]{2,1,0:T(8,128)(2,1)} %value.3, bf16[1,128,4096]{2,1,0:T(8,128)(2,1)} %upstream.3, ...), custom_call_target="tpu_custom_call" | custom-call | bytes 6291456 | tf_op jit(solution)/shard_map/pallas_call | solution.py:315
  149.0 2.8 %collective-permute-done.7.came_ref = bf16[4,128,128]{2,1,0:T(8,128)(2,1)S(1)} collective-permute-done((bf16[4,128,128]{2,1,0:T(8,128)(2,1)S(1)}, bf16[4,128,128]{2,1,0:T(8,128)(2,1)S(1)}, u32[]{:S(2)}, u32[]{:S(2)}) %collective-permute-start.7) | collective-permute-done | bytes 131104 | tf_op jit(solution)/shard_map/ppermute | solution.py:332
  151.8 0.8 shard_map.152
  (16 shorter events, 0.1 us)
Async XLA Ops:
  1.7 5.5 %collective-permute-start = (bf16[4,128,128]{2,1,0:T(8,128)(2,1)S(1)}, bf16[4,128,128]{2,1,0:T(8,128)(2,1)S(1)}, u32[]{:S(2)}, u32[]{:S(2)}) collective-permute-start(bf16[4,128,128]{2,1,0:T(8,128)(2,1)S(1)} %shard_map.148), channel_id=1, source_target_pairs={{0,128},{32,160},{64,192},{96,224},{128,0},{160,32},{192,64},{224,... | collective-permute-start | bytes 393224 | tf_op jit(solution)/shard_map/ppermute | solution.py:332
  7.2 64.5 %collective-permute-start.3 = (bf16[2,4,128,128]{3,2,1,0:T(8,128)(2,1)S(1)}, bf16[2,4,128,128]{3,2,1,0:T(8,128)(2,1)S(1)}, u32[]{:S(2)}, u32[]{:S(2)}) collective-permute-start(bf16[2,4,128,128]{3,2,1,0:T(8,128)(2,1)S(1)} %maximum_select_fusion.refs_0_), channel_id=1, source_target_pairs={{0,96},{32,0},{64,32},{96,64},{128,224},{160,128},{192,160},{224,1... | collective-permute-start | bytes 786440 | tf_op jit(solution)/shard_map/ppermute | solution.py:332
  10.3 61.4 %collective-permute-start.2 = (bf16[2,4,128,128]{3,2,1,0:T(8,128)(2,1)S(1)}, bf16[2,4,128,128]{3,2,1,0:T(8,128)(2,1)S(1)}, u32[]{:S(2)}, u32[]{:S(2)}) collective-permute-start(bf16[2,4,128,128]{3,2,1,0:T(8,128)(2,1)S(1)} %maximum_select_fusion.refs_0_), channel_id=1, source_target_pairs={{0,64},{32,96},{64,0},{96,32},{128,192},{160,224},{192,128},{224,1... | collective-permute-start | bytes 786440 | tf_op jit(solution)/shard_map/ppermute | solution.py:332
  11.0 60.8 %collective-permute-start.1 = (bf16[2,4,128,128]{3,2,1,0:T(8,128)(2,1)S(1)}, bf16[2,4,128,128]{3,2,1,0:T(8,128)(2,1)S(1)}, u32[]{:S(2)}, u32[]{:S(2)}) collective-permute-start(bf16[2,4,128,128]{3,2,1,0:T(8,128)(2,1)S(1)} %maximum_select_fusion.refs_0_), channel_id=1, source_target_pairs={{0,32},{32,64},{64,96},{96,0},{128,160},{160,192},{192,224},{224,1... | collective-permute-start | bytes 786440 | tf_op jit(solution)/shard_map/ppermute | solution.py:332
  11.9 59.8 %copy-start.3 = (f32[128]{0:T(128)S(1)}, f32[128]{0:T(128)}, u32[]{:S(2)}) copy-start(f32[128]{0:T(128)} %param.23) | copy-start | bytes 1540
  11.9 59.8 %copy-start.4 = (bf16[256,256]{1,0:T(8,128)(2,1)S(1)}, bf16[256,256]{1,0:T(8,128)(2,1)}, u32[]{:S(2)}) copy-start(bf16[256,256]{1,0:T(8,128)(2,1)} %constant.35.clone.refs_8_) | copy-start | bytes 393220
  11.9 59.8 %copy-start.5 = (bf16[256,256]{1,0:T(8,128)(2,1)S(1)}, bf16[256,256]{1,0:T(8,128)(2,1)}, u32[]{:S(2)}) copy-start(bf16[256,256]{1,0:T(8,128)(2,1)} %constant.34.clone.refs_7_) | copy-start | bytes 393220
  82.0 63.2 %collective-permute-start.4 = (bf16[2,4,128,128]{3,2,1,0:T(8,128)(2,1)}, bf16[2,4,128,128]{3,2,1,0:T(8,128)(2,1)S(1)}, u32[]{:S(2)}, u32[]{:S(2)}) collective-permute-start(bf16[2,4,128,128]{3,2,1,0:T(8,128)(2,1)} %get-tuple-element.33), channel_id=1, source_target_pairs={{0,64},{32,96},{64,0},{96,32},{128,192},{160,224},{192,128},{224,1... | collective-permute-start | bytes 786440 | tf_op jit(solution)/shard_map/ppermute | solution.py:332
  84.0 61.2 %collective-permute-start.5 = (bf16[2,4,128,128]{3,2,1,0:T(8,128)(2,1)}, bf16[2,4,128,128]{3,2,1,0:T(8,128)(2,1)S(1)}, u32[]{:S(2)}, u32[]{:S(2)}) collective-permute-start(bf16[2,4,128,128]{3,2,1,0:T(8,128)(2,1)} %get-tuple-element.34), channel_id=1, source_target_pairs={{0,32},{32,64},{64,96},{96,0},{128,160},{160,192},{192,224},{224,1... | collective-permute-start | bytes 786440 | tf_op jit(solution)/shard_map/ppermute | solution.py:332
  85.2 60.0 %collective-permute-start.6 = (bf16[2,4,128,128]{3,2,1,0:T(8,128)(2,1)}, bf16[2,4,128,128]{3,2,1,0:T(8,128)(2,1)S(1)}, u32[]{:S(2)}, u32[]{:S(2)}) collective-permute-start(bf16[2,4,128,128]{3,2,1,0:T(8,128)(2,1)} %get-tuple-element.35), channel_id=1, source_target_pairs={{0,96},{32,0},{64,32},{96,64},{128,224},{160,128},{192,160},{224,1... | collective-permute-start | bytes 786440 | tf_op jit(solution)/shard_map/ppermute | solution.py:332
  87.3 58.0 %copy-start = (bf16[2,4,128,128]{3,2,1,0:T(8,128)(2,1)S(1)}, bf16[2,4,128,128]{3,2,1,0:T(8,128)(2,1)}, u32[]{:S(2)}) copy-start(bf16[2,4,128,128]{3,2,1,0:T(8,128)(2,1)} %get-tuple-element.40.refs_0_) | copy-start | bytes 786436
  87.3 58.2 %copy-start.1 = (bf16[4,4096]{1,0:T(4,128)(2,1)S(1)}, bf16[4,4096]{1,0:T(4,128)(2,1)}, u32[]{:S(2)}) copy-start(bf16[4,4096]{1,0:T(4,128)(2,1)} %rows_ref.1) | copy-start | bytes 98308
  87.3 58.2 %copy-start.2 = (s32[1,128]{1,0:T(1,128)S(1)}, s32[1,128]{1,0:T(1,128)}, u32[]{:S(2)}) copy-start(s32[1,128]{1,0:T(1,128)} %bases_ref.1) | copy-start | bytes 1540
  145.4 6.4 %collective-permute-start.7 = (bf16[4,128,128]{2,1,0:T(8,128)(2,1)S(1)}, bf16[4,128,128]{2,1,0:T(8,128)(2,1)S(1)}, u32[]{:S(2)}, u32[]{:S(2)}) collective-permute-start(bf16[4,128,128]{2,1,0:T(8,128)(2,1)S(1)} %get-tuple-element.45), channel_id=1, source_target_pairs={{0,128},{32,160},{64,192},{96,224},{128,0},{160,32},{192,64},{224,... | collective-permute-start | bytes 393224 | tf_op jit(solution)/shard_map/ppermute | solution.py:332
